TPU v7x, 32 devices: a whole 2x2x4 slice. The times are simulated.
32 devices in a mesh: fsdp: 4 (over x, core), ctx: 2 (over y), tp: 4 (over z).
Axes of the slice: x: 2, y: 2, z: 4, core: 2. Of those that a mesh axis runs over, the one named last changes fastest.
Arguments:
- tokens: bfloat16 [8, 1024, 768], P('fsdp', 'ctx'), may hold values from -6 to 6
- teacher: bfloat16 [8, 1024, 768], P('fsdp', 'ctx'), may hold values from -6 to 6
- lengths: int32 [8], P('fsdp'), may hold values from 256 to 1024, as said below
- valid_mask: int32 [8, 1024], P('fsdp', 'ctx'), may hold values 0 or 1
- random_blocks: int32 [8, 16, 3], P('fsdp', 'ctx'), may hold values from 2 to 15
- step_count: int32 [1], replicated, may hold values from 2 to 20
- qkv_weight: float32 [3, 768, 768], P(None, 'fsdp', 'tp'), may hold values from -0.21875 to 0.21875
- out_weight: float32 [768, 768], P('tp', 'fsdp'), may hold values from -2.5 to 2.5
- up_weight: float32 [768, 3072], P('fsdp', 'tp'), may hold values from -0.21875 to 0.21875
- down_weight: float32 [3072, 768], P('tp', 'fsdp'), may hold values from -0.109375 to 0.109375
- norm_params: float32 [4, 768], P(None, 'fsdp'), may hold values from -1 to 1.5, as said below
- qkv_moment: float32 [3, 768, 768], P(None, 'fsdp', 'tp'), may hold values from -5.9604645e-07 to 5.9604645e-07
- qkv_square: float32 [3, 768, 768], P(None, 'fsdp', 'tp'), may hold values from 1.4122379e-16 to 5.6489517e-16
- out_moment: float32 [768, 768], P('tp', 'fsdp'), may hold values from -5.2154064e-08 to 5.2154064e-08
- out_square: float32 [768, 768], P('tp', 'fsdp'), may hold values from 1.1033109e-18 to 4.4132435e-18
- up_moment: float32 [768, 3072], P('fsdp', 'tp'), may hold values from -5.9604645e-07 to 5.9604645e-07
- up_square: float32 [768, 3072], P('fsdp', 'tp'), may hold values from 1.4122379e-16 to 5.6489517e-16
- down_moment: float32 [3072, 768], P('tp', 'fsdp'), may hold values from -5.9604645e-07 to 5.9604645e-07
- down_square: float32 [3072, 768], P('tp', 'fsdp'), may hold values from 1.4122379e-16 to 5.6489517e-16
- norm_moment: float32 [4, 768], P(None, 'fsdp'), may hold values from -2.3841858e-06 to 2.3841858e-06
- norm_square: float32 [4, 768], P(None, 'fsdp'), may hold values from 2.2595807e-15 to 9.038323e-15
Outputs:
- layer_out: bfloat16 [8, 1024, 768], P('fsdp', 'ctx')
- loss_value: float32 [], replicated
- input_grad: float32 [8, 1024, 768], P('fsdp', 'ctx')
- grad_norm: float32 [], replicated
- qkv_updated: float32 [3, 768, 768], P(None, 'fsdp', 'tp')
- qkv_moment_new: float32 [3, 768, 768], P(None, 'fsdp', 'tp')
- qkv_square_new: float32 [3, 768, 768], P(None, 'fsdp', 'tp')
- out_updated: float32 [768, 768], P('tp', 'fsdp')
- out_moment_new: float32 [768, 768], P('tp', 'fsdp')
- out_square_new: float32 [768, 768], P('tp', 'fsdp')
- up_updated: float32 [768, 3072], P('fsdp', 'tp')
- up_moment_new: float32 [768, 3072], P('fsdp', 'tp')
- up_square_new: float32 [768, 3072], P('fsdp', 'tp')
- down_updated: float32 [3072, 768], P('tp', 'fsdp')
- down_moment_new: float32 [3072, 768], P('tp', 'fsdp')
- down_square_new: float32 [3072, 768], P('tp', 'fsdp')
- norm_updated: float32 [4, 768], P(None, 'fsdp')
- norm_moment_new: float32 [4, 768], P(None, 'fsdp')
- norm_square_new: float32 [4, 768], P(None, 'fsdp')
Inputs may be any that keep to these rules, and one draw needn't show every extreme that they name: `lengths`: one slot has exactly 1024 tokens and another exactly 256. `norm_params`: rows 0 and 2 are gains, rows 1 and 3 biases.
All inputs are finite; a program needn't handle non-finite values. No bound on the sum of `valid_mask` on one device may be relied on, other than what follows from the above.
Results may differ from a plain program's by a relative error of at most 0.019.
Values may be sent and summed in bfloat16 or wider, within the bound.
A program may use at most 256 MiB of HBM per device.

v0:
```python
from functools import partial

import jax
import jax.numpy as jnp
from jax import lax
from jax.sharding import PartitionSpec as P

HD = 64
BLK = 64


norm_eps = 1e-06
beta_one = 0.9
beta_two = 0.999
adam_eps = 1e-08
decay_rate = 0.01
clip_level = 0.001
rate_list = (0.04, 0.4, 0.04, 0.02, 0.2)
negative = -1e30


def layer_norm(values, gain, shift):
    center = values - jnp.mean(values, -1, keepdims=True)
    inverse = lax.rsqrt(jnp.mean(center * center, -1, keepdims=True) + norm_eps)
    normed = center * inverse
    return (normed * gain + shift, normed, inverse)


def norm_backward(upstream, normed, inverse, gain):
    scaled = upstream * gain
    return inverse * (
        scaled
        - jnp.mean(scaled, -1, keepdims=True)
        - normed * jnp.mean(scaled * normed, -1, keepdims=True)
    )


def adam_update(weight, gradient, moment, square, factor, steps_done, rate):
    clipped = gradient * factor
    new_moment = beta_one * moment + (1.0 - beta_one) * clipped
    new_square = beta_two * square + (1.0 - beta_two) * clipped * clipped
    corrected = new_moment / (1.0 - beta_one**steps_done)
    scaled = new_square / (1.0 - beta_two**steps_done)
    new_weight = weight - rate * (corrected / (jnp.sqrt(scaled) + adam_eps) + decay_rate * weight)
    return (new_weight, new_moment, new_square)


def body(
    tokens,
    teacher,
    lengths,
    valid_mask,
    random_blocks,
    step_count,
    qkv_weight,
    out_weight,
    up_weight,
    down_weight,
    norm_params,
    qkv_moment,
    qkv_square,
    out_moment,
    out_square,
    up_moment,
    up_square,
    down_moment,
    down_square,
    norm_moment,
    norm_square,
):
    ctx_index = lax.axis_index("ctx")
    ctx_count = lax.axis_size("ctx")
    tp_index = lax.axis_index("tp")
    seqs_here, tok_count, width = tokens.shape
    local_blocks = tok_count // BLK
    block_count = local_blocks * ctx_count
    seq_len = tok_count * ctx_count
    width_local = qkv_weight.shape[2]
    heads_local = width_local // HD
    scale = HD ** (-0.5)
    f32 = jnp.float32
    bf16 = jnp.bfloat16
    full_qkv, full_out, full_up, full_down, full_norms = (
        lax.all_gather(qkv_weight.astype(bf16), "fsdp", axis=1, tiled=True),
        lax.all_gather(out_weight.astype(bf16), "fsdp", axis=1, tiled=True),
        lax.all_gather(up_weight.astype(bf16), "fsdp", axis=0, tiled=True),
        lax.all_gather(down_weight.astype(bf16), "fsdp", axis=1, tiled=True),
        lax.all_gather(norm_params.astype(bf16), "fsdp", axis=1, tiled=True),
    )
    gains = full_norms.astype(f32)
    projected = jnp.einsum("std,cde->stce", tokens, full_qkv, preferred_element_type=f32).astype(
        bf16
    )
    queries = projected[:, :, 0, :]
    kv_local = projected[:, :, 1:, :]
    gathered = lax.all_gather(kv_local, "ctx", axis=1, tiled=True)
    own_blocks = ctx_index * local_blocks + jnp.arange(local_blocks, dtype=jnp.int32)
    zero_row = own_blocks * 0
    window = jnp.stack([zero_row, zero_row + 1, own_blocks - 1, own_blocks, own_blocks + 1], -1)
    listed = jnp.concatenate(
        [jnp.broadcast_to(window[None], (seqs_here, local_blocks, 5)), random_blocks], -1
    )
    inside = (listed >= 0) & (listed < block_count)
    safe = jnp.clip(listed, 0, block_count - 1)
    key_pos = safe[..., None] * BLK + jnp.arange(BLK, dtype=jnp.int32)
    counted = (inside[..., None] & (key_pos < lengths[:, None, None, None])).reshape(
        seqs_here, local_blocks, 8 * BLK
    )
    key_live = jnp.arange(seq_len, dtype=jnp.int32)[None, :] < lengths[:, None]
    q_blocks = queries.reshape(seqs_here, local_blocks, BLK, heads_local, HD)
    head_rows = queries[:, : 2 * BLK].reshape(seqs_here, 2 * BLK, heads_local, HD)
    blocked = gathered.reshape(seqs_here, block_count, BLK, 2, width_local)
    picked = jax.vmap(lambda source, chosen: source[chosen])(blocked, safe)
    key_rows = picked[..., 0, :].reshape(seqs_here, local_blocks, 8 * BLK, heads_local, HD)
    value_rows = picked[..., 1, :].reshape(seqs_here, local_blocks, 8 * BLK, heads_local, HD)
    scores = (
        jnp.einsum("sbqhd,sbkhd->sbhqk", q_blocks, key_rows, preferred_element_type=f32) * scale
    )
    scores = jnp.where(counted[:, :, None, None, :], scores, negative)
    all_keys = gathered[:, :, 0, :].reshape(seqs_here, seq_len, heads_local, HD)
    all_values = gathered[:, :, 1, :].reshape(seqs_here, seq_len, heads_local, HD)
    wide_scores = (
        jnp.einsum("sqhd,skhd->shqk", head_rows, all_keys, preferred_element_type=f32) * scale
    )
    wide_scores = jnp.where(key_live[:, None, None, :], wide_scores, negative)
    top_value = jnp.max(scores, -1, keepdims=True)
    expo = jnp.exp(scores - top_value)
    summed = jnp.sum(expo, -1, keepdims=True)
    sparse_lse = top_value + jnp.log(summed)
    probs_b = (expo / summed).astype(bf16)
    sparse_out = jnp.einsum(
        "sbhqk,sbkhd->sbqhd", probs_b, value_rows, preferred_element_type=f32
    ).reshape(seqs_here, tok_count, width_local)
    wide_top = jnp.max(wide_scores, -1, keepdims=True)
    wide_expo = jnp.exp(wide_scores - wide_top)
    wide_sum = jnp.sum(wide_expo, -1, keepdims=True)
    wide_lse = wide_top + jnp.log(wide_sum)
    wide_probs = (wide_expo / wide_sum).astype(bf16)
    wide_out = jnp.einsum(
        "shqk,skhd->sqhd", wide_probs, all_values, preferred_element_type=f32
    ).reshape(seqs_here, 2 * BLK, width_local)
    is_first = ctx_index == 0
    row_ids = jnp.arange(tok_count, dtype=jnp.int32)
    global_row = (row_ids < 2 * BLK) & is_first
    rest_zeros = jnp.zeros((seqs_here, tok_count - 2 * BLK, width_local), f32)
    padded_wide = jnp.concatenate([wide_out, rest_zeros], 1)
    attended = jnp.where(global_row[None, :, None], padded_wide, sparse_out).astype(bf16)
    attn_part = jnp.einsum("ste,ed->std", attended, full_out, preferred_element_type=f32)
    positions = ctx_index * tok_count + row_ids
    live_rows = ((valid_mask == 1) & (positions[None, :] < lengths[:, None])).astype(f32)
    count_local = jnp.sum(live_rows)
    gelu_fn = partial(jax.nn.gelu, approximate=True)
    attn = lax.psum(attn_part.astype(jnp.bfloat16), "tp").astype(jnp.float32)
    hidden, normed_one, inverse_one = layer_norm(tokens.astype(f32) + attn, gains[0], gains[1])
    hidden_b = hidden.astype(bf16)
    upper = jnp.einsum("std,df->stf", hidden_b, full_up, preferred_element_type=f32)
    active_f, gelu_back = jax.vjp(gelu_fn, upper)
    active = active_f.astype(bf16)
    mixed = lax.psum(
        jnp.einsum("stf,fd->std", active, full_down, preferred_element_type=f32).astype(
            jnp.bfloat16
        ),
        "tp",
    ).astype(jnp.float32)
    result, normed_two, inverse_two = layer_norm(hidden + mixed, gains[2], gains[3])
    differ = result - teacher.astype(f32)
    error_local = jnp.sum(live_rows[..., None] * differ * differ)
    error_total, live_count = lax.psum((error_local, count_local), ("fsdp", "ctx"))
    loss_value = error_total / (live_count * width)
    grad_y = 2.0 * differ * live_rows[..., None] / (live_count * width)
    gain_two_grad = jnp.sum(grad_y * normed_two, (0, 1))
    bias_two_grad = jnp.sum(grad_y, (0, 1))
    grad_two = norm_backward(grad_y, normed_two, inverse_two, gains[2])
    grad_mixed = grad_two.astype(bf16)
    grad_active = jnp.einsum("std,fd->stf", grad_mixed, full_down, preferred_element_type=f32)
    grad_upper = gelu_back(grad_active)[0].astype(bf16)
    down_grad = jnp.einsum("stf,std->fd", active, grad_mixed, preferred_element_type=f32)
    up_grad = jnp.einsum("std,stf->df", hidden_b, grad_upper, preferred_element_type=f32)
    grad_hidden = grad_two + lax.psum(
        jnp.einsum("stf,df->std", grad_upper, full_up, preferred_element_type=f32).astype(
            jnp.bfloat16
        ),
        "tp",
    ).astype(jnp.float32)
    gain_one_grad = jnp.sum(grad_hidden * normed_one, (0, 1))
    bias_one_grad = jnp.sum(grad_hidden, (0, 1))
    grad_one = norm_backward(grad_hidden, normed_one, inverse_one, gains[0])
    norm_grad = jnp.stack([gain_one_grad, bias_one_grad, gain_two_grad, bias_two_grad], 0)
    grad_attn = grad_one.astype(bf16)
    out_grad = jnp.einsum("ste,std->ed", attended, grad_attn, preferred_element_type=f32)
    grad_attended = jnp.einsum(
        "std,ed->ste", grad_attn, full_out, preferred_element_type=f32
    ).astype(bf16)
    sparse_grad = jnp.where(global_row[None, :, None], jnp.zeros_like(grad_attended), grad_attended)
    sparse_grad = sparse_grad.reshape(seqs_here, local_blocks, BLK, heads_local, HD)
    probs = jnp.exp(scores - sparse_lse)
    grad_probs = jnp.einsum(
        "sbqhd,sbkhd->sbhqk", sparse_grad, value_rows, preferred_element_type=f32
    )
    row_dot = jnp.sum(probs * grad_probs, -1, keepdims=True)
    grad_scores = (probs * (grad_probs - row_dot)).astype(bf16)
    dq_sparse = (
        jnp.einsum("sbhqk,sbkhd->sbqhd", grad_scores, key_rows, preferred_element_type=f32) * scale
    )
    dk_rows = (
        jnp.einsum("sbhqk,sbqhd->sbkhd", grad_scores, q_blocks, preferred_element_type=f32) * scale
    )
    dv_rows = jnp.einsum(
        "sbhqk,sbqhd->sbkhd", probs.astype(bf16), sparse_grad, preferred_element_type=f32
    )
    list_grads = jnp.stack(
        [
            dk_rows.reshape(seqs_here, local_blocks, 8, BLK, width_local),
            dv_rows.reshape(seqs_here, local_blocks, 8, BLK, width_local),
        ],
        4,
    )
    seq_ids = jnp.broadcast_to(jnp.arange(seqs_here, dtype=jnp.int32)[:, None, None], safe.shape)
    kv_term = (
        jnp.zeros((block_count, seqs_here, BLK, 2, width_local), f32)
        .at[safe, seq_ids]
        .add(list_grads)
    )
    head_grad = jnp.where(
        is_first, grad_attended[:, : 2 * BLK], jnp.zeros_like(grad_attended[:, : 2 * BLK])
    )
    head_grad = head_grad.reshape(seqs_here, 2 * BLK, heads_local, HD)
    wide_probs_f = jnp.exp(wide_scores - wide_lse)
    wide_dprobs = jnp.einsum("sqhd,skhd->shqk", head_grad, all_values, preferred_element_type=f32)
    wide_dot = jnp.sum(wide_probs_f * wide_dprobs, -1, keepdims=True)
    wide_dscores = (wide_probs_f * (wide_dprobs - wide_dot)).astype(bf16)
    dq_wide = (
        jnp.einsum("shqk,skhd->sqhd", wide_dscores, all_keys, preferred_element_type=f32) * scale
    )
    split_scores = wide_dscores.reshape(seqs_here, heads_local, 2 * BLK, block_count, BLK)
    split_probs = wide_probs_f.astype(bf16).reshape(
        seqs_here, heads_local, 2 * BLK, block_count, BLK
    )
    dk_wide = (
        jnp.einsum("shqnb,sqhd->nsbhd", split_scores, head_rows, preferred_element_type=f32) * scale
    )
    dv_wide = jnp.einsum("shqnb,sqhd->nsbhd", split_probs, head_grad, preferred_element_type=f32)
    kv_term = kv_term + jnp.stack(
        [
            dk_wide.reshape(block_count, seqs_here, BLK, width_local),
            dv_wide.reshape(block_count, seqs_here, BLK, width_local),
        ],
        3,
    )
    kv_grads = lax.psum_scatter(
        kv_term.astype(jnp.bfloat16), "ctx", scatter_dimension=0, tiled=True
    ).astype(jnp.float32)
    kv_grads = jnp.transpose(kv_grads, (1, 0, 2, 3, 4)).reshape(
        seqs_here, tok_count, 2, width_local
    )
    dq_total = dq_sparse.reshape(seqs_here, tok_count, width_local) + jnp.concatenate(
        [dq_wide.reshape(seqs_here, 2 * BLK, width_local), rest_zeros], 1
    )
    grad_projected = jnp.concatenate([dq_total[:, :, None, :], kv_grads], 2).astype(bf16)
    qkv_grad = jnp.einsum("std,stce->cde", tokens, grad_projected, preferred_element_type=f32)
    input_part = jnp.einsum("stce,cde->std", grad_projected, full_qkv, preferred_element_type=f32)
    input_grad = grad_one + lax.psum(input_part.astype(jnp.bfloat16), "tp").astype(jnp.float32)
    local_grads = (qkv_grad, out_grad, up_grad, down_grad, norm_grad)
    owned = (
        lax.psum_scatter(
            local_grads[0].astype(jnp.bfloat16), "fsdp", scatter_dimension=1, tiled=True
        ).astype(jnp.float32),
        lax.psum_scatter(
            local_grads[1].astype(jnp.bfloat16), "fsdp", scatter_dimension=1, tiled=True
        ).astype(jnp.float32),
        lax.psum_scatter(
            local_grads[2].astype(jnp.bfloat16), "fsdp", scatter_dimension=0, tiled=True
        ).astype(jnp.float32),
        lax.psum_scatter(
            local_grads[3].astype(jnp.bfloat16), "fsdp", scatter_dimension=1, tiled=True
        ).astype(jnp.float32),
        lax.psum_scatter(
            local_grads[4].astype(jnp.bfloat16), "fsdp", scatter_dimension=1, tiled=True
        ).astype(jnp.float32),
    )
    shards = (
        lax.psum(owned[0].astype(jnp.bfloat16), "ctx").astype(jnp.float32),
        lax.psum(owned[1].astype(jnp.bfloat16), "ctx").astype(jnp.float32),
        lax.psum(owned[2].astype(jnp.bfloat16), "ctx").astype(jnp.float32),
        lax.psum(owned[3].astype(jnp.bfloat16), "ctx").astype(jnp.float32),
        lax.psum(owned[4].astype(jnp.bfloat16), "ctx").astype(jnp.float32),
    )
    matrix_squares = sum((jnp.sum(member * member) for member in shards[:4]))
    norm_squares = jnp.where(tp_index == 0, jnp.sum(shards[4] * shards[4]), 0.0)
    squares_total = lax.psum(matrix_squares + norm_squares, ("fsdp", "tp"))
    grad_norm = jnp.sqrt(squares_total)
    factor = jnp.minimum(1.0, clip_level / (grad_norm + 1e-06))
    steps_done = step_count[0].astype(f32)
    qkv_new = adam_update(
        qkv_weight, shards[0], qkv_moment, qkv_square, factor, steps_done, rate_list[0]
    )
    out_new = adam_update(
        out_weight, shards[1], out_moment, out_square, factor, steps_done, rate_list[1]
    )
    up_new = adam_update(
        up_weight, shards[2], up_moment, up_square, factor, steps_done, rate_list[2]
    )
    down_new = adam_update(
        down_weight, shards[3], down_moment, down_square, factor, steps_done, rate_list[3]
    )
    norm_new = adam_update(
        norm_params, shards[4], norm_moment, norm_square, factor, steps_done, rate_list[4]
    )
    return (
        result.astype(bf16),
        loss_value,
        input_grad,
        grad_norm,
        qkv_new[0],
        qkv_new[1],
        qkv_new[2],
        out_new[0],
        out_new[1],
        out_new[2],
        up_new[0],
        up_new[1],
        up_new[2],
        down_new[0],
        down_new[1],
        down_new[2],
        norm_new[0],
        norm_new[1],
        norm_new[2],
    )


def solution(mesh):
    in_specs = (
        P("fsdp", "ctx", None),
        P("fsdp", "ctx", None),
        P("fsdp"),
        P("fsdp", "ctx"),
        P("fsdp", "ctx", None),
        P(),
        P(None, "fsdp", "tp"),
        P("tp", "fsdp"),
        P("fsdp", "tp"),
        P("tp", "fsdp"),
        P(None, "fsdp"),
        P(None, "fsdp", "tp"),
        P(None, "fsdp", "tp"),
        P("tp", "fsdp"),
        P("tp", "fsdp"),
        P("fsdp", "tp"),
        P("fsdp", "tp"),
        P("tp", "fsdp"),
        P("tp", "fsdp"),
        P(None, "fsdp"),
        P(None, "fsdp"),
    )
    out_specs = (
        P("fsdp", "ctx", None),
        P(),
        P("fsdp", "ctx", None),
        P(),
        P(None, "fsdp", "tp"),
        P(None, "fsdp", "tp"),
        P(None, "fsdp", "tp"),
        P("tp", "fsdp"),
        P("tp", "fsdp"),
        P("tp", "fsdp"),
        P("fsdp", "tp"),
        P("fsdp", "tp"),
        P("fsdp", "tp"),
        P("tp", "fsdp"),
        P("tp", "fsdp"),
        P("tp", "fsdp"),
        P(None, "fsdp"),
        P(None, "fsdp"),
        P(None, "fsdp"),
    )
    return jax.shard_map(body, mesh=mesh, in_specs=in_specs, out_specs=out_specs, check_vma=False)
```

profile of v0, /device:TPU:0, one launch (start us, length us, event | category | flops | bytes accessed | tf_op | source)
XLA Modules:
  0.0 859.9 jit_solution(9670359910504586056)
XLA Ops:
  9.6 14.3 %all_gather.18 = bf16[3,768,192]{2,0,1:T(4,128)(2,1)S(1)} all-gather(bf16[3,192,192]{2,0,1:T(4,128)(2,1)S(1)} %copy.167), channel_id=1, replica_groups=mesh['fsdp'=4,'ctx'=2,'tp'=4] {'fsdp'}, dimensions={1}, use_global_device_ids=true | all-gather | bytes 1105920 | tf_op jit(solution)/shard_map/all_gather | solution.py:84
  35.2 7.5 all_gather.20
  43.0 15.7 %all-gather.5.cloned.1.call-done = bf16[2,1024,2,192]{1,3,2,0:T(8,128)(2,1)} async-done(((bf16[2,512,2,192]{1,3,2,0:T(8,128)(2,1)}), bf16[2,1024,2,192]{1,3,2,0:T(8,128)(2,1)}) %all-gather.5.cloned.1.call-update) | async-done | bytes 1572880 | tf_op jit(solution)/shard_map/all_gather | solution.py:96
  64.1 7.2 gather_fusion
  71.3 6.0 fusion.108
  77.3 8.2 copy.221
  85.5 8.0 reshape_squeeze.19
  93.6 8.5 copy.220
  102.1 9.3 %reshape_squeeze.17 = bf16[2,8,512,3,64]{2,4,3,1,0:T(8,128)(2,1)} reshape(bf16[2,8,8,64,1,192]{3,2,5,1,0,4:T(8,128)(2,1)} %copy.220) | data formatting | bytes 6291456 | tf_op jit(solution)/shard_map/reshape;squeeze | solution.py:115
  136.2 61.5 %all-reduce.9.cloned.1.call-done = bf16[2,512,768]{2,1,0:T(8,128)(2,1)} async-done(((bf16[2,512,768]{2,1,0:T(8,128)(2,1)}), bf16[2,512,768]{2,1,0:T(8,128)(2,1)}) %all-reduce.9.cloned.1.call-update) | async-done | bytes 1572880 | tf_op jit(solution)/shard_map/psum | solution.py:153
  205.2 5.3 convolution_convert_fusion.1
  213.2 14.4 %psum.87 = f32[]{:T(128)} all-reduce(f32[]{:T(128)} %get-tuple-element.163), channel_id=1, replica_groups=mesh['fsdp'=4,'ctx'=2,'tp'=4] {'fsdp','ctx'}, use_global_device_ids=true, to_apply=%region_13.14 | all-reduce | flops 1 | bytes 8 | tf_op jit(solution)/shard_map/psum | solution.py:168
  228.2 50.7 %all-reduce.11.cloned.1.call-done = bf16[2,512,768]{2,1,0:T(8,128)(2,1)} async-done(((bf16[2,512,768]{2,1,0:T(8,128)(2,1)}), bf16[2,512,768]{2,1,0:T(8,128)(2,1)}) %all-reduce.11.cloned.1.call-update) | async-done | bytes 1572880 | tf_op jit(solution)/shard_map/psum | solution.py:159
  299.0 64.8 %all-reduce.13.cloned.1.call-done = bf16[2,512,768]{2,1,0:T(8,128)(2,1)} async-done(((bf16[2,512,768]{2,1,0:T(8,128)(2,1)}), bf16[2,512,768]{2,1,0:T(8,128)(2,1)}) %all-reduce.13.cloned.1.call-update) | async-done | bytes 1572880 | tf_op jit(solution)/shard_map/psum | solution.py:179
  374.4 9.2 %multiply_reduce_fusion = (f32[2,8,3,64]{3,2,1,0:T(4,128)}, f32[2,8,3,64,512]{4,3,2,1,0:T(8,128)}) fusion(f32[2,8,3,64,512]{4,3,2,1,0:T(8,128)} %copy-done, f32[2,8,3,64]{3,2,1,0:T(4,128)S(1)} %copy-done.41, bf16[2,8,512,3,64]{2,4,3,1,0:T(8,128)(2,1)} %reshape_squeeze.17, bf16[2,8,64,3,64]{2,1,4,3,0:T(8,128)(2,1)S(1)} %reshape.275), kind=kOutput, calls=%fused_computation.5 | convolution fusion | flops 206042112 | bytes 16146432 | tf_op jit(solution)/shard_map/sbqhd,sbkhd->sbhqk/dot_general | solution.py:197
  407.2 5.4 multiply_convert_fusion
  417.9 10.7 %stack_reshape.14 = f32[2,8,8,64,1,192]{3,2,5,1,0,4:T(8,128)} reshape(f32[2,8,512,3,64]{2,4,3,1,0:T(8,128)} %multiply_bitcast_fusion) | data formatting | bytes 12582912 | tf_op jit(solution)/shard_map/stack;reshape | solution.py:211
  428.6 10.2 %stack_reshape.15 = f32[2,8,8,64,1,192]{3,2,5,1,0,4:T(8,128)} reshape(f32[2,8,512,3,64]{2,4,3,1,0:T(8,128)} %fusion.20) | data formatting | bytes 12582912 | tf_op jit(solution)/shard_map/stack;reshape | solution.py:211
  438.8 17.4 %pad_maximum_fusion = f32[2,8,8,64,2,192]{3,2,5,1,0,4:T(8,128)} fusion(f32[2,8,8,64,1,192]{3,2,5,1,0,4:T(8,128)} %stack_reshape.15, f32[2,8,8,64,1,192]{3,2,5,1,0,4:T(8,128)} %stack_reshape.14), kind=kLoop, calls=%fused_computation.2 | loop fusion | flops 3145728 | bytes 25165824 | tf_op jit(solution)/shard_map/stack | solution.py:211
  456.2 23.1 %copy.191 = f32[2,8,8,64,2,192]{5,3,4,2,1,0:T(8,128)} copy(f32[2,8,8,64,2,192]{3,2,5,1,0,4:T(8,128)} %pad_maximum_fusion) | data formatting | bytes 25165824 | tf_op jit(solution)/shard_map/stack | solution.py:211
  483.3 37.7 %scatter_fusion = f32[16,2,64,2,192]{4,2,3,1,0:T(8,128)} fusion(f32[16,2,64,2,192]{4,2,3,1,0:T(8,128)} %pad_maximum_fusion.1, s32[128]{0:T(128)S(1)} %reshape.288, f32[128,64,2,192]{3,1,2,0:T(8,128)} %bitcast.177), kind=kCustom, calls=%fused_computation.1 | custom fusion | flops 3145728 | bytes 37749760 | tf_op jit(solution)/shard_map/scatter-add | solution.py:222
  529.1 5.7 multiply_bitcast_fusion.2
  543.9 12.3 %reduce-scatter.13.cloned.1.call-done = bf16[8,2,64,2,192]{4,2,3,1,0:T(8,128)(2,1)} async-done(((bf16[16,2,64,2,192]{4,2,3,1,0:T(8,128)(2,1)}), bf16[8,2,64,2,192]{4,2,3,1,0:T(8,128)(2,1)}) %reduce-scatter.13.cloned.1.call-update) | async-done | bytes 786448 | tf_op jit(solution)/shard_map/reduce_scatter | solution.py:250
  572.0 5.6 bitcast_convert_fusion.1
  577.9 5.2 bitcast_convert_fusion.2
  585.9 21.5 %reduce-scatter.19.cloned.1.call-done = bf16[192,576]{1,0:T(8,128)(2,1)} async-done(((bf16[768,576]{1,0:T(8,128)(2,1)}), bf16[192,576]{1,0:T(8,128)(2,1)}) %reduce-scatter.19.cloned.1.call-update) | async-done | bytes 221200
  609.5 26.2 %reduce-scatter.17.cloned.1.call-done = bf16[768,192]{0,1:T(8,128)(2,1)} async-done(((bf16[768,768]{0,1:T(8,128)(2,1)}), bf16[768,192]{0,1:T(8,128)(2,1)}) %reduce-scatter.17.cloned.1.call-update) | async-done | bytes 294928 | tf_op jit(solution)/shard_map/reduce_scatter | solution.py:274
  635.7 29.1 %reduce-scatter.15.cloned.1.call-done = bf16[192,768]{1,0:T(8,128)(2,1)} async-done(((bf16[768,768]{1,0:T(8,128)(2,1)}), bf16[192,768]{1,0:T(8,128)(2,1)}) %reduce-scatter.15.cloned.1.call-update) | async-done | bytes 294928 | tf_op jit(solution)/shard_map/reduce_scatter | solution.py:271
  676.4 13.9 %psum.86 = f32[]{:T(128)} all-reduce(f32[]{:T(128)} %get-tuple-element.120), channel_id=1, replica_groups=mesh['fsdp'=4,'ctx'=2,'tp'=4] {'fsdp','ctx'}, use_global_device_ids=true, to_apply=%region_11.12 | all-reduce | flops 1 | bytes 8 | tf_op jit(solution)/shard_map/psum | solution.py:168
  698.1 31.6 %all-reduce.17.cloned.1.call-done = (bf16[3,192,192]{1,2,0:T(8,128)(2,1)}, bf16[192,192]{1,0:T(8,128)(2,1)}, bf16[192,768]{1,0:T(8,128)(2,1)}, bf16[768,192]{0,1:T(8,128)(2,1)}) async-done(((bf16[3,192,192]{1,2,0:T(8,128)(2,1)}, bf16[192,192]{1,0:T(8,128)(2,1)}, bf16[192,768]{1,0:T(8,128)(2,1)}, bf16[768,192]{0,1:T(8,128)(2,1)}), (bf16[3,192,192]{1,2,0:T(8,128)(2,1)}, bf16[192,192]{1,0:T(8,128)(2,1)}, ...) | async-done | bytes 884752 | tf_op jit(solution)/shard_map/psum | solution.py:282
  739.1 62.8 %all-reduce.15.cloned.1.call-done = bf16[2,512,768]{2,1,0:T(8,128)(2,1)} async-done(((bf16[2,512,768]{2,1,0:T(8,128)(2,1)}), bf16[2,512,768]{2,1,0:T(8,128)(2,1)}) %all-reduce.15.cloned.1.call-update) | async-done | bytes 1572880 | tf_op jit(solution)/shard_map/psum | solution.py:262
  805.2 32.2 %psum.95 = f32[]{:T(128)} all-reduce(f32[]{:T(128)S(6)} %add.326), channel_id=1, replica_groups=mesh['fsdp'=4,'ctx'=2,'tp'=4] {'fsdp','tp'}, use_global_device_ids=true, to_apply=%region_43.44 | all-reduce | flops 1 | bytes 8 | tf_op jit(solution)/shard_map/psum | solution.py:290
  (315 shorter events, 193.4 us)
Async XLA Ops:
  8.0 18.0 %copy-start.5 = (bf16[2,512,768]{2,1,0:T(8,128)(2,1)S(1)}, bf16[2,512,768]{2,1,0:T(8,128)(2,1)}, u32[]{:S(2)}) copy-start(bf16[2,512,768]{2,1,0:T(8,128)(2,1)} %param.21) | copy-start | bytes 4718596
  8.0 50.6 %all-gather.5.cloned.1.call-start = ((), (), s32[]{:S(2)}) async-start(), calls=%async_computation.6 | async-start | bytes 2359296 | tf_op jit(solution)/shard_map/all_gather | solution.py:96
  26.1 6.0 copy-start.36
  29.4 13.4 %copy-start.63 = (s32[2]{0:T(128)S(1)}, s32[2]{0:T(128)}, u32[]{:S(2)}) copy-start(s32[2]{0:T(128)} %param.23) | copy-start | bytes 28
  30.4 167.3 %all-reduce.9.cloned.1.call-start = ((), (), s32[]{:S(2)}) async-start(), calls=%async_computation.7 | async-start | bytes 3145728 | tf_op jit(solution)/shard_map/psum | solution.py:153
  42.8 83.2 %copy-start.64 = (pred[512]{0:T(512)(128)(4,1)}, pred[512]{0:T(512)(128)(4,1)S(1)}, u32[]{:S(2)}) copy-start(pred[512]{0:T(512)(128)(4,1)S(1)} %fusion.87) | copy-start | bytes 1540
  93.6 17.9 %copy-start.10 = (bf16[2,8,512,3,64]{2,4,3,1,0:T(8,128)(2,1)}, bf16[2,8,512,3,64]{2,4,3,1,0:T(8,128)(2,1)S(1)}, u32[]{:S(2)}) copy-start(bf16[2,8,512,3,64]{2,4,3,1,0:T(8,128)(2,1)S(1)} %reshape_squeeze.19) | copy-start | bytes 9437188
  126.6 71.1 %copy-start.6 = (bf16[2,512,768]{2,1,0:T(8,128)(2,1)S(1)}, bf16[2,512,768]{2,1,0:T(8,128)(2,1)}, u32[]{:S(2)}) copy-start(bf16[2,512,768]{2,1,0:T(8,128)(2,1)} %param.21) | copy-start | bytes 4718596
  128.4 72.1 %all-gather.7.cloned.1.call-start = ((), (), s32[]{:S(2)}) async-start(), calls=%async_computation.8 | async-start | bytes 1474560 | tf_op jit(solution)/shard_map/all_gather | solution.py:86
  129.4 75.8 %all-gather.9.cloned.1.call-start = ((), (), s32[]{:S(2)}) async-start(), calls=%async_computation.9 | async-start | bytes 1474560 | tf_op jit(solution)/shard_map/all_gather | solution.py:87
  130.2 148.6 %all-reduce.11.cloned.1.call-start = ((), (), s32[]{:S(2)}) async-start(), calls=%async_computation.10 | async-start | bytes 3145728 | tf_op jit(solution)/shard_map/psum | solution.py:159
  136.2 142.7 %copy-start.52 = (f32[768]{0:T(1024)}, f32[768]{0:T(1024)S(1)}, u32[]{:S(2)}) copy-start(f32[768]{0:T(1024)S(1)} %get-tuple-element.126) | copy-start | bytes 9220
  210.6 153.2 %all-reduce.13.cloned.1.call-start = ((), (), s32[]{:S(2)}) async-start(), calls=%async_computation.11 | async-start | bytes 3145728 | tf_op jit(solution)/shard_map/psum | solution.py:179
  295.5 260.7 %reduce-scatter.13.cloned.1.call-start = ((), (), s32[]{:S(2)}) async-start(), calls=%async_computation.12 | async-start | bytes 3145728 | tf_op jit(solution)/shard_map/reduce_scatter | solution.py:250
  371.3 12.3 %slice-start = ((s8[6291456]{0:T(1024)(128)(4,1)}), s8[2097152]{0:T(1024)(128)(4,1)S(1)}, s32[]{:S(2)}) async-start(s8[6291456]{0:T(1024)(128)(4,1)} %bitcast.175), calls=%async_computation.20 | async-start | bytes 4194304
  374.4 9.2 %slice-start.1 = ((s8[6291456]{0:T(1024)(128)(4,1)}), s8[4194304]{0:T(1024)(128)(4,1)S(1)}, s32[]{:S(2)}) async-start(s8[6291456]{0:T(1024)(128)(4,1)} %bitcast.175), calls=%async_computation.21 | async-start | bytes 8388608
  390.6 10.5 %copy-start.12 = (bf16[2,3,128,1024]{3,2,1,0:T(8,128)(2,1)}, bf16[2,3,128,1024]{3,2,1,0:T(8,128)(2,1)S(1)}, u32[]{:S(2)}) copy-start(bf16[2,3,128,1024]{3,2,1,0:T(8,128)(2,1)S(1)} %get-tuple-element.154) | copy-start | bytes 4718596
  407.2 7.1 copy-start.15
  456.2 23.2 %copy-start.14 = (f32[16,2,64,1,192]{4,2,3,1,0:T(8,128)S(1)}, f32[16,2,64,1,192]{4,2,3,1,0:T(8,128)}, u32[]{:S(2)}) copy-start(f32[16,2,64,1,192]{4,2,3,1,0:T(8,128)} %copy.188) | copy-start | bytes 4718596
  525.1 59.2 %reduce-scatter.21.cloned.1.call-start = ((), (), s32[]{:S(2)}) async-start(), calls=%async_computation.17 | async-start | bytes 491520
  534.8 72.6 %reduce-scatter.19.cloned.1.call-start = ((), (), s32[]{:S(2)}) async-start(), calls=%async_computation.16 | async-start | bytes 1228800
  543.9 16.8 %copy-start.42 = (bf16[2,512,1,192]{1,3,2,0:T(8,128)(2,1)S(1)}, bf16[2,512,1,192]{1,3,2,0:T(8,128)(2,1)}, u32[]{:S(2)}) copy-start(bf16[2,512,1,192]{1,3,2,0:T(8,128)(2,1)} %fusion.68) | copy-start | bytes 1179652
  571.9 5.9 copy-start.53
  572.0 63.7 %reduce-scatter.17.cloned.1.call-start = ((), (), s32[]{:S(2)}) async-start(), calls=%async_computation.15 | async-start | bytes 1474560 | tf_op jit(solution)/shard_map/reduce_scatter | solution.py:274
  577.6 87.1 %reduce-scatter.15.cloned.1.call-start = ((), (), s32[]{:S(2)}) async-start(), calls=%async_computation.14 | async-start | bytes 1474560 | tf_op jit(solution)/shard_map/reduce_scatter | solution.py:271
  583.1 107.9 %reduce-scatter.23.cloned.1.call-start = ((), (), s32[]{:S(2)}) async-start(), calls=%async_computation.18 | async-start | bytes 245760
  584.2 145.6 %all-reduce.17.cloned.1.call-start = ((), (), s32[]{:S(2)}) async-start(), calls=%async_computation.19 | async-start | bytes 1966080 | tf_op jit(solution)/shard_map/psum | solution.py:282
  664.8 137.0 %all-reduce.15.cloned.1.call-start = ((), (), s32[]{:S(2)}) async-start(), calls=%async_computation.13 | async-start | bytes 3145728 | tf_op jit(solution)/shard_map/psum | solution.py:262
  739.0 99.1 %copy-start.32 = (bf16[3,192,192]{1,2,0:T(8,128)(2,1)S(1)}, bf16[3,192,192]{1,2,0:T(8,128)(2,1)}, u32[]{:S(2)}) copy-start(bf16[3,192,192]{1,2,0:T(8,128)(2,1)} %get-tuple-element.127) | copy-start | bytes 663556
  838.1 5.9 copy-start.37
  842.3 6.2 copy-start.29
  842.3 6.2 copy-start.30
  (57 other events, 186.1 us)
Sparse Core Ops, SparseCore 0:
  30.5 28.1 all-gather.4
  128.5 69.0 all-reduce.8
  210.7 68.1 all-reduce.10
  295.6 68.1 all-reduce.12
  525.2 30.9 reduce-scatter.12
  559.3 20.8 reduce-scatter.20
  582.9 24.4 reduce-scatter.18
  609.9 25.7 reduce-scatter.16
  639.0 25.7 reduce-scatter.14
  667.6 19.7 reduce-scatter.22
  690.5 39.1 all-reduce.16
  732.6 69.1 all-reduce.14
Sparse Core Ops, SparseCore 1:
  131.0 17.3 all-gather.6
  150.3 17.3 all-gather.8
where the time goes:
time: 866 us; the launch traced here: 860 us
  waiting for transfers between devices  376 us (43%)
  local copies, waits for them, and re-layouts  165 us (19%)
  other arithmetic  121 us (14%)
  blocking collectives  92.5 us (11%)
  matrix products  78.6 us (9%)
  between operations  25.2 us (3%)
    psum x1, waiting for transfers between devices, body(): lax.psum(jnp.einsum('stf,df->std', grad_upper, full_up, preferred_element...  64.8 us
    psum x1, waiting for transfers between devices, body(): lax.psum(input_part.astype(jnp.bfloat16), 'tp').astype(jnp.float32)  62.8 us
    psum x1, waiting for transfers between devices, body(): attn = lax.psum(attn_part.astype(jnp.bfloat16), 'tp').astype(jnp.float32)  61.5 us
    unnamed x168, local copies, waits for them, and re-layouts  53.3 us
    psum x1, waiting for transfers between devices, body(): lax.psum(jnp.einsum('stf,fd->std', active, full_down, preferred_element_t...  50.7 us
    another operation x3, local copies, waits for them, and re-layouts, body(): jnp.stack([dk_rows.reshape(seqs_here, local_blocks, 8, BLK, width_local),...  44.1 us
    scatter-add x1, other arithmetic, body(): kv_term = jnp.zeros((block_count, seqs_here, BLK, 2, width_local), f32).a...  37.7 us
    psum x1, blocking collectives, body(): squares_total = lax.psum(matrix_squares + norm_squares, ('fsdp', 'tp'))  32.2 us
  transfers between devices with their start and end apart: 14, of which 10 were waited for; matrix products, arithmetic and copies ran while one was open for 10% of the time, Pallas kernels for 0%

commit v1 on v0

--- a/solution.py
+++ b/solution.py
@@ -1,13 +1,18 @@
+import functools
 from functools import partial
 
 import jax
 import jax.numpy as jnp
 from jax import lax
+from jax.experimental import pallas as pl
+from jax.experimental.pallas import tpu as pltpu
 from jax.sharding import PartitionSpec as P
 
 HD = 64
 BLK = 64
-
+MESH = pl.DeviceIdType.MESH
+f32 = jnp.float32
+bf16 = jnp.bfloat16
 
 norm_eps = 1e-06
 beta_one = 0.9
@@ -17,6 +22,7 @@
 clip_level = 0.001
 rate_list = (0.04, 0.4, 0.04, 0.02, 0.2)
 negative = -1e30
+VMEM_LIMIT = 58 * 2**20
 
 
 def layer_norm(values, gain, shift):
@@ -45,7 +51,7 @@
     return (new_weight, new_moment, new_square)
 
 
-def body(
+def body_general(
     tokens,
     teacher,
     lengths,
@@ -78,8 +84,6 @@
     width_local = qkv_weight.shape[2]
     heads_local = width_local // HD
     scale = HD ** (-0.5)
-    f32 = jnp.float32
-    bf16 = jnp.bfloat16
     full_qkv, full_out, full_up, full_down, full_norms = (
         lax.all_gather(qkv_weight.astype(bf16), "fsdp", axis=1, tiled=True),
         lax.all_gather(out_weight.astype(bf16), "fsdp", axis=1, tiled=True),
@@ -110,7 +114,11 @@
     q_blocks = queries.reshape(seqs_here, local_blocks, BLK, heads_local, HD)
     head_rows = queries[:, : 2 * BLK].reshape(seqs_here, 2 * BLK, heads_local, HD)
     blocked = gathered.reshape(seqs_here, block_count, BLK, 2, width_local)
-    picked = jax.vmap(lambda source, chosen: source[chosen])(blocked, safe)
+    flat = blocked.reshape(seqs_here * block_count, BLK, 2, width_local)
+    offset = jnp.arange(seqs_here, dtype=jnp.int32)[:, None, None] * block_count
+    picked = lax.map(
+        lambda at: lax.dynamic_index_in_dim(flat, at, 0, keepdims=False), (safe + offset).reshape(-1)
+    ).reshape(seqs_here, local_blocks, 8, BLK, 2, width_local)
     key_rows = picked[..., 0, :].reshape(seqs_here, local_blocks, 8 * BLK, heads_local, HD)
     value_rows = picked[..., 1, :].reshape(seqs_here, local_blocks, 8 * BLK, heads_local, HD)
     scores = (
@@ -329,6 +337,638 @@
     )
 
 
+def remote(src, dst, send, recv, dev):
+    return pltpu.make_async_remote_copy(
+        src_ref=src, dst_ref=dst, send_sem=send, recv_sem=recv, device_id=dev, device_id_type=MESH
+    )
+
+
+def dot_nn(a, b):
+    return lax.dot_general(a, b, (((1,), (0,)), ((), ())), preferred_element_type=f32)
+
+
+def dot_nt(a, b):
+    return lax.dot_general(a, b, (((1,), (1,)), ((), ())), preferred_element_type=f32)
+
+
+def dot_tn(a, b):
+    return lax.dot_general(a, b, (((0,), (0,)), ((), ())), preferred_element_type=f32)
+
+
+UW = 1792
+
+
+class Peers:
+    def __init__(self):
+        f, c, t = lax.axis_index("fsdp"), lax.axis_index("ctx"), lax.axis_index("tp")
+        x, k = f // 2, f % 2
+        self.f, self.c, self.t = f, c, t
+        self.f_core = x * 2 + (1 - k)
+        self.f_x = (1 - x) * 2 + k
+        self.f_xc = (1 - x) * 2 + (1 - k)
+        self.core = (self.f_core, c, t)
+        self.xdev = (self.f_x, c, t)
+        self.ydev = (f, 1 - c, t)
+
+    def z(self, t):
+        return (self.f, self.c, t)
+
+    def barrier(self):
+        sem = pltpu.get_barrier_semaphore()
+        for dev in (self.core, self.xdev, self.ydev, *(self.z((self.t + d) % 4) for d in (1, 2, 3))):
+            pl.semaphore_signal(sem, inc=1, device_id=dev, device_id_type=MESH)
+        pl.semaphore_wait(sem, 6)
+
+
+def forward_attention_kernel(
+    lengths_ref,
+    tokens_ref,
+    teacher_ref,
+    qkvb_ref,
+    upack_ref,
+    rbt_ref,
+    mask_ref,
+    att_ref,
+    u_ref,
+    t_ref,
+    w_ref,
+    q_ref,
+    k_ref,
+    v_ref,
+    kt_ref,
+    pt_ref,
+    tok_ref,
+    teach_ref,
+    live_ref,
+    vt,
+    bias,
+    rb,
+    att_out,
+    att_tok,
+    loc_sem,
+    w_sem,
+    y_sem,
+    z_send,
+    z_recv,
+    x_send,
+    x_recv,
+    yw_send,
+    yw_recv,
+    c_send,
+    c_recv,
+    h_send,
+    h_recv,
+    a_send,
+    a_recv,
+):
+    me = Peers()
+    f, c, t = me.f, me.c, me.t
+    seq = t_ref.shape[0]
+    half = seq // 2
+    rows_f = qkvb_ref.shape[1]
+    me.barrier()
+    sends = []
+
+    def go(copy, pred=None):
+        if pred is None:
+            copy.start()
+        else:
+            pl.when(pred)(copy.start)
+        sends.append((copy, pred))
+
+    own_rows = pl.ds(pl.multiple_of(c * half, half), half)
+    go(remote(tokens_ref.at[1 - c], t_ref.at[own_rows], y_sem.at[0], y_sem.at[1], me.ydev))
+    go(remote(rbt_ref.at[1 - c], rb.at[c], y_sem.at[2], y_sem.at[3], me.ydev))
+    go(remote(mask_ref.at[1 - c, t], live_ref.at[c], y_sem.at[4], y_sem.at[5], me.ydev))
+    part = pl.ds(pl.multiple_of(t * 128, 128), 128)
+    go(remote(teacher_ref.at[1 - c, part], teach_ref.at[c], y_sem.at[6], y_sem.at[7], me.ydev))
+
+    def wblock(ff):
+        return w_ref.at[:, pl.ds(pl.multiple_of(ff * rows_f, rows_f), rows_f), :]
+
+    go(remote(qkvb_ref, wblock(f), w_sem.at[0], w_sem.at[1], me.xdev))
+    go(remote(qkvb_ref, wblock(f), w_sem.at[2], w_sem.at[3], me.core))
+
+    def shard(tt, ff):
+        return u_ref.at[tt, pl.ds(pl.multiple_of(ff * rows_f, rows_f), rows_f), :]
+
+    hrows = rows_f // 2
+
+    def slab(tt, ff, h):
+        return u_ref.at[tt, pl.ds(pl.multiple_of(ff * rows_f + h * hrows, hrows), hrows), :]
+
+    def own_half(h):
+        return upack_ref.at[pl.ds(pl.multiple_of(h * hrows, hrows), hrows), :]
+
+    hs = (c, 1 - c)
+    go(remote(own_half(c), slab(t, f, c), x_send.at[t], x_recv.at[t], me.xdev))
+    for i in (0, 1):
+        go(remote(own_half(hs[i]), slab(t, f, hs[i]), z_send.at[0, t, i], z_recv.at[t, i], me.z(t + 1)), t < 3)
+        go(remote(own_half(hs[i]), slab(t, f, hs[i]), z_send.at[1, t, i], z_recv.at[t, i], me.z(t - 1)), t > 0)
+    go(remote(upack_ref, shard(t, f), c_send.at[t], c_recv.at[t], me.core))
+
+    local = [
+        pltpu.make_async_copy(tokens_ref.at[c], t_ref.at[own_rows], loc_sem.at[0]),
+        pltpu.make_async_copy(qkvb_ref, wblock(f), loc_sem.at[1]),
+        pltpu.make_async_copy(upack_ref, shard(t, f), loc_sem.at[2]),
+        pltpu.make_async_copy(teacher_ref.at[c, part], teach_ref.at[c], loc_sem.at[3]),
+    ]
+    for copy in local:
+        copy.start()
+    rb[c] = rbt_ref[c]
+    live_ref[c] = mask_ref[c, t]
+
+    def z_step(d):
+        for tt, ok, on, nxt, way in ((t - d, t - d >= 0, t < 3, t + 1, 0), (t + d, t + d <= 3, t > 0, t - 1, 1)):
+            go_on = ok & on
+            for i in (0, 1):
+                piece = slab(tt, f, hs[i])
+                arrived = remote(piece, piece, z_send.at[way, tt, i], z_recv.at[tt, i], me.z(t))
+                pl.when(ok)(arrived.wait_recv)
+                go(remote(piece, piece, z_send.at[way, tt, i], z_recv.at[tt, i], me.z(nxt)), go_on)
+                if i == 0:
+                    go(remote(piece, piece, x_send.at[tt], x_recv.at[tt], me.xdev), ok)
+            go(remote(shard(tt, f), shard(tt, f), c_send.at[tt], c_recv.at[tt], me.core), ok)
+
+    def around(d):
+        return ((t, None),) if d == 0 else ((t - d, t - d >= 0), (t + d, t + d <= 3))
+
+    def when(ok, fn):
+        if ok is None:
+            fn()
+        else:
+            pl.when(ok)(fn)
+
+    def x_step(d):
+        for tt, ok in around(d):
+            piece = slab(tt, me.f_x, c)
+            when(ok, remote(piece, piece, x_send.at[tt], x_recv.at[tt], me.xdev).wait_recv)
+            go(remote(piece, piece, yw_send.at[tt], yw_recv.at[tt], me.ydev), ok)
+            go(remote(piece, piece, h_send.at[tt, 0], h_recv.at[tt, 0], me.core), ok)
+
+    def y_step(d):
+        for tt, ok in around(d):
+            piece = slab(tt, me.f_x, 1 - c)
+            when(ok, remote(piece, piece, yw_send.at[tt], yw_recv.at[tt], me.ydev).wait_recv)
+            go(remote(piece, piece, h_send.at[tt, 1], h_recv.at[tt, 1], me.core), ok)
+
+    remote(wblock(me.f_x), wblock(me.f_x), w_sem.at[0], w_sem.at[1], me.xdev).wait_recv()
+    go(remote(wblock(me.f_x), wblock(me.f_x), w_sem.at[4], w_sem.at[5], me.core))
+    remote(wblock(me.f_core), wblock(me.f_core), w_sem.at[2], w_sem.at[3], me.core).wait_recv()
+    for copy in local[:2]:
+        copy.wait()
+    remote(wblock(me.f_xc), wblock(me.f_xc), w_sem.at[4], w_sem.at[5], me.core).wait_recv()
+
+    width = q_ref.shape[0] * HD
+    heads = q_ref.shape[0]
+
+    def project(base, count):
+        def step(i, carry):
+            rows = pl.ds(pl.multiple_of(base + i * 256, 256), 256)
+            piece = t_ref[rows, :]
+            for j, ref in enumerate((q_ref, k_ref, v_ref)):
+                made = dot_nn(piece, w_ref[j])
+                for h in range(heads):
+                    ref[h, rows, :] = made[:, h * HD : (h + 1) * HD].astype(bf16)
+                if j:
+                    (kt_ref if j == 1 else vt)[:, rows] = made.T.astype(bf16)
+            return carry
+
+        lax.fori_loop(0, count, step, 0)
+
+    project(c * half, half // 256)
+    x_step(0)
+    other_rows = pl.ds(pl.multiple_of((1 - c) * half, half), half)
+    remote(t_ref.at[other_rows], t_ref.at[other_rows], y_sem.at[0], y_sem.at[1], me.ydev).wait_recv()
+    project((1 - c) * half, half // 256)
+    remote(rb.at[1 - c], rb.at[1 - c], y_sem.at[2], y_sem.at[3], me.ydev).wait_recv()
+
+    length = lengths_ref[c]
+    nblk = seq // BLK
+    pos_block = lax.broadcasted_iota(jnp.int32, (128, seq), 1) // BLK
+    row = lax.broadcasted_iota(jnp.int32, (128, seq), 0)
+    picks = dot_nn(rb[0].astype(bf16), (pos_block == row).astype(bf16)) + dot_nn(
+        rb[1].astype(bf16), (pos_block == row + nblk // 2).astype(bf16)
+    )
+    key_block = lax.broadcasted_iota(jnp.int32, (nblk, seq), 0)
+    query = lax.broadcasted_iota(jnp.int32, (nblk, seq), 1)
+    own = query // BLK
+
+    def same(a, b):
+        return (a == b).astype(f32)
+
+    times = same(key_block, 0) + same(key_block, 1) + same(key_block, own - 1)
+    times += same(key_block, own) + same(key_block, own + 1)
+    for j in range(3):
+        times += same(key_block.astype(f32), picks[j : j + 1, :])
+    times = jnp.where(query < 2 * BLK, 1.0, times)
+    level = jnp.where(times > 0, jnp.log2(jnp.maximum(times, 1.0)), negative)
+    for b in range(nblk):
+        place = b * BLK + lax.broadcasted_iota(jnp.int32, (BLK, seq), 0)
+        bias[b * BLK : (b + 1) * BLK, :] = jnp.where(
+            place < length, jnp.broadcast_to(level[b : b + 1, :], (BLK, seq)), negative
+        )
+
+    factor = HD ** (-0.5) * 1.4426950408889634
+    wide = 256
+
+    def attend(h):
+        def step(i, carry):
+            cols = pl.ds(pl.multiple_of(i * wide, wide), wide)
+            scores = dot_nt(k_ref[h], q_ref[h, cols, :]) * factor + bias[:, cols]
+            top = jnp.max(scores, 0, keepdims=True)
+            expo = jnp.exp2(scores - top)
+            probs = (expo * (1.0 / jnp.sum(expo, 0, keepdims=True))).astype(bf16)
+            pt_ref[h, :, cols] = probs
+            att_out[h * HD : (h + 1) * HD, cols] = dot_nn(vt[h * HD : (h + 1) * HD, :], probs)
+            return carry
+
+        lax.fori_loop(0, seq // wide, step, 0)
+
+    attend(0)
+    z_step(1)
+    x_step(1)
+    attend(1)
+    y_step(0)
+    attend(2)
+    for s in range(2):
+        for tt in range(4):
+            at = s * half + tt * 128
+            tok_at = att_out[:, at : at + 128].T.astype(bf16)
+            att_tok[s, tt] = tok_at
+    for d in (1, 2, 3):
+        to = (t + d) % 4
+        go(remote(att_tok.at[:, to], att_ref.at[t], a_send.at[d], a_recv.at[d], me.z(to)))
+    own_copy = pltpu.make_async_copy(att_tok.at[:, t], att_ref.at[t], loc_sem.at[4])
+    own_copy.start()
+    z_step(2)
+    x_step(2)
+    y_step(1)
+    z_step(3)
+    x_step(3)
+    y_step(2)
+    y_step(3)
+    for s in range(2):
+        tok_ref[s] = t_ref[pl.ds(pl.multiple_of(s * half + t * 128, 128), 128), :]
+    for d in (1, 2, 3):
+        src = (t + 4 - d) % 4
+        remote(att_ref.at[src], att_ref.at[src], a_send.at[d], a_recv.at[d], me.z(src)).wait_recv()
+    for tt in range(4):
+        whole = shard(tt, me.f_core)
+        remote(whole, whole, c_send.at[tt], c_recv.at[tt], me.core).wait_recv()
+        for i in (0, 1):
+            piece = slab(tt, me.f_xc, hs[i])
+            remote(piece, piece, h_send.at[tt, i], h_recv.at[tt, i], me.core).wait_recv()
+    there = live_ref.at[1 - c]
+    remote(there, there, y_sem.at[4], y_sem.at[5], me.ydev).wait_recv()
+    there = teach_ref.at[1 - c]
+    remote(there, there, y_sem.at[6], y_sem.at[7], me.ydev).wait_recv()
+    for copy in local[2:]:
+        copy.wait()
+    own_copy.wait()
+    for copy, pred in sends:
+        when(pred, copy.wait_send)
+
+
+def forward_attention(lengths, tokens, teacher, qkvb, upack, rbt, mask, seq):
+    heads = qkvb.shape[2] // HD
+    width = heads * HD
+    rows_f = qkvb.shape[1]
+    depth = rows_f * 4
+    vm = pl.BlockSpec(memory_space=pltpu.VMEM)
+    hbm = pl.BlockSpec(memory_space=pl.ANY)
+    dma = pltpu.SemaphoreType.DMA
+    outs = [
+        ((4, 2, 128, width), bf16, vm),
+        ((4, depth, UW), bf16, hbm),
+        ((seq, depth), bf16, vm),
+        ((3, depth, width), bf16, vm),
+        ((heads, seq, HD), bf16, vm),
+        ((heads, seq, HD), bf16, vm),
+        ((heads, seq, HD), bf16, vm),
+        ((width, seq), bf16, vm),
+        ((heads, seq, seq), bf16, vm),
+        ((2, 128, depth), bf16, vm),
+        ((2, 128, depth), bf16, vm),
+        ((2, 8, 128), f32, vm),
+    ]
+    return pl.pallas_call(
+        forward_attention_kernel,
+        name="forward_attention",
+        out_shape=[jax.ShapeDtypeStruct(s, d) for s, d, _ in outs],
+        in_specs=[pl.BlockSpec(memory_space=pltpu.SMEM), hbm, hbm, vm, vm, vm, vm],
+        out_specs=[m for _, _, m in outs],
+        scratch_shapes=[
+            pltpu.VMEM((width, seq), bf16),
+            pltpu.VMEM((seq, seq), f32),
+            pltpu.VMEM((2, 8, 128), f32),
+            pltpu.VMEM((width, seq), f32),
+            pltpu.VMEM((2, 4, 128, width), bf16),
+            dma((5,)),
+            dma((6,)),
+            dma((8,)),
+            dma((2, 4, 2)),
+            dma((4, 2)),
+            dma((4,)),
+            dma((4,)),
+            dma((4,)),
+            dma((4,)),
+            dma((4,)),
+            dma((4,)),
+            dma((4, 2)),
+            dma((4, 2)),
+            dma((4,)),
+            dma((4,)),
+        ],
+        compiler_params=pltpu.CompilerParams(
+            collective_id=0, has_side_effects=True, vmem_limit_bytes=VMEM_LIMIT
+        ),
+    )(lengths, tokens, teacher, qkvb, upack, rbt, mask)
+
+
+def column(row):
+    return row.T[:, 0:1]
+
+
+def layer_kernel(
+    lengths_ref,
+    count_ref,
+    att_ref,
+    u_ref,
+    tok_ref,
+    teach_ref,
+    live_ref,
+    out_ref,
+    err_ref,
+    g_ref,
+    gatt_ref,
+    gone_ref,
+    act,
+    slope,
+):
+    c, t = lax.axis_index("ctx"), lax.axis_index("tp")
+    depth = tok_ref.shape[2]
+    rows = 2 * 128
+    length = lengths_ref[c]
+    inv_width = 1.0 / depth
+    norms = u_ref[0, :, 1728:1736].astype(f32).T
+    gains = [norms[i : i + 1, :] for i in range(4)]
+
+    def both(ref):
+        return ref[...].reshape(rows, depth).astype(f32)
+
+    def mean(v):
+        return jnp.sum(v, -1, keepdims=True) * inv_width
+
+    def normalize(v):
+        center = v - mean(v)
+        inverse = lax.rsqrt(mean(center * center) + norm_eps)
+        return center * inverse, inverse
+
+    def back(up, normed, inverse, gain):
+        scaled = up * gain
+        return inverse * (scaled - mean(scaled) - normed * mean(scaled * normed))
+
+    att = [att_ref[tt].reshape(rows, att_ref.shape[3]) for tt in range(4)]
+    attn = dot_nt(att[0], u_ref[0, :, 1536:1728])
+    for tt in range(1, 4):
+        attn += dot_nt(att[tt], u_ref[tt, :, 1536:1728])
+    normed_one, inverse_one = normalize(both(tok_ref) + attn)
+    hidden = normed_one * gains[0] + gains[1]
+    hidden_b = hidden.astype(bf16)
+    cube = 0.044715
+    root = 0.7978845608028654
+
+    def up_step(tt, mixed):
+        upper = dot_nn(hidden_b, u_ref[tt, :, 0:768])
+        square = upper * upper
+        th = jnp.tanh(root * upper * (1.0 + cube * square))
+        act_t = (0.5 * upper * (1.0 + th)).astype(bf16)
+        act[tt] = act_t
+        slope[tt] = 0.5 * (1.0 + th) + 0.5 * upper * (1.0 - th * th) * root * (1.0 + 3.0 * cube * square)
+        return mixed + dot_nt(act_t, u_ref[tt, :, 768:1536])
+
+    mixed = lax.fori_loop(0, 4, up_step, jnp.zeros((rows, depth), f32))
+    normed_two, inverse_two = normalize(hidden + mixed)
+    result = normed_two * gains[2] + gains[3]
+    out_ref[...] = result.astype(bf16).reshape(2, 128, depth)
+    alive = jnp.concatenate([column(live_ref[0]), column(live_ref[1])], 0)
+    row = lax.broadcasted_iota(jnp.int32, (rows, 1), 0)
+    place = jnp.where(row < 128, row, row - 128 + 512) + t * 128
+    live = jnp.where((alive == 1.0) & (place < length), 1.0, 0.0)
+    differ = result - both(teach_ref)
+    weighed = differ * live
+    err_ref[0, 0] = jnp.sum(weighed * differ)
+    grad_y = weighed * (2.0 / (count_ref[0, 0] * depth))
+    sums = [None] * 4
+    sums[2] = jnp.sum(grad_y * normed_two, 0, keepdims=True)
+    sums[3] = jnp.sum(grad_y, 0, keepdims=True)
+    grad_two = back(grad_y, normed_two, inverse_two, gains[2])
+    gm = grad_two.astype(bf16)
+    gm_t = grad_two.T.astype(bf16)
+    hidden_t = hidden.T.astype(bf16)
+
+    def down_step(tt, total):
+        ga = dot_nn(gm, u_ref[tt, :, 768:1536])
+        gu = (ga * slope[tt]).astype(bf16)
+        g_ref[tt, :, 768:1536] = dot_nn(gm_t, act[tt]).astype(bf16)
+        g_ref[tt, :, 0:768] = dot_nn(hidden_t, gu).astype(bf16)
+        return total + dot_nt(gu, u_ref[tt, :, 0:768])
+
+    grad_hidden = lax.fori_loop(0, 4, down_step, grad_two)
+    sums[0] = jnp.sum(grad_hidden * normed_one, 0, keepdims=True)
+    sums[1] = jnp.sum(grad_hidden, 0, keepdims=True)
+    grad_one = back(grad_hidden, normed_one, inverse_one, gains[0])
+    gone_ref[...] = grad_one.reshape(2, 128, depth)
+    ga = grad_one.astype(bf16)
+    ga_t = grad_one.T.astype(bf16)
+    norm_rows = jnp.concatenate(sums + [jnp.zeros((4, depth), f32)], 0)
+    norm_cols = jnp.concatenate([norm_rows.T, jnp.zeros((depth, UW - 1736), f32)], 1).astype(bf16)
+    for tt in range(4):
+        back_t = dot_nn(ga, u_ref[tt, :, 1536:1728]).astype(bf16)
+        gatt_ref[tt] = back_t.reshape(2, 128, back_t.shape[1])
+        g_ref[tt, :, 1536:1728] = dot_nn(ga_t, att[tt]).astype(bf16)
+        g_ref[tt, :, 1728:1792] = norm_cols
+
+
+def layer(lengths, count, att, u, tok, teach, live):
+    depth = tok.shape[2]
+    vm = pl.BlockSpec(memory_space=pltpu.VMEM)
+    smem = pl.BlockSpec(memory_space=pltpu.SMEM)
+    return pl.pallas_call(
+        layer_kernel,
+        name="layer",
+        out_shape=[
+            jax.ShapeDtypeStruct((2, 128, depth), bf16),
+            jax.ShapeDtypeStruct((1, 1), f32),
+            jax.ShapeDtypeStruct((4, depth, UW), bf16),
+            jax.ShapeDtypeStruct(att.shape, bf16),
+            jax.ShapeDtypeStruct((2, 128, depth), f32),
+        ],
+        in_specs=[smem, smem, vm, vm, vm, vm, vm],
+        out_specs=[vm, smem, vm, vm, vm],
+        scratch_shapes=[
+            pltpu.VMEM((4, 256, 768), bf16),
+            pltpu.VMEM((4, 256, 768), f32),
+        ],
+        compiler_params=pltpu.CompilerParams(vmem_limit_bytes=VMEM_LIMIT),
+    )(lengths, count, att, u, tok, teach, live)
+
+
+def attention_back_kernel(
+    do_ref, q_ref, k_ref, v_ref, kt_ref, pt_ref, t_ref, w_ref, part_ref, grad_ref, do, dqt, dk, dv, proj
+):
+    heads, seq = q_ref.shape[0], q_ref.shape[1]
+    width = heads * HD
+    scale = HD ** (-0.5)
+    wide = 256
+    for h in range(heads):
+        do[h] = do_ref[:, h * HD : (h + 1) * HD]
+    for h in range(heads):
+        dk[...] = jnp.zeros_like(dk)
+        dv[...] = jnp.zeros_like(dv)
+
+        def step(i, carry):
+            cols = pl.ds(pl.multiple_of(i * wide, wide), wide)
+            mine = do[h, cols, :]
+            probs = pt_ref[h, :, cols]
+            gp = dot_nt(v_ref[h], mine)
+            pf = probs.astype(f32)
+            mix = jnp.sum(pf * gp, 0, keepdims=True)
+            gs = (pf * (gp - mix)).astype(bf16)
+            dk[...] += dot_nn(gs, q_ref[h, cols, :])
+            dv[...] += dot_nn(probs, mine)
+            dqt[h * HD : (h + 1) * HD, cols] = dot_nn(kt_ref[h * HD : (h + 1) * HD, :], gs)
+            return carry
+
+        lax.fori_loop(0, seq // wide, step, 0)
+        proj[1, :, h * HD : (h + 1) * HD] = (dk[...] * scale).astype(bf16)
+        proj[2, :, h * HD : (h + 1) * HD] = dv[...].astype(bf16)
+    proj[0] = (dqt[...].T * scale).astype(bf16)
+
+    def rows_step(i, carry):
+        rows = pl.ds(pl.multiple_of(i * 256, 256), 256)
+        total = dot_nt(proj[0, rows, :], w_ref[0])
+        for j in (1, 2):
+            total += dot_nt(proj[j, rows, :], w_ref[j])
+        part_ref[rows, :] = total.astype(bf16)
+        return carry
+
+    lax.fori_loop(0, seq // 256, rows_step, 0)
+    for j in range(3):
+        grad_ref[j] = dot_tn(t_ref[...], proj[j]).astype(bf16)
+
+
+def attention_back(do, q, k, v, kt, pt, tokens, w):
+    heads, seq = q.shape[:2]
+    width = heads * HD
+    vm = pl.BlockSpec(memory_space=pltpu.VMEM)
+    return pl.pallas_call(
+        attention_back_kernel,
+        name="attention_back",
+        out_shape=[
+            jax.ShapeDtypeStruct(tokens.shape, bf16),
+            jax.ShapeDtypeStruct(w.shape, bf16),
+        ],
+        in_specs=[vm] * 8,
+        out_specs=[vm] * 2,
+        scratch_shapes=[
+            pltpu.VMEM((heads, seq, HD), bf16),
+            pltpu.VMEM((width, seq), f32),
+            pltpu.VMEM((seq, HD), f32),
+            pltpu.VMEM((seq, HD), f32),
+            pltpu.VMEM((3, seq, width), bf16),
+        ],
+        compiler_params=pltpu.CompilerParams(vmem_limit_bytes=VMEM_LIMIT),
+    )(do, q, k, v, kt, pt, tokens, w)
+
+
+def body_swapped(
+    tokens,
+    teacher,
+    lengths,
+    valid_mask,
+    random_blocks,
+    step_count,
+    qkv_weight,
+    out_weight,
+    up_weight,
+    down_weight,
+    norm_params,
+    qkv_moment,
+    qkv_square,
+    out_moment,
+    out_square,
+    up_moment,
+    up_square,
+    down_moment,
+    down_square,
+    norm_moment,
+    norm_square,
+):
+    c, t = lax.axis_index("ctx"), lax.axis_index("tp")
+    seqs, tok_count, width = tokens.shape
+    seq = tok_count * 2
+    upack = jnp.concatenate(
+        [
+            up_weight,
+            down_weight.T,
+            out_weight.T,
+            norm_params.T,
+            jnp.zeros((192, 60), f32),
+        ],
+        1,
+    ).astype(bf16)
+    qkvb = qkv_weight.astype(bf16)
+    rbt = jnp.pad(
+        jnp.swapaxes(random_blocks, 1, 2).astype(f32), ((0, 0), (0, 5), (0, 120))
+    )
+    mask = jnp.broadcast_to(valid_mask.reshape(seqs, 4, 1, 128).astype(f32), (seqs, 4, 8, 128))
+    positions = c * tok_count + jnp.arange(tok_count, dtype=jnp.int32)
+    live_rows = ((valid_mask == 1) & (positions[None, :] < lengths[:, None])).astype(f32)
+    live_count = lax.psum(jnp.sum(live_rows), ("fsdp", "ctx"))
+    att, u, tk, w, q, k, v, kt, pt, tok, teach, live = forward_attention(
+        lengths, tokens, teacher, qkvb, upack, rbt, mask, seq
+    )
+    out_part, err, g, gatt, gone = layer(lengths, live_count.reshape(1, 1), att, u, tok, teach, live)
+    do = lax.all_to_all(gatt, "tp", 0, 0)
+    do = jnp.swapaxes(do, 0, 1).reshape(seq, att.shape[3])
+    part, qkv_part = attention_back(do, q, k, v, kt, pt, tk, w)
+    error_total = lax.psum(err[0, 0], ("fsdp", "ctx", "tp"))
+    loss_value = error_total / (live_count * width)
+
+    def spread(piece):
+        swapped = lax.all_to_all(piece, "ctx", 0, 0)
+        return lax.all_gather(swapped, "tp", axis=1, tiled=True)
+
+    layer_out = spread(out_part)
+    summed = lax.psum_scatter(part.reshape(2, 4, 128, width), "tp", scatter_dimension=1, tiled=False)
+    input_grad = spread((summed.astype(f32) + gone).astype(bf16)).astype(f32)
+    g = lax.psum_scatter(g, "tp", scatter_dimension=0, tiled=False)
+    g = lax.psum_scatter(g, "fsdp", scatter_dimension=0, tiled=True)
+    g = lax.psum(g, "ctx").astype(f32)
+    qkv_grad = lax.psum_scatter(qkv_part, "fsdp", scatter_dimension=1, tiled=True)
+    qkv_grad = lax.psum(qkv_grad, "ctx").astype(f32)
+    up_grad, down_grad, out_grad, norm_grad = g[:, :768], g[:, 768:1536].T, g[:, 1536:1728].T, g[:, 1728:1732].T
+    shards = (qkv_grad, out_grad, up_grad, down_grad, norm_grad)
+    squares = sum(jnp.sum(m * m) for m in shards[:4]) + jnp.where(t == 0, jnp.sum(norm_grad * norm_grad), 0.0)
+    grad_norm = jnp.sqrt(lax.psum(squares, ("fsdp", "tp")))
+    factor = jnp.minimum(1.0, clip_level / (grad_norm + 1e-06))
+    steps_done = step_count[0].astype(f32)
+    state = (
+        (qkv_weight, qkv_moment, qkv_square),
+        (out_weight, out_moment, out_square),
+        (up_weight, up_moment, up_square),
+        (down_weight, down_moment, down_square),
+        (norm_params, norm_moment, norm_square),
+    )
+    new = [
+        adam_update(weight, grad, moment, square, factor, steps_done, rate)
+        for (weight, moment, square), grad, rate in zip(state, shards, rate_list)
+    ]
+    return (layer_out, loss_value, input_grad, grad_norm, *(v for group in new for v in group))
+
+
 def solution(mesh):
     in_specs = (
         P("fsdp", "ctx", None),
@@ -374,4 +1014,7 @@
         P(None, "fsdp"),
         P(None, "fsdp"),
     )
+    sizes = dict(mesh.shape)
+    small = sizes == {"fsdp": 4, "ctx": 2, "tp": 4}
+    body = body_swapped if small else body_general
     return jax.shard_map(body, mesh=mesh, in_specs=in_specs, out_specs=out_specs, check_vma=False)

time: 866 us -> 626 us (0.72)
  local copies, waits for them, and re-layouts: 165 us -> 23.2 us
  Pallas kernels: 0 us -> 134 us
  other arithmetic: 121 us -> 21.1 us
  waiting for transfers between devices: 376 us -> 288 us
  matrix products: 78.6 us -> 0 us
  blocking collectives: 92.5 us -> 135 us
    psum x5 -> x1, waiting for transfers between devices: 271 us -> 23.4 us  [body_swapped(): qkv_grad = lax.psum(qkv_grad, 'ctx').astype(f32)]
    reduce_scatter x3 -> x4, waiting for transfers between devices: 67.6 us -> 233 us  [the longest x1 140 us: body_swapped(): g = lax.psum_scatter(g, 'tp', scatter_dimension=0, tiled=False)]
    pallas_call x0 -> x3, Pallas kernels: none -> 134 us  [the longest x1 87.8 us: forward_attention(): pl.pallas_call(forward_attention_kernel, name='forward_attention', out_sh...]
    dot_general x24 -> x0, matrix products: 78.6 us -> none  [the longest x1 9.17 us: body(): jnp.einsum('sbqhd,sbkhd->sbhqk', sparse_grad, value_rows, preferred_eleme...]
    another operation x15 -> x1, local copies, waits for them, and re-layouts: 68.8 us -> 0.15 us  [the longest x3 44.1 us: body(): jnp.stack([dk_rows.reshape(seqs_here, local_blocks, 8, BLK, width_local),...]
    all_to_all x0 -> x3, blocking collectives: none -> 47.3 us  [the longest x1 27.5 us: body_swapped(): do = lax.all_to_all(gatt, 'tp', 0, 0)]
    unnamed x168 -> x53, local copies, waits for them, and re-layouts: 53.3 us -> 15 us
    scatter-add x1 -> x0, other arithmetic: 37.7 us -> none  [body(): kv_term = jnp.zeros((block_count, seqs_here, BLK, 2, width_local), f32).a...]
  transfers between devices with their start and end apart: 14 -> 7, of which waited for: 10 -> 6; matrix products, arithmetic and copies ran while one was open for 10% -> 2% of each run, Pallas kernels for 0% -> 4%
where the time goes in v1:
time: 626 us; the launch traced here: 625 us
  waiting for transfers between devices  288 us (46%)
  blocking collectives  135 us (22%)
  Pallas kernels  134 us (21%)
  local copies, waits for them, and re-layouts  23.2 us (4%)
  between operations  22.8 us (4%)
  other arithmetic  21.1 us (3%)
    reduce_scatter x1, waiting for transfers between devices, body_swapped(): g = lax.psum_scatter(g, 'tp', scatter_dimension=0, tiled=False)  140 us
    pallas_call x1, Pallas kernels, forward_attention(): pl.pallas_call(forward_attention_kernel, name='forward_attention', out_sh...  87.8 us
    psum x1, blocking collectives, body_swapped(): error_total = lax.psum(err[0, 0], ('fsdp', 'ctx', 'tp'))  40.3 us
    reduce_scatter x1, waiting for transfers between devices, body_swapped(): g = lax.psum_scatter(g, 'fsdp', scatter_dimension=0, tiled=True)  38.2 us
    reduce_scatter x1, waiting for transfers between devices, body_swapped(): lax.psum_scatter(part.reshape(2, 4, 128, width), 'tp', scatter_dimension=...  38 us
    psum x1, blocking collectives, body_swapped(): grad_norm = jnp.sqrt(lax.psum(squares, ('fsdp', 'tp')))  31.9 us
    all_gather x2, waiting for transfers between devices, spread(): return lax.all_gather(swapped, 'tp', axis=1, tiled=True)  31.5 us
    all_to_all x1, blocking collectives, body_swapped(): do = lax.all_to_all(gatt, 'tp', 0, 0)  27.5 us
  transfers between devices with their start and end apart: 7, of which 6 were waited for; matrix products, arithmetic and copies ran while one was open for 2% of the time, Pallas kernels for 4%

profile of v1, /device:TPU:0, one launch (start us, length us, event | category | flops | bytes accessed | tf_op | source)
XLA Modules:
  0.0 625.0 jit_solution(774231204151465229)
XLA Ops:
  7.3 1.1 copy.89
  11.3 15.8 %psum.35 = f32[]{:T(128)} all-reduce(f32[]{:T(128)} %fusion.13), channel_id=1, replica_groups=mesh['fsdp'=4,'ctx'=2,'tp'=4] {'fsdp','ctx'}, use_global_device_ids=true, to_apply=%region_1.2 | all-reduce | flops 1 | bytes 8 | tf_op jit(solution)/shard_map/psum | solution.py:929
  29.3 87.8 %forward_attention.1 = (bf16[4,2,128,192]{3,2,1,0:T(8,128)(2,1)}, bf16[4,768,1792]{2,1,0:T(8,128)(2,1)}, bf16[1024,768]{1,0:T(8,128)(2,1)}, bf16[3,768,192]{2,1,...) custom-call(s32[2]{0:T(128)} %lengths_ref.3, ...), custom_call_target="tpu_custom_call" | custom-call | tf_op jit(solution)/shard_map/forward_attention/pallas_call | solution.py:655
  117.2 24.3 %layer.1 = (bf16[2,128,768]{2,1,0:T(8,128)(2,1)}, f32[1,1]{1,0:T(1,128)}, bf16[4,768,1792]{2,1,0:T(8,128)(2,1)}, bf16[4,2,128,192]{3,2,1,0:T(8,128)(2,1)}, f32[2,128,768]{2,1,0:T(8,128)}) custom-call(s32[2]{0:T(128)} %lengths_ref.3, f32[1,1]{1,0:T(1,128)} %bitcast.count_ref, bf16[4,2,128,192]{3,2,1,0:T(8,128)(2,1)} %get-tuple-element.38.att_ref, ...), custom_call_target="tpu_custom_call" | custom-call | tf_op jit(solution)/shard_map/layer/pallas_call | solution.py:798
  142.8 27.5 %all_to_all.15 = bf16[4,2,128,192]{2,3,1,0:T(8,128)(2,1)S(1)} all-to-all(bf16[4,2,128,192]{2,3,1,0:T(8,128)(2,1)S(1)} %copy.92), channel_id=1, replica_groups=mesh['fsdp'=4,'ctx'=2,'tp'=4] {'tp'}, dimensions={0} | all-to-all | bytes 786432 | tf_op jit(solution)/shard_map/all_to_all | solution.py:934
  171.3 22.1 %attention_back.1 = (bf16[1024,768]{1,0:T(8,128)(2,1)}, bf16[3,768,192]{2,1,0:T(8,128)(2,1)}) custom-call(bf16[1024,192]{1,0:T(8,128)(2,1)} %bitcast.40, bf16[3,1024,64]{2,1,0:T(8,128)(2,1)} %get-tuple-element.46.q_ref, bf16[3,1024,64]{2,1,0:T(8,128)(2,1)} %get-tuple-element.47.k_ref, bf16[3,1024,64]{2,1,0:T(8,128)(2,1)} %get-tuple-element.48.v_ref, ...), custom_call_target="tpu_custom_call" | custom-call | tf_op jit(solution)/shard_map/attention_back/pallas_call | solution.py:866
  193.5 139.9 %reduce-scatter.9.cloned.1.call-done = bf16[1,768,1792]{2,1,0:T(8,128)(2,1)} async-done(((bf16[4,768,1792]{2,1,0:T(8,128)(2,1)}), bf16[1,768,1792]{2,1,0:T(8,128)(2,1)}) %reduce-scatter.9.cloned.1.call-update) | async-done | bytes 2752528 | tf_op jit(solution)/shard_map/reduce_scatter | solution.py:947
  333.5 1.3 copy.94
  335.8 10.0 %all_to_all.16 = bf16[2,128,768]{2,1,0:T(8,128)(2,1)} all-to-all(bf16[2,128,768]{2,1,0:T(8,128)(2,1)S(1)} %copy-done.12), channel_id=1, replica_groups=mesh['fsdp'=4,'ctx'=2,'tp'=4] {'ctx'}, dimensions={0} | all-to-all | bytes 786432 | tf_op jit(solution)/shard_map/all_to_all | solution.py:941
  345.9 16.9 %reduce-scatter.7.cloned.1.call-done = bf16[3,192,192]{2,1,0:T(8,128)(2,1)} async-done(((bf16[3,768,192]{2,1,0:T(8,128)(2,1)}), bf16[3,192,192]{2,1,0:T(8,128)(2,1)}) %reduce-scatter.7.cloned.1.call-update) | async-done | bytes 221200 | tf_op jit(solution)/shard_map/reduce_scatter | solution.py:950
  362.7 38.2 %reduce-scatter.11.cloned.1.call-done = bf16[192,1792]{1,0:T(8,128)(2,1)} async-done(((bf16[768,1792]{1,0:T(8,128)(2,1)}), bf16[192,1792]{1,0:T(8,128)(2,1)}) %reduce-scatter.11.cloned.1.call-update) | async-done | bytes 688144 | tf_op jit(solution)/shard_map/reduce_scatter | solution.py:948
  401.1 38.0 %reduce-scatter.5.cloned.1.call-done = bf16[2,1,128,768]{3,2,0,1:T(8,128)(2,1)} async-done(((bf16[2,4,128,768]{3,2,0,1:T(8,128)(2,1)}), bf16[2,1,128,768]{3,2,0,1:T(8,128)(2,1)}) %reduce-scatter.5.cloned.1.call-update) | async-done | bytes 393232 | tf_op jit(solution)/shard_map/reduce_scatter | solution.py:945
  439.1 1.1 fusion
  440.2 9.8 %all_to_all.17 = bf16[2,128,768]{2,1,0:T(8,128)(2,1)} all-to-all(bf16[2,128,768]{2,1,0:T(8,128)(2,1)S(1)} %fusion), channel_id=1, replica_groups=mesh['fsdp'=4,'ctx'=2,'tp'=4] {'ctx'}, dimensions={0} | all-to-all | bytes 786432 | tf_op jit(solution)/shard_map/all_to_all | solution.py:941
  450.0 40.3 %psum.36 = f32[]{:T(128)} all-reduce(f32[]{:T(128)} %bitcast.5), channel_id=1, replica_groups=mesh['fsdp'=4,'ctx'=2,'tp'=4] {'fsdp','ctx','tp'}, use_global_device_ids=true, to_apply=%region_2.3 | all-reduce | flops 1 | bytes 8 | tf_op jit(solution)/shard_map/psum | solution.py:937
  494.4 23.4 %all-reduce.4.cloned.1.call-done = (bf16[3,192,192]{2,1,0:T(8,128)(2,1)}, bf16[192,1792]{1,0:T(8,128)(2,1)}) async-done(((bf16[3,192,192]{2,1,0:T(8,128)(2,1)}, bf16[192,1792]{1,0:T(8,128)(2,1)}), (bf16[3,192,192]{2,1,0:T(8,128)(2,1)}, bf16[192,1792]{1,0:T(8,128)(2,1)})) %all-reduce.4.cloned.1.call-update) | async-done | bytes 909328 | tf_op jit(solution)/shard_map/psum | solution.py:951
  517.8 1.2 convert_element_type.59
  525.1 31.4 %all-gather.5.cloned.1.call-done = bf16[2,512,768]{2,1,0:T(8,128)(2,1)} async-done(((bf16[2,128,768]{2,1,0:T(8,128)(2,1)}), bf16[2,512,768]{2,1,0:T(8,128)(2,1)}) %all-gather.5.cloned.1.call-update) | async-done | bytes 1572880 | tf_op jit(solution)/shard_map/all_gather | solution.py:942
  556.5 3.3 convert_element_type.57
  559.8 31.9 %psum.39 = f32[]{:T(128)} all-reduce(f32[]{:T(128)S(6)} %add.129), channel_id=1, replica_groups=mesh['fsdp'=4,'ctx'=2,'tp'=4] {'fsdp','tp'}, use_global_device_ids=true, to_apply=%region_14.15 | all-reduce | flops 1 | bytes 8 | tf_op jit(solution)/shard_map/psum | solution.py:955
  592.5 1.8 multiply_divide_fusion
  596.0 1.5 sub.43
  597.6 1.6 copy.108
  599.1 1.6 copy.109
  600.7 1.6 copy.110
  603.2 1.7 copy.105
  604.9 1.7 copy.106
  606.6 1.7 copy.107
  608.3 2.8 multiply_subtract_fusion
  611.2 1.5 multiply_subtract_fusion.1
  612.7 1.5 multiply_subtract_fusion.2
  614.8 1.1 copy.118
  (89 shorter events, 16.6 us)
Async XLA Ops:
  7.2 2.4 copy-start
  7.2 2.4 copy-start.15
  7.2 2.6 copy-start.2
  7.2 326.2 %reduce-scatter.9.cloned.1.call-start = ((), (), s32[]{:S(2)}) async-start(), calls=%async_computation.11 | async-start | bytes 13762560 | tf_op jit(solution)/shard_map/reduce_scatter | solution.py:947
  8.4 2.1 copy-start.16
  8.4 2.1 copy-start.20
  8.4 2.2 copy-start.17
  141.5 1.0 copy-start.11
  141.5 221.2 %reduce-scatter.7.cloned.1.call-start = ((), (), s32[]{:S(2)}) async-start(), calls=%async_computation.10 | async-start | bytes 1474560 | tf_op jit(solution)/shard_map/reduce_scatter | solution.py:950
  193.5 140.0 %copy-start.4 = (bf16[1024,768]{1,0:T(8,128)(2,1)S(1)}, bf16[1024,768]{1,0:T(8,128)(2,1)}, u32[]{:S(2)}) copy-start(bf16[1024,768]{1,0:T(8,128)(2,1)} %get-tuple-element.53) | copy-start | bytes 4718596
  193.5 207.5 %reduce-scatter.11.cloned.1.call-start = ((), (), s32[]{:S(2)}) async-start(), calls=%async_computation.12 | async-start | bytes 3440640 | tf_op jit(solution)/shard_map/reduce_scatter | solution.py:948
  333.5 105.6 %reduce-scatter.5.cloned.1.call-start = ((), (), s32[]{:S(2)}) async-start(), calls=%async_computation.8 | async-start | bytes 1966080 | tf_op jit(solution)/shard_map/reduce_scatter | solution.py:945
  334.8 1.0 copy-start.12
  334.8 104.3 %copy-start.6 = (f32[2,128,768]{2,1,0:T(8,128)S(1)}, f32[2,128,768]{2,1,0:T(8,128)}, u32[]{:S(2)}) copy-start(f32[2,128,768]{2,1,0:T(8,128)} %get-tuple-element.54) | copy-start | bytes 2359300
  334.8 159.5 %all-gather.3.cloned.1.call-start = ((), (), s32[]{:S(2)}) async-start(), calls=%async_computation.7 | async-start | bytes 1966080 | tf_op jit(solution)/shard_map/all_gather | solution.py:942
  345.8 171.9 %all-reduce.4.cloned.1.call-start = ((), (), s32[]{:S(2)}) async-start(), calls=%async_computation.13 | async-start | bytes 1966080 | tf_op jit(solution)/shard_map/psum | solution.py:951
  401.0 90.2 %copy-start.18 = (f32[4,192]{1,0:T(4,128)S(1)}, f32[4,192]{1,0:T(4,128)}, u32[]{:S(2)}) copy-start(f32[4,192]{1,0:T(4,128)} %param.40) | copy-start | bytes 9220
  401.0 91.0 %copy-start.19 = (f32[4,192]{1,0:T(4,128)S(1)}, f32[4,192]{1,0:T(4,128)}, u32[]{:S(2)}) copy-start(f32[4,192]{1,0:T(4,128)} %param.41) | copy-start | bytes 9220
  401.0 91.7 %copy-start.13 = (f32[192,192]{1,0:T(8,128)S(1)}, f32[192,192]{1,0:T(8,128)}, u32[]{:S(2)}) copy-start(f32[192,192]{1,0:T(8,128)} %param.34) | copy-start | bytes 442372
  401.0 155.5 %all-gather.5.cloned.1.call-start = ((), (), s32[]{:S(2)}) async-start(), calls=%async_computation.9 | async-start | bytes 1966080 | tf_op jit(solution)/shard_map/all_gather | solution.py:942
  439.1 53.8 %copy-start.14 = (f32[192,192]{1,0:T(8,128)S(1)}, f32[192,192]{1,0:T(8,128)}, u32[]{:S(2)}) copy-start(f32[192,192]{1,0:T(8,128)} %param.35) | copy-start | bytes 442372
  517.8 1.9 copy-start.5
  608.3 2.9 copy-start.1
  608.3 2.9 copy-start.7
  608.3 2.9 copy-start.8
  611.2 1.5 copy-start.9
  611.2 1.5 copy-start.10
  612.7 2.0 copy-start.3
Sparse Core Ops, SparseCore 0:
  141.6 191.7 reduce-scatter.8
  336.6 26.0 reduce-scatter.6
  365.5 35.4 reduce-scatter.10
  403.7 35.3 reduce-scatter.4
  440.5 36.7 all-gather.2
  479.5 38.2 all-reduce.3
  519.4 37.0 all-gather.4

commit v2 on v1

--- a/solution.py
+++ b/solution.py
@@ -690,29 +690,116 @@
     return row.T[:, 0:1]
 
 
-def layer_kernel(
-    lengths_ref,
-    count_ref,
-    att_ref,
-    u_ref,
-    tok_ref,
-    teach_ref,
-    live_ref,
-    out_ref,
-    err_ref,
-    g_ref,
-    gatt_ref,
-    gone_ref,
-    act,
-    slope,
-):
-    c, t = lax.axis_index("ctx"), lax.axis_index("tp")
-    depth = tok_ref.shape[2]
+def add_rows(dst, a, b, step=16):
+    def one(i, carry):
+        rows = pl.ds(pl.multiple_of(i * step, step), step)
+        dst[rows, :] = a[rows, :] + b[rows, :]
+        return carry
+
+    lax.fori_loop(0, dst.shape[0] // step, one, 0)
+
+
+class Line:
+    def __init__(self, me, go, block, send, recv):
+        self.me, self.go, self.block, self.send, self.recv = me, go, block, send, recv
+
+    def start(self):
+        t = self.me.t
+        mine = self.block(t)
+        self.go(remote(mine, mine, self.send.at[0, t], self.recv.at[t], self.me.z(t + 1)), t < 3)
+        self.go(remote(mine, mine, self.send.at[1, t], self.recv.at[t], self.me.z(t - 1)), t > 0)
+
+    def step(self, d):
+        t = self.me.t
+        for tt, ok, on, nxt, way in ((t - d, t - d >= 0, t < 3, t + 1, 0), (t + d, t + d <= 3, t > 0, t - 1, 1)):
+            piece = self.block(tt)
+            pl.when(ok)(remote(piece, piece, self.send.at[way, tt], self.recv.at[tt], self.me.z(t)).wait_recv)
+            if d < 3:
+                self.go(remote(piece, piece, self.send.at[way, tt], self.recv.at[tt], self.me.z(nxt)), ok & on)
+
+
+class Chain:
+    def __init__(self, me, go, own, left, right, send, recv_l, recv_r):
+        self.me, self.go, self.own, self.left, self.right = me, go, own, left, right
+        self.send, self.recv_l, self.recv_r = send, recv_l, recv_r
+
+    def arrived(self, tt, way):
+        buf, recv = (self.left, self.recv_l) if way == 0 else (self.right, self.recv_r)
+        remote(buf(tt), buf(tt), self.send.at[tt], recv.at[tt], self.me.z(self.me.t)).wait_recv()
+
+    def pass_on(self, tt, way):
+        t = self.me.t
+        inner = (t > 0) if way == 0 else (t < 3)
+        ahead = (tt > t) if way == 0 else (tt < t)
+        buf, recv = (self.left, self.recv_l) if way == 0 else (self.right, self.recv_r)
+
+        @pl.when(ahead & inner)
+        def _():
+            self.arrived(tt, way)
+            add_rows(self.own(tt), self.own(tt), buf(tt))
+
+        to = self.me.z(t + 1 if way == 0 else t - 1)
+        self.go(remote(self.own(tt), buf(tt), self.send.at[tt], recv.at[tt], to), ahead)
+
+    def end(self):
+        t = self.me.t
+        mine = self.own(t)
+
+        @pl.when(t > 0)
+        def _():
+            self.arrived(t, 0)
+            add_rows(mine, mine, self.left(t))
+
+        @pl.when(t < 3)
+        def _():
+            self.arrived(t, 1)
+            add_rows(mine, mine, self.right(t))
+
+
+CHAIN_ORDER = ((3, 0), (0, 1), (2, 0), (1, 1), (1, 0), (2, 1))
+
+
+def backward_kernel(names, *refs):
+    r = dict(zip(names, refs, strict=True))
+    me = Peers()
+    f, c, t = me.f, me.c, me.t
+    x = f // 2
+    k = f % 2
+    depth = r["u"].shape[1]
+    rows_f = depth // 4
+    hrows = rows_f // 2
+    qrows = rows_f // 4
+    seq = r["t"].shape[0]
+    half = seq // 2
+    heads = r["q"].shape[0]
+    width = heads * HD
+    sends = []
+
+    def when(ok, fn):
+        if ok is None:
+            fn()
+        else:
+            pl.when(ok)(fn)
+
+    def go(copy, pred=None):
+        when(pred, copy.start)
+        sends.append((copy, pred))
+
+    loads = {}
+    order = ["att", "u0", "u1", "u2", "u3", "pt", "q", "k", "v", "kt", "w", "t"]
+    for i, name in enumerate(order):
+        if name[0] == "u":
+            j = int(name[1])
+            loads[name] = pltpu.make_async_copy(r["u"].at[j], r["u_v"].at[j], r["load_sem"].at[i])
+        else:
+            loads[name] = pltpu.make_async_copy(r[name], r[name + "_v"], r["load_sem"].at[i])
+        loads[name].start()
+    me.barrier()
+
+    att_v, u_v, g_v, act, slope = r["att_v"], r["u_v"], r["g_v"], r["act"], r["slope"]
     rows = 2 * 128
-    length = lengths_ref[c]
+    length = r["lengths"][c]
     inv_width = 1.0 / depth
-    norms = u_ref[0, :, 1728:1736].astype(f32).T
-    gains = [norms[i : i + 1, :] for i in range(4)]
 
     def both(ref):
         return ref[...].reshape(rows, depth).astype(f32)
@@ -729,37 +816,54 @@
         scaled = up * gain
         return inverse * (scaled - mean(scaled) - normed * mean(scaled * normed))
 
-    att = [att_ref[tt].reshape(rows, att_ref.shape[3]) for tt in range(4)]
-    attn = dot_nt(att[0], u_ref[0, :, 1536:1728])
+    for name in ("att", "u0", "u1", "u2", "u3"):
+        loads[name].wait()
+    norms = u_v[0, :, 1728:1736].astype(f32).T
+    gains = [norms[i : i + 1, :] for i in range(4)]
+    att = [att_v[tt].reshape(rows, width) for tt in range(4)]
+    attn = dot_nt(att[0], u_v[0, :, 1536:1728])
     for tt in range(1, 4):
-        attn += dot_nt(att[tt], u_ref[tt, :, 1536:1728])
-    normed_one, inverse_one = normalize(both(tok_ref) + attn)
+        attn += dot_nt(att[tt], u_v[tt, :, 1536:1728])
+    normed_one, inverse_one = normalize(both(r["tok"]) + attn)
     hidden = normed_one * gains[0] + gains[1]
     hidden_b = hidden.astype(bf16)
     cube = 0.044715
     root = 0.7978845608028654
 
     def up_step(tt, mixed):
-        upper = dot_nn(hidden_b, u_ref[tt, :, 0:768])
+        upper = dot_nn(hidden_b, u_v[tt, :, 0:768])
         square = upper * upper
         th = jnp.tanh(root * upper * (1.0 + cube * square))
         act_t = (0.5 * upper * (1.0 + th)).astype(bf16)
         act[tt] = act_t
-        slope[tt] = 0.5 * (1.0 + th) + 0.5 * upper * (1.0 - th * th) * root * (1.0 + 3.0 * cube * square)
-        return mixed + dot_nt(act_t, u_ref[tt, :, 768:1536])
+        bend = 0.5 * (1.0 + th) + 0.5 * upper * (1.0 - th * th) * root * (1.0 + 3.0 * cube * square)
+        slope[tt] = bend.astype(bf16)
+        return mixed + dot_nt(act_t, u_v[tt, :, 768:1536])
 
     mixed = lax.fori_loop(0, 4, up_step, jnp.zeros((rows, depth), f32))
     normed_two, inverse_two = normalize(hidden + mixed)
     result = normed_two * gains[2] + gains[3]
-    out_ref[...] = result.astype(bf16).reshape(2, 128, depth)
-    alive = jnp.concatenate([column(live_ref[0]), column(live_ref[1])], 0)
+
+    r["piece"][...] = result.astype(bf16).reshape(2, 128, depth)
+    part = pl.ds(pl.multiple_of(t * 128, 128), 128)
+    lo = r["lo"]
+    go(remote(r["piece"].at[1 - c], lo.at[c, part], r["s_sem"].at[0], r["s_sem"].at[1], me.ydev))
+    own_lo = pltpu.make_async_copy(r["piece"].at[c], lo.at[c, part], r["load_sem"].at[12])
+    own_lo.start()
+
+    def lo_block(tt):
+        return lo.at[:, pl.ds(pl.multiple_of(tt * 128, 128), 128), :]
+
+    lo_line = Line(me, go, lo_block, r["lo_send"], r["lo_recv"])
+
+    alive = jnp.concatenate([column(r["live"][0]), column(r["live"][1])], 0)
     row = lax.broadcasted_iota(jnp.int32, (rows, 1), 0)
-    place = jnp.where(row < 128, row, row - 128 + 512) + t * 128
+    place = jnp.where(row < 128, row, row - 128 + half) + t * 128
     live = jnp.where((alive == 1.0) & (place < length), 1.0, 0.0)
-    differ = result - both(teach_ref)
+    differ = result - both(r["teach"])
     weighed = differ * live
-    err_ref[0, 0] = jnp.sum(weighed * differ)
-    grad_y = weighed * (2.0 / (count_ref[0, 0] * depth))
+    r["err"][0, 0] = jnp.sum(weighed * differ)
+    grad_y = weighed * (2.0 / (r["count"][0, 0] * depth))
     sums = [None] * 4
     sums[2] = jnp.sum(grad_y * normed_two, 0, keepdims=True)
     sums[3] = jnp.sum(grad_y, 0, keepdims=True)
@@ -768,119 +872,303 @@
     gm_t = grad_two.T.astype(bf16)
     hidden_t = hidden.T.astype(bf16)
 
+    there = lo.at[1 - c, part]
+    remote(there, there, r["s_sem"].at[0], r["s_sem"].at[1], me.ydev).wait_recv()
+    own_lo.wait()
+    lo_line.start()
+
     def down_step(tt, total):
-        ga = dot_nn(gm, u_ref[tt, :, 768:1536])
-        gu = (ga * slope[tt]).astype(bf16)
-        g_ref[tt, :, 768:1536] = dot_nn(gm_t, act[tt]).astype(bf16)
-        g_ref[tt, :, 0:768] = dot_nn(hidden_t, gu).astype(bf16)
-        return total + dot_nt(gu, u_ref[tt, :, 0:768])
+        ga = dot_nn(gm, u_v[tt, :, 768:1536])
+        gu = (ga * slope[tt].astype(f32)).astype(bf16)
+        g_v[tt, :, 768:1536] = dot_nn(gm_t, act[tt]).astype(bf16)
+        g_v[tt, :, 0:768] = dot_nn(hidden_t, gu).astype(bf16)
+        return total + dot_nt(gu, u_v[tt, :, 0:768])
 
     grad_hidden = lax.fori_loop(0, 4, down_step, grad_two)
     sums[0] = jnp.sum(grad_hidden * normed_one, 0, keepdims=True)
     sums[1] = jnp.sum(grad_hidden, 0, keepdims=True)
     grad_one = back(grad_hidden, normed_one, inverse_one, gains[0])
-    gone_ref[...] = grad_one.reshape(2, 128, depth)
+    r["gone"][...] = grad_one.reshape(2, 128, depth)
     ga = grad_one.astype(bf16)
+    gatt, do_in = r["gatt"], r["do_in"]
+    for tt in range(4):
+        back_t = dot_nn(ga, u_v[tt, :, 1536:1728]).astype(bf16)
+        gatt[tt] = back_t.reshape(2, 128, width)
+    for d in (1, 2, 3):
+        to = (t + d) % 4
+        go(remote(gatt.at[to], do_in.at[t], r["a_send"].at[d], r["a_recv"].at[d], me.z(to)))
+    do_in[t] = gatt[t]
+    for i, dev in enumerate((me.core, me.xdev, me.ydev)):
+        pl.semaphore_signal(r["free"].at[i], inc=1, device_id=dev, device_id_type=MESH)
     ga_t = grad_one.T.astype(bf16)
     norm_rows = jnp.concatenate(sums + [jnp.zeros((4, depth), f32)], 0)
     norm_cols = jnp.concatenate([norm_rows.T, jnp.zeros((depth, UW - 1736), f32)], 1).astype(bf16)
     for tt in range(4):
-        back_t = dot_nn(ga, u_ref[tt, :, 1536:1728]).astype(bf16)
-        gatt_ref[tt] = back_t.reshape(2, 128, back_t.shape[1])
-        g_ref[tt, :, 1536:1728] = dot_nn(ga_t, att[tt]).astype(bf16)
-        g_ref[tt, :, 1728:1792] = norm_cols
-
-
-def layer(lengths, count, att, u, tok, teach, live):
-    depth = tok.shape[2]
-    vm = pl.BlockSpec(memory_space=pltpu.VMEM)
-    smem = pl.BlockSpec(memory_space=pltpu.SMEM)
-    return pl.pallas_call(
-        layer_kernel,
-        name="layer",
-        out_shape=[
-            jax.ShapeDtypeStruct((2, 128, depth), bf16),
-            jax.ShapeDtypeStruct((1, 1), f32),
-            jax.ShapeDtypeStruct((4, depth, UW), bf16),
-            jax.ShapeDtypeStruct(att.shape, bf16),
-            jax.ShapeDtypeStruct((2, 128, depth), f32),
-        ],
-        in_specs=[smem, smem, vm, vm, vm, vm, vm],
-        out_specs=[vm, smem, vm, vm, vm],
-        scratch_shapes=[
-            pltpu.VMEM((4, 256, 768), bf16),
-            pltpu.VMEM((4, 256, 768), f32),
-        ],
-        compiler_params=pltpu.CompilerParams(vmem_limit_bytes=VMEM_LIMIT),
-    )(lengths, count, att, u, tok, teach, live)
-
-
-def attention_back_kernel(
-    do_ref, q_ref, k_ref, v_ref, kt_ref, pt_ref, t_ref, w_ref, part_ref, grad_ref, do, dqt, dk, dv, proj
-):
-    heads, seq = q_ref.shape[0], q_ref.shape[1]
-    width = heads * HD
+        g_v[tt, :, 1536:1728] = dot_nn(ga_t, att[tt]).astype(bf16)
+        g_v[tt, :, 1728:1792] = norm_cols
+
+    far = 1 - x
+    for i in range(3):
+        pl.semaphore_wait(r["free"].at[i], 1)
+
+    def g_rows(tt, ff):
+        return g_v.at[tt, pl.ds(pl.multiple_of(ff * rows_f, rows_f), rows_f), :]
+
+    def rc_all(xx, tt):
+        return u_v.at[tt, pl.ds(pl.multiple_of(xx * rows_f, rows_f), rows_f), :]
+
+    def room(n):
+        return lambda tt, i=0, size=hrows: u_v.at[tt, pl.ds((4 + n) * hrows + i * qrows, size), :]
+
+    xg_at, yg_at, zl_at, zr_at = (room(n) for n in range(4))
+
+    for xx in (far, x):
+        for tt in range(4):
+            ff = xx * 2 + (1 - k)
+            go(remote(g_rows(tt, ff), rc_all(xx, tt), r["rc_send"].at[xx, tt], r["rc_recv"].at[xx, tt], me.core))
+
+    lo_line.step(1)
+
+    def rc_rows(xx, tt, h, q0, n):
+        return u_v.at[tt, pl.ds(pl.multiple_of(xx * rows_f + h * hrows + q0, qrows), n), :]
+
+    def core_step(xx, tt):
+        view = rc_all(xx, tt)
+        remote(view, view, r["rc_send"].at[xx, tt], r["rc_recv"].at[xx, tt], me.core).wait_recv()
+        add_rows(view, view, g_rows(tt, xx * 2 + k))
+
+    def far_step(tt):
+        core_step(far, tt)
+        dx, dy = r["dx"], r["dy"]
+        go(remote(rc_rows(far, tt, 1 - c, 0, qrows), dx.at[tt], r["dx_send"].at[tt], r["dx_recv"].at[tt], me.xdev))
+        go(remote(rc_rows(far, tt, 1 - c, qrows, qrows), dy.at[tt], r["dy_send"].at[tt], r["dy_recv"].at[tt], me.ydev))
+        go(remote(rc_rows(far, tt, c, 0, qrows), xg_at(tt, 0, qrows), r["xg_send"].at[tt, 0], r["xg_recv"].at[tt, 0], me.xdev))
+
+    def near_step(tt):
+        core_step(x, tt)
+        go(remote(rc_rows(x, tt, 1 - c, qrows, qrows), yg_at(tt, 1, qrows), r["yg_send"].at[tt, 1], r["yg_recv"].at[tt, 1], me.ydev))
+
+    def diag_step(tt):
+        dx, dy = r["dx"], r["dy"]
+        remote(dx.at[tt], dx.at[tt], r["dx_send"].at[tt], r["dx_recv"].at[tt], me.xdev).wait_recv()
+        mine = rc_rows(x, tt, 1 - c, 0, qrows)
+        add_rows(mine, mine, dx.at[tt])
+        go(remote(mine, yg_at(tt, 0, qrows), r["yg_send"].at[tt, 0], r["yg_recv"].at[tt, 0], me.ydev))
+        remote(dy.at[tt], dy.at[tt], r["dy_send"].at[tt], r["dy_recv"].at[tt], me.ydev).wait_recv()
+        mine = rc_rows(far, tt, c, qrows, qrows)
+        add_rows(mine, mine, dy.at[tt])
+        go(remote(mine, xg_at(tt, 1, qrows), r["xg_send"].at[tt, 1], r["xg_recv"].at[tt, 1], me.xdev))
+
+    def sum_step(tt):
+        for i in (0, 1):
+            xg, yg = xg_at(tt, i, qrows), yg_at(tt, i, qrows)
+            mine = rc_rows(x, tt, c, i * qrows, qrows)
+            remote(xg, xg, r["xg_send"].at[tt, i], r["xg_recv"].at[tt, i], me.xdev).wait_recv()
+            add_rows(mine, mine, xg)
+            remote(yg, yg, r["yg_send"].at[tt, i], r["yg_recv"].at[tt, i], me.ydev).wait_recv()
+            add_rows(mine, mine, yg)
+
+    ORDER = (3, 0, 2, 1)
+    w_chain = Chain(
+        me, go, lambda tt: rc_rows(x, tt, c, 0, hrows), zl_at, zr_at,
+        r["zw_send"], r["zw_recv_l"], r["zw_recv_r"],
+    )
+
+    for tt in ORDER:
+        far_step(tt)
+    lo_line.step(2)
+
+    for name in ("pt", "q", "k", "v", "kt", "w", "t"):
+        loads[name].wait()
+    do, proj, dqt, dk, dv = r["do"], r["proj"], r["dqt"], r["dk"], r["dv"]
+    for d in (1, 2, 3):
+        src = (t + 4 - d) % 4
+        remote(do_in.at[src], do_in.at[src], r["a_send"].at[d], r["a_recv"].at[d], me.z(src)).wait_recv()
+    for s in range(2):
+        for tt in range(4):
+            at = s * half + tt * 128
+            for h in range(heads):
+                do[h, at : at + 128, :] = do_in[tt, s, :, h * HD : (h + 1) * HD]
+    q_v, k_v, v_v, kt_v, pt_v, t_v, w_v = (r[n + "_v"] for n in ("q", "k", "v", "kt", "pt", "t", "w"))
     scale = HD ** (-0.5)
     wide = 256
-    for h in range(heads):
-        do[h] = do_ref[:, h * HD : (h + 1) * HD]
-    for h in range(heads):
+
+    def attend_back(h):
         dk[...] = jnp.zeros_like(dk)
         dv[...] = jnp.zeros_like(dv)
 
         def step(i, carry):
             cols = pl.ds(pl.multiple_of(i * wide, wide), wide)
             mine = do[h, cols, :]
-            probs = pt_ref[h, :, cols]
-            gp = dot_nt(v_ref[h], mine)
+            probs = pt_v[h, :, cols]
+            gp = dot_nt(v_v[h], mine)
             pf = probs.astype(f32)
             mix = jnp.sum(pf * gp, 0, keepdims=True)
             gs = (pf * (gp - mix)).astype(bf16)
-            dk[...] += dot_nn(gs, q_ref[h, cols, :])
+            dk[...] += dot_nn(gs, q_v[h, cols, :])
             dv[...] += dot_nn(probs, mine)
-            dqt[h * HD : (h + 1) * HD, cols] = dot_nn(kt_ref[h * HD : (h + 1) * HD, :], gs)
+            dqt[h * HD : (h + 1) * HD, cols] = dot_nn(kt_v[h * HD : (h + 1) * HD, :], gs)
             return carry
 
         lax.fori_loop(0, seq // wide, step, 0)
         proj[1, :, h * HD : (h + 1) * HD] = (dk[...] * scale).astype(bf16)
         proj[2, :, h * HD : (h + 1) * HD] = dv[...].astype(bf16)
+
+    attend_back(0)
+    for tt in ORDER:
+        near_step(tt)
+    attend_back(1)
+    for tt in ORDER:
+        diag_step(tt)
+    lo_line.step(3)
+    attend_back(2)
     proj[0] = (dqt[...].T * scale).astype(bf16)
+    ip = r["ip"]
 
     def rows_step(i, carry):
-        rows = pl.ds(pl.multiple_of(i * 256, 256), 256)
-        total = dot_nt(proj[0, rows, :], w_ref[0])
+        at = pl.ds(pl.multiple_of(i * 128, 128), 128)
+        total = dot_nt(proj[0, at, :], w_v[0])
         for j in (1, 2):
-            total += dot_nt(proj[j, rows, :], w_ref[j])
-        part_ref[rows, :] = total.astype(bf16)
+            total += dot_nt(proj[j, at, :], w_v[j])
+        ip[i // 4, i % 4] = total.astype(bf16)
         return carry
 
-    lax.fori_loop(0, seq // 256, rows_step, 0)
+    lax.fori_loop(0, seq // 128, rows_step, 0)
+
+    def ip_chain(j, s):
+        return Chain(
+            me, go, lambda tt: ip.at[s, tt], lambda tt: act.at[tt, pl.ds(j * 128, 128), :], lambda tt: slope.at[tt, pl.ds(j * 128, 128), :],
+            r["i_send"].at[j], r["i_recv_l"].at[j], r["i_recv_r"].at[j],
+        )
+
+    chains = [ip_chain(0, 1 - c), ip_chain(1, c)]
+    for tt, way in CHAIN_ORDER[:2]:
+        chains[0].pass_on(tt, way)
+    qg = r["qg"]
     for j in range(3):
-        grad_ref[j] = dot_tn(t_ref[...], proj[j]).astype(bf16)
-
-
-def attention_back(do, q, k, v, kt, pt, tokens, w):
+        qg[j] = dot_tn(t_v[...], proj[j]).astype(bf16)
+
+    def q_rows(ff):
+        return qg.at[:, pl.ds(pl.multiple_of(ff * rows_f, rows_f), rows_f), :]
+
+    qc, qs = r["qc"], r["q_sem"]
+    go(remote(q_rows(far * 2 + 1 - k), qc.at[0], qs.at[0], qs.at[1], me.core))
+    go(remote(q_rows(x * 2 + 1 - k), qc.at[1], qs.at[2], qs.at[3], me.core))
+    for tt, way in CHAIN_ORDER[2:]:
+        chains[0].pass_on(tt, way)
+    remote(qc.at[0], qc.at[0], qs.at[0], qs.at[1], me.core).wait_recv()
+    qc[0] = qc[0] + qg[:, pl.ds(pl.multiple_of((far * 2 + k) * rows_f, rows_f), rows_f), :]
+    go(remote(qc.at[0], qc.at[2], qs.at[4], qs.at[5], me.xdev))
+    for tt, way in CHAIN_ORDER:
+        chains[1].pass_on(tt, way)
+    remote(qc.at[1], qc.at[1], qs.at[2], qs.at[3], me.core).wait_recv()
+    qc[1] = qc[1] + qg[:, pl.ds(pl.multiple_of((x * 2 + k) * rows_f, rows_f), rows_f), :]
+    for tt in ORDER:
+        sum_step(tt)
+    remote(qc.at[2], qc.at[2], qs.at[4], qs.at[5], me.xdev).wait_recv()
+    qc[1] = qc[1] + qc[2]
+    go(remote(qc.at[1], qc.at[3], qs.at[6], qs.at[7], me.ydev))
+
+    ig = r["ig"]
+    igp = r["igp"]
+
+    def finish(j, s):
+        chains[j].end()
+        igp[j] = (ip[s, t].astype(f32) + r["gone"][s]).astype(bf16)
+
+    finish(0, 1 - c)
+    go(remote(igp.at[0], ig.at[c, part], r["s_sem"].at[2], r["s_sem"].at[3], me.ydev))
+    finish(1, c)
+    own_ig = pltpu.make_async_copy(igp.at[1], ig.at[c, part], r["load_sem"].at[13])
+    own_ig.start()
+
+    def ig_line(j, s):
+        def block(tt):
+            return ig.at[s, pl.ds(pl.multiple_of(tt * 128, 128), 128), :]
+
+        return Line(me, go, block, r["ig_send"].at[j], r["ig_recv"].at[j])
+
+    lines = [ig_line(0, c), ig_line(1, 1 - c)]
+    own_ig.wait()
+    lines[0].start()
+    there = ig.at[1 - c, part]
+    remote(there, there, r["s_sem"].at[2], r["s_sem"].at[3], me.ydev).wait_recv()
+    lines[1].start()
+    for tt, way in CHAIN_ORDER[:2]:
+        w_chain.pass_on(tt, way)
+    lines[0].step(1)
+    lines[1].step(1)
+    for tt, way in CHAIN_ORDER[2:]:
+        w_chain.pass_on(tt, way)
+    lines[0].step(2)
+    lines[1].step(2)
+    w_chain.end()
+    fin = r["fin"]
+    fin[c] = rc_rows(x, t, c, 0, hrows)[...]
+    go(remote(fin.at[c], fin.at[c], r["s_sem"].at[4], r["s_sem"].at[5], me.ydev))
+    lines[0].step(3)
+    lines[1].step(3)
+    remote(qc.at[3], qc.at[3], qs.at[6], qs.at[7], me.ydev).wait_recv()
+    r["qsum"][...] = qc[1].astype(f32) + qc[3].astype(f32)
+    remote(fin.at[1 - c], fin.at[1 - c], r["s_sem"].at[4], r["s_sem"].at[5], me.ydev).wait_recv()
+    r["gsum"][...] = fin[...].reshape(rows_f, UW).astype(f32)
+    for copy, pred in sends:
+        when(pred, copy.wait_send)
+
+
+def backward(lengths, count, att, u, tok, teach, live, q, k, v, kt, pt, tokens, w):
+    depth = tok.shape[2]
     heads, seq = q.shape[:2]
     width = heads * HD
+    rows_f = depth // 4
     vm = pl.BlockSpec(memory_space=pltpu.VMEM)
+    smem = pl.BlockSpec(memory_space=pltpu.SMEM)
+    hbm = pl.BlockSpec(memory_space=pl.ANY)
+    dma = pltpu.SemaphoreType.DMA
+
+    def vb(*shape):
+        return pltpu.VMEM(shape, bf16)
+
+    def vf(*shape):
+        return pltpu.VMEM(shape, f32)
+
+    ins = dict(
+        lengths=(lengths, smem), count=(count, smem), att=(att, hbm), u=(u, hbm), tok=(tok, vm), teach=(teach, vm),
+        live=(live, vm), q=(q, hbm), k=(k, hbm), v=(v, hbm), kt=(kt, hbm), pt=(pt, hbm), t=(tokens, hbm), w=(w, hbm),
+    )
+    outs = dict(
+        lo=((2, seq // 2, depth), bf16, hbm),
+        ig=((2, seq // 2, depth), bf16, hbm),
+        gsum=((rows_f, UW), f32, vm),
+        qsum=((3, rows_f, width), f32, vm),
+        err=((1, 1), f32, smem),
+    )
+    h, qr = rows_f // 2, rows_f // 4
+    scratch = dict(
+        att_v=vb(*att.shape), u_v=vb(*u.shape), pt_v=vb(*pt.shape), q_v=vb(*q.shape), k_v=vb(*k.shape), v_v=vb(*v.shape),
+        kt_v=vb(*kt.shape), w_v=vb(*w.shape), t_v=vb(*tokens.shape), g_v=vb(*u.shape), act=vb(4, 256, 768),
+        slope=vb(4, 256, 768), piece=vb(2, 128, depth), gone=vf(2, 128, depth), gatt=vb(*att.shape), do_in=vb(*att.shape),
+        dx=vb(4, qr, UW), dy=vb(4, qr, UW),
+        do=vb(heads, seq, HD), proj=vb(3, seq, width), dqt=vf(width, seq),
+        dk=vf(seq, HD), dv=vf(seq, HD), ip=vb(2, 4, 128, depth),
+        igp=vb(2, 128, depth), qg=vb(3, depth, width), qc=vb(4, 3, rows_f, width), fin=vb(2, h, UW),
+        load_sem=dma((14,)), s_sem=dma((6,)), lo_send=dma((2, 4)), lo_recv=dma((4,)), a_send=dma((4,)), a_recv=dma((4,)),
+        rc_send=dma((2, 4)), rc_recv=dma((2, 4)), dx_send=dma((4,)), dx_recv=dma((4,)), dy_send=dma((4,)),
+        dy_recv=dma((4,)), xg_send=dma((4, 2)), xg_recv=dma((4, 2)), yg_send=dma((4, 2)), yg_recv=dma((4, 2)),
+        zw_send=dma((4,)), zw_recv_l=dma((4,)), zw_recv_r=dma((4,)), i_send=dma((2, 4)), i_recv_l=dma((2, 4)),
+        i_recv_r=dma((2, 4)), ig_send=dma((2, 2, 4)), ig_recv=dma((2, 4)), q_sem=dma((8,)), free=pltpu.SemaphoreType.REGULAR((3,)),
+    )
     return pl.pallas_call(
-        attention_back_kernel,
-        name="attention_back",
-        out_shape=[
-            jax.ShapeDtypeStruct(tokens.shape, bf16),
-            jax.ShapeDtypeStruct(w.shape, bf16),
-        ],
-        in_specs=[vm] * 8,
-        out_specs=[vm] * 2,
-        scratch_shapes=[
-            pltpu.VMEM((heads, seq, HD), bf16),
-            pltpu.VMEM((width, seq), f32),
-            pltpu.VMEM((seq, HD), f32),
-            pltpu.VMEM((seq, HD), f32),
-            pltpu.VMEM((3, seq, width), bf16),
-        ],
-        compiler_params=pltpu.CompilerParams(vmem_limit_bytes=VMEM_LIMIT),
-    )(do, q, k, v, kt, pt, tokens, w)
+        functools.partial(backward_kernel, (*ins, *outs, *scratch)),
+        name="backward",
+        out_shape=[jax.ShapeDtypeStruct(s, d) for s, d, _ in outs.values()],
+        in_specs=[m for _, m in ins.values()],
+        out_specs=[m for _, _, m in outs.values()],
+        scratch_shapes=list(scratch.values()),
+        compiler_params=pltpu.CompilerParams(
+            collective_id=1, has_side_effects=True, vmem_limit_bytes=60 * 2**20
+        ),
+    )(*(a for a, _ in ins.values()))
 
 
 def body_swapped(
@@ -930,25 +1218,12 @@
     att, u, tk, w, q, k, v, kt, pt, tok, teach, live = forward_attention(
         lengths, tokens, teacher, qkvb, upack, rbt, mask, seq
     )
-    out_part, err, g, gatt, gone = layer(lengths, live_count.reshape(1, 1), att, u, tok, teach, live)
-    do = lax.all_to_all(gatt, "tp", 0, 0)
-    do = jnp.swapaxes(do, 0, 1).reshape(seq, att.shape[3])
-    part, qkv_part = attention_back(do, q, k, v, kt, pt, tk, w)
+    layer_out, ig, g, qkv_grad, err = backward(
+        lengths, live_count.reshape(1, 1), att, u, tok, teach, live, q, k, v, kt, pt, tk, w
+    )
     error_total = lax.psum(err[0, 0], ("fsdp", "ctx", "tp"))
     loss_value = error_total / (live_count * width)
-
-    def spread(piece):
-        swapped = lax.all_to_all(piece, "ctx", 0, 0)
-        return lax.all_gather(swapped, "tp", axis=1, tiled=True)
-
-    layer_out = spread(out_part)
-    summed = lax.psum_scatter(part.reshape(2, 4, 128, width), "tp", scatter_dimension=1, tiled=False)
-    input_grad = spread((summed.astype(f32) + gone).astype(bf16)).astype(f32)
-    g = lax.psum_scatter(g, "tp", scatter_dimension=0, tiled=False)
-    g = lax.psum_scatter(g, "fsdp", scatter_dimension=0, tiled=True)
-    g = lax.psum(g, "ctx").astype(f32)
-    qkv_grad = lax.psum_scatter(qkv_part, "fsdp", scatter_dimension=1, tiled=True)
-    qkv_grad = lax.psum(qkv_grad, "ctx").astype(f32)
+    input_grad = ig.astype(f32)
     up_grad, down_grad, out_grad, norm_grad = g[:, :768], g[:, 768:1536].T, g[:, 1536:1728].T, g[:, 1728:1732].T
     shards = (qkv_grad, out_grad, up_grad, down_grad, norm_grad)
     squares = sum(jnp.sum(m * m) for m in shards[:4]) + jnp.where(t == 0, jnp.sum(norm_grad * norm_grad), 0.0)

time: 626 us -> 383 us (0.61)
  waiting for transfers between devices: 288 us -> 0 us
  Pallas kernels: 134 us -> 253 us
  blocking collectives: 135 us -> 85.4 us
  between operations: 22.8 us -> 9.32 us
  local copies, waits for them, and re-layouts: 23.2 us -> 13.9 us
    reduce_scatter x4 -> x0, waiting for transfers between devices: 233 us -> none  [the longest x1 140 us: body_swapped(): g = lax.psum_scatter(g, 'tp', scatter_dimension=0, tiled=False)]
    pallas_call x2 -> x1, Pallas kernels: 46.4 us -> 165 us  [backward(): pl.pallas_call(functools.partial(backward_kernel, (*ins, *outs, *scratch)...]
    all_to_all x3 -> x0, blocking collectives: 47.3 us -> none  [the longest x1 27.5 us: body_swapped(): do = lax.all_to_all(gatt, 'tp', 0, 0)]
    all_gather x2 -> x0, waiting for transfers between devices: 31.5 us -> none  [spread(): return lax.all_gather(swapped, 'tp', axis=1, tiled=True)]
    psum x1 -> x0, waiting for transfers between devices: 23.4 us -> none  [body_swapped(): qkv_grad = lax.psum(qkv_grad, 'ctx').astype(f32)]
    unnamed x53 -> x47, local copies, waits for them, and re-layouts: 15 us -> 10.2 us
  transfers between devices with their start and end apart: 7 -> 0, of which waited for: 6 -> 0; matrix products, arithmetic and copies ran while one was open for 2% -> 0% of each run, Pallas kernels for 4% -> 0%
where the time goes in v2:
time: 383 us; the launch traced here: 382 us
  Pallas kernels  253 us (66%)
  blocking collectives  85.4 us (22%)
  other arithmetic  20.6 us (5%)
  local copies, waits for them, and re-layouts  13.9 us (4%)
  between operations  9.32 us (2%)
    pallas_call x1, Pallas kernels, backward(): pl.pallas_call(functools.partial(backward_kernel, (*ins, *outs, *scratch)...  165 us
    pallas_call x1, Pallas kernels, forward_attention(): pl.pallas_call(forward_attention_kernel, name='forward_attention', out_sh...  88 us
    psum x1, blocking collectives, body_swapped(): error_total = lax.psum(err[0, 0], ('fsdp', 'ctx', 'tp'))  40.1 us
    psum x1, blocking collectives, body_swapped(): grad_norm = jnp.sqrt(lax.psum(squares, ('fsdp', 'tp')))  30.2 us
    psum x1, blocking collectives, body_swapped(): live_count = lax.psum(jnp.sum(live_rows), ('fsdp', 'ctx'))  15.1 us
    unnamed x47, local copies, waits for them, and re-layouts  10.2 us
    sub x5, other arithmetic, adam_update(): weight - rate * (corrected / (jnp.sqrt(scaled) + adam_eps) + decay_rate *...  9.02 us

profile of v2, /device:TPU:0, one launch (start us, length us, event | category | flops | bytes accessed | tf_op | source)
XLA Modules:
  0.0 381.9 jit_solution(16831686280225124693)
XLA Ops:
  0.7 1.1 copy.62
  1.8 1.2 convert.17
  3.2 1.0 concatenate.4.upack_ref
  4.3 0.7 convert_element_type.34.qkvb_ref
  5.0 0.6 broadcast_in_dim.5.mask_ref
  6.3 88.0 %forward_attention.1 = (bf16[4,2,128,192]{3,2,1,0:T(8,128)(2,1)}, bf16[4,768,1792]{2,1,0:T(8,128)(2,1)}, bf16[1024,768]{1,0:T(8,128)(2,1)}, bf16[3,768,192]{2,1,...) custom-call(s32[2]{0:T(128)} %refs_0_.1, ...), custom_call_target="tpu_custom_call" | custom-call | tf_op jit(solution)/shard_map/forward_attention/pallas_call | solution.py:655
  94.3 0.7 fusion.9
  95.0 15.1 %psum.21 = f32[]{:T(128)} all-reduce(f32[]{:T(128)} %fusion.9), channel_id=1, replica_groups=mesh['fsdp'=4,'ctx'=2,'tp'=4] {'fsdp','ctx'}, use_global_device_ids=true, to_apply=%region_1.2 | all-reduce | flops 1 | bytes 8 | tf_op jit(solution)/shard_map/psum | solution.py:1217
  110.1 164.5 %backward.1 = (bf16[2,512,768]{2,1,0:T(8,128)(2,1)}, bf16[2,512,768]{2,1,0:T(8,128)(2,1)}, f32[192,1792]{1,0:T(8,128)}, f32[3,192,192]{2,1,0:T(8,128)}, f32[1,1]{1,0:T(1,128)}) custom-call(s32[2]{0:T(128)} %refs_0_.1, f32[1,1]{1,0:T(1,128)} %bitcast.refs_1_, bf16[4,2,128,192]{3,2,1,0:T(8,128)(2,1)} %get-tuple-element.36.refs_2_, ...), custom_call_target="tpu_custom_call" | custom-call | tf_op jit(solution)/shard_map/backward/pallas_call | solution.py:1161
  274.7 1.9 multiply_reduce_fusion.2
  276.6 1.6 multiply_reduce_fusion.3
  279.6 2.0 multiply_reduce_fusion
  282.9 0.7 multiply_reduce_fusion.4
  284.2 30.2 %psum.23 = f32[]{:T(128)} all-reduce(f32[]{:T(128)S(6)} %add.113), channel_id=1, replica_groups=mesh['fsdp'=4,'ctx'=2,'tp'=4] {'fsdp','tp'}, use_global_device_ids=true, to_apply=%region_8.9 | all-reduce | flops 1 | bytes 8 | tf_op jit(solution)/shard_map/psum | solution.py:1230
  316.2 0.8 multiply_divide_fusion
  317.0 1.0 copy.72
  318.1 0.8 copy.73
  318.9 0.9 sub.43
  319.8 0.7 copy.78
  320.5 1.6 copy.79
  322.0 1.6 copy.80
  323.6 2.7 multiply_subtract_fusion
  326.3 1.5 multiply_subtract_fusion.1
  328.0 0.8 copy.66
  328.8 1.1 multiply_subtract_fusion.3
  329.8 0.8 copy.75
  330.6 0.8 copy.76
  331.4 0.8 copy.77
  332.2 2.8 multiply_subtract_fusion.2
  335.1 1.9 convert_element_type.39
  337.0 40.1 %psum.22 = f32[]{:T(128)} all-reduce(f32[]{:T(128)} %bitcast.5), channel_id=1, replica_groups=mesh['fsdp'=4,'ctx'=2,'tp'=4] {'fsdp','ctx','tp'}, use_global_device_ids=true, to_apply=%region_2.3 | all-reduce | flops 1 | bytes 8 | tf_op jit(solution)/shard_map/psum | solution.py:1224
  378.4 1.1 copy.86
  (53 shorter events, 1.4 us)
Async XLA Ops:
  0.7 2.3 copy-start.1
  0.7 2.4 copy-start.12
  1.8 2.5 copy-start.3
  3.0 2.0 copy-start.13
  3.0 2.7 copy-start.17
  6.3 88.0 %copy-start.14 = (s32[2]{0:T(128)S(1)}, s32[2]{0:T(128)}, u32[]{:S(2)}) copy-start(s32[2]{0:T(128)} %refs_0_.1) | copy-start | bytes 28
  274.7 8.2 %copy-start = (f32[192,1792]{1,0:T(8,128)S(1)}, f32[192,1792]{1,0:T(8,128)}, u32[]{:S(2)}) copy-start(f32[192,1792]{1,0:T(8,128)} %get-tuple-element.52) | copy-start | bytes 4128772
  274.7 41.2 %copy-start.15 = (f32[4,192]{1,0:T(4,128)S(1)}, f32[4,192]{1,0:T(4,128)}, u32[]{:S(2)}) copy-start(f32[4,192]{1,0:T(4,128)} %param.40) | copy-start | bytes 9220
  274.7 41.4 %copy-start.16 = (f32[4,192]{1,0:T(4,128)S(1)}, f32[4,192]{1,0:T(4,128)}, u32[]{:S(2)}) copy-start(f32[4,192]{1,0:T(4,128)} %param.41) | copy-start | bytes 9220
  278.2 45.4 %copy-start.7 = (f32[768,192]{0,1:T(8,128)S(1)}, f32[768,192]{0,1:T(8,128)}, u32[]{:S(2)}) copy-start(f32[768,192]{0,1:T(8,128)} %param.39) | copy-start | bytes 1769476
  323.6 2.7 copy-start.2
  323.6 2.7 copy-start.8
  323.6 2.7 copy-start.9
  326.3 1.5 copy-start.10
  326.3 1.6 copy-start.11
  327.9 4.3 %copy-start.4 = (f32[3,192,192]{2,1,0:T(8,128)S(1)}, f32[3,192,192]{2,1,0:T(8,128)}, u32[]{:S(2)}) copy-start(f32[3,192,192]{2,1,0:T(8,128)} %get-tuple-element.51) | copy-start | bytes 1327108
  332.2 2.9 copy-start.6
  335.1 43.4 %copy-start.5 = (bf16[2,512,768]{2,1,0:T(8,128)(2,1)S(1)}, bf16[2,512,768]{2,1,0:T(8,128)(2,1)}, u32[]{:S(2)}) copy-start(bf16[2,512,768]{2,1,0:T(8,128)(2,1)} %get-tuple-element.127) | copy-start | bytes 4718596

commit v3 on v2

--- a/solution.py
+++ b/solution.py
@@ -1,4 +1,5 @@
 import functools
+import types
 from functools import partial
 
 import jax
@@ -373,21 +374,35 @@
     def z(self, t):
         return (self.f, self.c, t)
 
-    def barrier(self):
+    def flipped(self, d):
+        x, k = self.f // 2, self.f % 2
+        x = 1 - x if d // 4 else x
+        k = 1 - k if d % 2 else k
+        return x * 2 + k, 1 - self.c if d // 2 % 2 else self.c
+
+    def owners(self):
+        return [(d, (*self.flipped(d), self.t)) for d in range(1, 8)]
+
+    def barrier(self, whole=False):
         sem = pltpu.get_barrier_semaphore()
-        for dev in (self.core, self.xdev, self.ydev, *(self.z((self.t + d) % 4) for d in (1, 2, 3))):
+        devs = [dev for _, dev in self.owners()] if whole else [self.core, self.xdev, self.ydev]
+        devs += [self.z((self.t + d) % 4) for d in (1, 2, 3)]
+        for dev in devs:
             pl.semaphore_signal(sem, inc=1, device_id=dev, device_id_type=MESH)
-        pl.semaphore_wait(sem, 6)
+        pl.semaphore_wait(sem, len(devs))
 
 
 def forward_attention_kernel(
     lengths_ref,
     tokens_ref,
     teacher_ref,
-    qkvb_ref,
-    upack_ref,
-    rbt_ref,
-    mask_ref,
+    qkv_ref,
+    up_ref,
+    down_ref,
+    out_ref,
+    norm_ref,
+    blocks_ref,
+    valid_ref,
     att_ref,
     u_ref,
     t_ref,
@@ -400,6 +415,12 @@
     tok_ref,
     teach_ref,
     live_ref,
+    count_ref,
+    upack_ref,
+    qkvb_ref,
+    rbt_ref,
+    mask_ref,
+    tally,
     vt,
     bias,
     rb,
@@ -420,14 +441,31 @@
     h_recv,
     a_send,
     a_recv,
+    n_sem,
 ):
     me = Peers()
     f, c, t = me.f, me.c, me.t
     seq = t_ref.shape[0]
     half = seq // 2
     rows_f = qkvb_ref.shape[1]
+    sends = []
+    qkvb_ref[...] = qkv_ref[...].astype(bf16)
+    upack_ref[:, 0:768] = up_ref[...].astype(bf16)
+    upack_ref[:, 768:1536] = down_ref[...].astype(bf16)
+    tail = jnp.concatenate(
+        [out_ref[...].T, jnp.concatenate([norm_ref[...], jnp.zeros((60, rows_f), f32)], 0).T], 1
+    )
+    upack_ref[:, 1536:1792] = tail.astype(bf16)
+    for s in range(2):
+        rbt_ref[s] = jnp.zeros((8, 128), f32)
+        rbt_ref[s, 0:3, 0 : blocks_ref.shape[2]] = blocks_ref[:, s, :].astype(f32)
+        mask_ref[s] = jnp.broadcast_to(valid_ref[s : s + 1, :].astype(f32), (8, half))
+    spot = c * half + lax.broadcasted_iota(jnp.int32, (1, half), 1)
+    found = jnp.zeros((1, half), f32)
+    for s in range(2):
+        found += jnp.where((valid_ref[s : s + 1, :] == 1) & (spot < lengths_ref[s]), 1.0, 0.0)
+    count_ref[...] = jnp.broadcast_to(jnp.sum(found, 1, keepdims=True), (8, 128))
     me.barrier()
-    sends = []
 
     def go(copy, pred=None):
         if pred is None:
@@ -435,11 +473,10 @@
         else:
             pl.when(pred)(copy.start)
         sends.append((copy, pred))
-
     own_rows = pl.ds(pl.multiple_of(c * half, half), half)
     go(remote(tokens_ref.at[1 - c], t_ref.at[own_rows], y_sem.at[0], y_sem.at[1], me.ydev))
     go(remote(rbt_ref.at[1 - c], rb.at[c], y_sem.at[2], y_sem.at[3], me.ydev))
-    go(remote(mask_ref.at[1 - c, t], live_ref.at[c], y_sem.at[4], y_sem.at[5], me.ydev))
+    go(remote(mask_ref.at[1 - c], live_ref.at[c], y_sem.at[4], y_sem.at[5], me.ydev))
     part = pl.ds(pl.multiple_of(t * 128, 128), 128)
     go(remote(teacher_ref.at[1 - c, part], teach_ref.at[c], y_sem.at[6], y_sem.at[7], me.ydev))
 
@@ -476,7 +513,18 @@
     for copy in local:
         copy.start()
     rb[c] = rbt_ref[c]
-    live_ref[c] = mask_ref[c, t]
+    live_ref[c] = mask_ref[c]
+
+    peers = (me.core, me.xdev, me.ydev)
+
+    def tally_send(i):
+        go(remote(count_ref if i == 0 else tally.at[i + 2], tally.at[i], n_sem.at[0, i], n_sem.at[1, i], peers[i]))
+
+    def tally_take(i):
+        remote(tally.at[i], tally.at[i], n_sem.at[0, i], n_sem.at[1, i], peers[i]).wait_recv()
+        tally[3 + i] = (count_ref[...] if i == 0 else tally[i + 2]) + tally[i]
+
+    tally_send(0)
 
     def z_step(d):
         for tt, ok, on, nxt, way in ((t - d, t - d >= 0, t < 3, t + 1, 0), (t + d, t + d <= 3, t > 0, t - 1, 1)):
@@ -511,7 +559,6 @@
             piece = slab(tt, me.f_x, 1 - c)
             when(ok, remote(piece, piece, yw_send.at[tt], yw_recv.at[tt], me.ydev).wait_recv)
             go(remote(piece, piece, h_send.at[tt, 1], h_recv.at[tt, 1], me.core), ok)
-
     remote(wblock(me.f_x), wblock(me.f_x), w_sem.at[0], w_sem.at[1], me.xdev).wait_recv()
     go(remote(wblock(me.f_x), wblock(me.f_x), w_sem.at[4], w_sem.at[5], me.core))
     remote(wblock(me.f_core), wblock(me.f_core), w_sem.at[2], w_sem.at[3], me.core).wait_recv()
@@ -535,14 +582,17 @@
             return carry
 
         lax.fori_loop(0, count, step, 0)
-
+    tally_take(0)
+    tally_send(1)
     project(c * half, half // 256)
+    tally_take(1)
+    tally_send(2)
     x_step(0)
+    z_step(1)
     other_rows = pl.ds(pl.multiple_of((1 - c) * half, half), half)
     remote(t_ref.at[other_rows], t_ref.at[other_rows], y_sem.at[0], y_sem.at[1], me.ydev).wait_recv()
     project((1 - c) * half, half // 256)
     remote(rb.at[1 - c], rb.at[1 - c], y_sem.at[2], y_sem.at[3], me.ydev).wait_recv()
-
     length = lengths_ref[c]
     nblk = seq // BLK
     pos_block = lax.broadcasted_iota(jnp.int32, (128, seq), 1) // BLK
@@ -584,10 +634,9 @@
             return carry
 
         lax.fori_loop(0, seq // wide, step, 0)
-
     attend(0)
-    z_step(1)
     x_step(1)
+    z_step(2)
     attend(1)
     y_step(0)
     attend(2)
@@ -601,12 +650,11 @@
         go(remote(att_tok.at[:, to], att_ref.at[t], a_send.at[d], a_recv.at[d], me.z(to)))
     own_copy = pltpu.make_async_copy(att_tok.at[:, t], att_ref.at[t], loc_sem.at[4])
     own_copy.start()
-    z_step(2)
+    y_step(1)
     x_step(2)
-    y_step(1)
     z_step(3)
+    y_step(2)
     x_step(3)
-    y_step(2)
     y_step(3)
     for s in range(2):
         tok_ref[s] = t_ref[pl.ds(pl.multiple_of(s * half + t * 128, 128), 128), :]
@@ -626,14 +674,17 @@
     for copy in local[2:]:
         copy.wait()
     own_copy.wait()
+    tally_take(2)
     for copy, pred in sends:
         when(pred, copy.wait_send)
-
-
-def forward_attention(lengths, tokens, teacher, qkvb, upack, rbt, mask, seq):
-    heads = qkvb.shape[2] // HD
+    count_ref[...] = tally[5]
+
+
+def forward_attention(lengths, tokens, teacher, qkv, up, down, out, norm, blocks, valid):
+    seq = tokens.shape[1] * 2
+    heads = qkv.shape[2] // HD
     width = heads * HD
-    rows_f = qkvb.shape[1]
+    rows_f = qkv.shape[1]
     depth = rows_f * 4
     vm = pl.BlockSpec(memory_space=pltpu.VMEM)
     hbm = pl.BlockSpec(memory_space=pl.ANY)
@@ -650,15 +701,21 @@
         ((heads, seq, seq), bf16, vm),
         ((2, 128, depth), bf16, vm),
         ((2, 128, depth), bf16, vm),
-        ((2, 8, 128), f32, vm),
+        ((2, 8, seq // 2), f32, vm),
+        ((8, 128), f32, vm),
     ]
     return pl.pallas_call(
         forward_attention_kernel,
         name="forward_attention",
         out_shape=[jax.ShapeDtypeStruct(s, d) for s, d, _ in outs],
-        in_specs=[pl.BlockSpec(memory_space=pltpu.SMEM), hbm, hbm, vm, vm, vm, vm],
+        in_specs=[pl.BlockSpec(memory_space=pltpu.SMEM), hbm, hbm, *[vm] * 7],
         out_specs=[m for _, _, m in outs],
         scratch_shapes=[
+            pltpu.VMEM((rows_f, UW), bf16),
+            pltpu.VMEM(qkv.shape, bf16),
+            pltpu.VMEM((2, 8, 128), f32),
+            pltpu.VMEM((2, 8, seq // 2), f32),
+            pltpu.VMEM((6, 8, 128), f32),
             pltpu.VMEM((width, seq), bf16),
             pltpu.VMEM((seq, seq), f32),
             pltpu.VMEM((2, 8, 128), f32),
@@ -679,11 +736,12 @@
             dma((4, 2)),
             dma((4,)),
             dma((4,)),
+            dma((2, 3)),
         ],
         compiler_params=pltpu.CompilerParams(
             collective_id=0, has_side_effects=True, vmem_limit_bytes=VMEM_LIMIT
         ),
-    )(lengths, tokens, teacher, qkvb, upack, rbt, mask)
+    )(lengths, tokens, teacher, qkv, up, down, out, norm, blocks, valid)
 
 
 def column(row):
@@ -691,6 +749,11 @@
 
 
 def add_rows(dst, a, b, step=16):
+    if len(dst.shape) == 3:
+        for i in range(dst.shape[0]):
+            add_rows(dst.at[i], a.at[i], b.at[i], step)
+        return
+
     def one(i, carry):
         rows = pl.ds(pl.multiple_of(i * step, step), step)
         dst[rows, :] = a[rows, :] + b[rows, :]
@@ -759,19 +822,23 @@
 CHAIN_ORDER = ((3, 0), (0, 1), (2, 0), (1, 1), (1, 0), (2, 1))
 
 
+TAIL = None
+FF_COLS = 1536
+
+
 def backward_kernel(names, *refs):
-    r = dict(zip(names, refs, strict=True))
+    r = types.SimpleNamespace(**dict(zip(names, refs, strict=True)))
     me = Peers()
     f, c, t = me.f, me.c, me.t
     x = f // 2
     k = f % 2
-    depth = r["u"].shape[1]
+    depth = r.u.shape[1]
     rows_f = depth // 4
     hrows = rows_f // 2
     qrows = rows_f // 4
-    seq = r["t"].shape[0]
+    seq = r.t.shape[0]
     half = seq // 2
-    heads = r["q"].shape[0]
+    heads = r.q.shape[0]
     width = heads * HD
     sends = []
 
@@ -785,20 +852,17 @@
         when(pred, copy.start)
         sends.append((copy, pred))
 
-    loads = {}
-    order = ["att", "u0", "u1", "u2", "u3", "pt", "q", "k", "v", "kt", "w", "t"]
-    for i, name in enumerate(order):
-        if name[0] == "u":
-            j = int(name[1])
-            loads[name] = pltpu.make_async_copy(r["u"].at[j], r["u_v"].at[j], r["load_sem"].at[i])
-        else:
-            loads[name] = pltpu.make_async_copy(r[name], r[name + "_v"], r["load_sem"].at[i])
-        loads[name].start()
-    me.barrier()
-
-    att_v, u_v, g_v, act, slope = r["att_v"], r["u_v"], r["g_v"], r["act"], r["slope"]
+    def load(i, src, dst):
+        copy = pltpu.make_async_copy(src, dst, r.load_sem.at[i])
+        copy.start()
+        return copy
+
+    first = [load(0, r.att, r.att_v), *(load(1 + j, r.u.at[j], r.u_v.at[j]) for j in range(4))]
+    me.barrier(True)
+
+    att_v, u_v, g_v, act, slope = r.att_v, r.u_v, r.g_v, r.act, r.slope
     rows = 2 * 128
-    length = r["lengths"][c]
+    length = r.lengths[c]
     inv_width = 1.0 / depth
 
     def both(ref):
@@ -815,16 +879,17 @@
     def back(up, normed, inverse, gain):
         scaled = up * gain
         return inverse * (scaled - mean(scaled) - normed * mean(scaled * normed))
-
-    for name in ("att", "u0", "u1", "u2", "u3"):
-        loads[name].wait()
+    for copy in first:
+        copy.wait()
+    pairs = ((r.pt, r.pt_v), (r.q, r.q_v), (r.k, r.k_v), (r.v, r.v_v), (r.kt, r.kt_v), (r.w, r.w_v), (r.t, r.t_v))
+    later = [load(5 + i, src, dst) for i, (src, dst) in enumerate(pairs)]
     norms = u_v[0, :, 1728:1736].astype(f32).T
     gains = [norms[i : i + 1, :] for i in range(4)]
     att = [att_v[tt].reshape(rows, width) for tt in range(4)]
     attn = dot_nt(att[0], u_v[0, :, 1536:1728])
     for tt in range(1, 4):
         attn += dot_nt(att[tt], u_v[tt, :, 1536:1728])
-    normed_one, inverse_one = normalize(both(r["tok"]) + attn)
+    normed_one, inverse_one = normalize(both(r.tok) + attn)
     hidden = normed_one * gains[0] + gains[1]
     hidden_b = hidden.astype(bf16)
     cube = 0.044715
@@ -839,31 +904,30 @@
         bend = 0.5 * (1.0 + th) + 0.5 * upper * (1.0 - th * th) * root * (1.0 + 3.0 * cube * square)
         slope[tt] = bend.astype(bf16)
         return mixed + dot_nt(act_t, u_v[tt, :, 768:1536])
-
     mixed = lax.fori_loop(0, 4, up_step, jnp.zeros((rows, depth), f32))
     normed_two, inverse_two = normalize(hidden + mixed)
     result = normed_two * gains[2] + gains[3]
 
-    r["piece"][...] = result.astype(bf16).reshape(2, 128, depth)
+    r.piece[...] = result.astype(bf16).reshape(2, 128, depth)
     part = pl.ds(pl.multiple_of(t * 128, 128), 128)
-    lo = r["lo"]
-    go(remote(r["piece"].at[1 - c], lo.at[c, part], r["s_sem"].at[0], r["s_sem"].at[1], me.ydev))
-    own_lo = pltpu.make_async_copy(r["piece"].at[c], lo.at[c, part], r["load_sem"].at[12])
+    lo = r.lo
+    go(remote(r.piece.at[1 - c], lo.at[c, part], r.s_sem.at[0], r.s_sem.at[1], me.ydev))
+    own_lo = pltpu.make_async_copy(r.piece.at[c], lo.at[c, part], r.load_sem.at[12])
     own_lo.start()
 
     def lo_block(tt):
         return lo.at[:, pl.ds(pl.multiple_of(tt * 128, 128), 128), :]
 
-    lo_line = Line(me, go, lo_block, r["lo_send"], r["lo_recv"])
-
-    alive = jnp.concatenate([column(r["live"][0]), column(r["live"][1])], 0)
+    lo_line = Line(me, go, lo_block, r.lo_send, r.lo_recv)
+
+    alive = jnp.concatenate([column(r.live[s, :, part]) for s in range(2)], 0)
     row = lax.broadcasted_iota(jnp.int32, (rows, 1), 0)
     place = jnp.where(row < 128, row, row - 128 + half) + t * 128
     live = jnp.where((alive == 1.0) & (place < length), 1.0, 0.0)
-    differ = result - both(r["teach"])
+    differ = result - both(r.teach)
     weighed = differ * live
-    r["err"][0, 0] = jnp.sum(weighed * differ)
-    grad_y = weighed * (2.0 / (r["count"][0, 0] * depth))
+    missed = jnp.sum(jnp.sum(weighed * differ, 1, keepdims=True), 0, keepdims=True)
+    grad_y = weighed * (2.0 / (r.count[0:1, 0:1] * depth))
     sums = [None] * 4
     sums[2] = jnp.sum(grad_y * normed_two, 0, keepdims=True)
     sums[3] = jnp.sum(grad_y, 0, keepdims=True)
@@ -871,125 +935,204 @@
     gm = grad_two.astype(bf16)
     gm_t = grad_two.T.astype(bf16)
     hidden_t = hidden.T.astype(bf16)
-
     there = lo.at[1 - c, part]
-    remote(there, there, r["s_sem"].at[0], r["s_sem"].at[1], me.ydev).wait_recv()
+    remote(there, there, r.s_sem.at[0], r.s_sem.at[1], me.ydev).wait_recv()
     own_lo.wait()
     lo_line.start()
 
-    def down_step(tt, total):
+    far = 1 - x
+    trio = (me.core, me.xdev, me.ydev)
+
+    def region(ref, unit, at, n):
+        rows_at = pl.ds(pl.multiple_of(at, qrows), n)
+        return ref.at[:, rows_at, FF_COLS:UW] if unit is TAIL else ref.at[unit, rows_at, 0:FF_COLS]
+
+    def g_rows(unit, ff):
+        return region(g_v, unit, ff * rows_f, rows_f)
+
+    def rc_rows(xx, unit, at=0, n=rows_f):
+        return region(u_v, unit, xx * rows_f + at, n)
+
+    def room(n):
+        return lambda unit, i: region(u_v, unit, (4 + n) * hrows + i * qrows, qrows)
+
+    xg_at, yg_at = room(0), room(1)
+
+    def d_at(ref, unit):
+        return ref.at[:, :, FF_COLS:UW] if unit is TAIL else ref.at[unit, :, 0:FF_COLS]
+
+    def slot(unit):
+        return 4 if unit is TAIL else unit
+
+    def credit(unit):
+        for j, dev in enumerate(trio):
+            pl.semaphore_signal(r.free.at[j, slot(unit)], inc=1, device_id=dev, device_id_type=MESH)
+
+    def rc_copies(unit):
+        return [
+            remote(g_rows(unit, xx * 2 + 1 - k), rc_rows(xx, unit), r.rc_send.at[xx, slot(unit)],
+                   r.rc_recv.at[xx, slot(unit)], me.core)
+            for xx in (far, x)
+        ]
+
+    def far_copies(unit):
+        i = slot(unit)
+        h, other = c * hrows, (1 - c) * hrows
+        return [
+            remote(rc_rows(far, unit, other, qrows), d_at(r.dx, unit), r.dx_send.at[i], r.dx_recv.at[i], me.xdev),
+            remote(rc_rows(far, unit, other + qrows, qrows), d_at(r.dy, unit), r.dy_send.at[i], r.dy_recv.at[i], me.ydev),
+            remote(rc_rows(far, unit, h, qrows), xg_at(unit, 0), r.xg_send.at[i, 0], r.xg_recv.at[i, 0], me.xdev),
+        ]
+
+    def rc_step(unit):
+        pl.semaphore_wait(r.free.at[0, slot(unit)], 1)
+        for copy in rc_copies(unit):
+            copy.start()
+
+    def core_step(xx, unit):
+        view = rc_rows(xx, unit)
+        i = slot(unit)
+        remote(view, view, r.rc_send.at[xx, i], r.rc_recv.at[xx, i], me.core).wait_recv()
+        add_rows(view, view, g_rows(unit, xx * 2 + k))
+
+    def far_step(unit):
+        core_step(far, unit)
+        for j in (1, 2):
+            pl.semaphore_wait(r.free.at[j, slot(unit)], 1)
+        for copy in far_copies(unit):
+            copy.start()
+
+    def near_step(unit):
+        core_step(x, unit)
+        i = slot(unit)
+        mine = rc_rows(x, unit, (1 - c) * hrows + qrows, qrows)
+        go(remote(mine, yg_at(unit, 1), r.yg_send.at[i, 1], r.yg_recv.at[i, 1], me.ydev))
+
+    def diag_step(unit):
+        i = slot(unit)
+        dx, dy = d_at(r.dx, unit), d_at(r.dy, unit)
+        remote(dx, dx, r.dx_send.at[i], r.dx_recv.at[i], me.xdev).wait_recv()
+        mine = rc_rows(x, unit, (1 - c) * hrows, qrows)
+        add_rows(mine, mine, dx)
+        go(remote(mine, yg_at(unit, 0), r.yg_send.at[i, 0], r.yg_recv.at[i, 0], me.ydev))
+        remote(dy, dy, r.dy_send.at[i], r.dy_recv.at[i], me.ydev).wait_recv()
+        mine = rc_rows(far, unit, c * hrows + qrows, qrows)
+        add_rows(mine, mine, dy)
+        go(remote(mine, xg_at(unit, 1), r.xg_send.at[i, 1], r.xg_recv.at[i, 1], me.xdev))
+
+    def sum_step(unit):
+        at = slot(unit)
+        for i in (0, 1):
+            xg, yg = xg_at(unit, i), yg_at(unit, i)
+            mine = rc_rows(x, unit, c * hrows + i * qrows, qrows)
+            remote(xg, xg, r.xg_send.at[at, i], r.xg_recv.at[at, i], me.xdev).wait_recv()
+            add_rows(mine, mine, xg)
+            remote(yg, yg, r.yg_send.at[at, i], r.yg_recv.at[at, i], me.ydev).wait_recv()
+            add_rows(mine, mine, yg)
+
+    def own_rows(tt):
+        return u_v.at[tt, pl.ds(pl.multiple_of(x * rows_f + c * hrows, hrows), hrows), :]
+
+    w_chain = Chain(
+        me, go, own_rows, lambda tt: u_v.at[tt, pl.ds(6 * hrows, hrows), :],
+        lambda tt: u_v.at[tt, pl.ds(7 * hrows, hrows), :], r.zw_send, r.zw_recv_l, r.zw_recv_r,
+    )
+
+    def turn(i):
+        return ((i + 1) % 2) * (3 - i // 2) + (i % 2) * (i // 2)
+
+    ORDER = (3, 0, 2, 1)
+
+    def down_step(i, total):
+        tt = turn(i)
         ga = dot_nn(gm, u_v[tt, :, 768:1536])
         gu = (ga * slope[tt].astype(f32)).astype(bf16)
         g_v[tt, :, 768:1536] = dot_nn(gm_t, act[tt]).astype(bf16)
         g_v[tt, :, 0:768] = dot_nn(hidden_t, gu).astype(bf16)
-        return total + dot_nt(gu, u_v[tt, :, 0:768])
+        total = total + dot_nt(gu, u_v[tt, :, 0:768])
+        credit(tt)
+
+        @pl.when(i >= 1)
+        def _():
+            rc_step(turn(i - 1))
+
+        @pl.when(i >= 2)
+        def _():
+            far_step(turn(i - 2))
+
+        return total
 
     grad_hidden = lax.fori_loop(0, 4, down_step, grad_two)
+    rc_step(ORDER[3])
     sums[0] = jnp.sum(grad_hidden * normed_one, 0, keepdims=True)
     sums[1] = jnp.sum(grad_hidden, 0, keepdims=True)
     grad_one = back(grad_hidden, normed_one, inverse_one, gains[0])
-    r["gone"][...] = grad_one.reshape(2, 128, depth)
+    r.gone[...] = grad_one.reshape(2, 128, depth)
     ga = grad_one.astype(bf16)
-    gatt, do_in = r["gatt"], r["do_in"]
+    gatt, do_in = r.gatt, r.do_in
     for tt in range(4):
         back_t = dot_nn(ga, u_v[tt, :, 1536:1728]).astype(bf16)
         gatt[tt] = back_t.reshape(2, 128, width)
     for d in (1, 2, 3):
         to = (t + d) % 4
-        go(remote(gatt.at[to], do_in.at[t], r["a_send"].at[d], r["a_recv"].at[d], me.z(to)))
+        go(remote(gatt.at[to], do_in.at[t], r.a_send.at[d], r.a_recv.at[d], me.z(to)))
     do_in[t] = gatt[t]
-    for i, dev in enumerate((me.core, me.xdev, me.ydev)):
-        pl.semaphore_signal(r["free"].at[i], inc=1, device_id=dev, device_id_type=MESH)
+    credit(TAIL)
+    far_step(ORDER[2])
     ga_t = grad_one.T.astype(bf16)
-    norm_rows = jnp.concatenate(sums + [jnp.zeros((4, depth), f32)], 0)
-    norm_cols = jnp.concatenate([norm_rows.T, jnp.zeros((depth, UW - 1736), f32)], 1).astype(bf16)
+    ez, ef = r.ez, r.ef
+    mine_at = f * 2 + c
+    ez[t] = jnp.concatenate(sums + [jnp.broadcast_to(missed, (4, depth))], 0)
+    for d in (1, 2, 3):
+        go(remote(ez.at[t], ez.at[t], r.e_sem.at[0, d], r.e_sem.at[1, d], me.z((t + d) % 4)))
+
+    def sums_on():
+        for d in (1, 2, 3):
+            src = ez.at[(t + 4 - d) % 4]
+            remote(src, src, r.e_sem.at[0, d], r.e_sem.at[1, d], me.z(t)).wait_recv()
+        ef[mine_at] = (ez[0] + ez[1]) + (ez[2] + ez[3])
+        for d, dev in me.owners():
+            go(remote(ef.at[mine_at], ef.at[mine_at], r.e_sem.at[0, 3 + d], r.e_sem.at[1, 3 + d], dev))
+
+    def sums_end():
+        for d, dev in me.owners():
+            ff, cc = me.flipped(d)
+            src = ef.at[ff * 2 + cc]
+            remote(src, src, r.e_sem.at[0, 3 + d], r.e_sem.at[1, 3 + d], dev).wait_recv()
+        total = ef[0]
+        for i in range(1, 8):
+            total += ef[i]
+        r.sums[...] = total
+
     for tt in range(4):
         g_v[tt, :, 1536:1728] = dot_nn(ga_t, att[tt]).astype(bf16)
-        g_v[tt, :, 1728:1792] = norm_cols
-
-    far = 1 - x
-    for i in range(3):
-        pl.semaphore_wait(r["free"].at[i], 1)
-
-    def g_rows(tt, ff):
-        return g_v.at[tt, pl.ds(pl.multiple_of(ff * rows_f, rows_f), rows_f), :]
-
-    def rc_all(xx, tt):
-        return u_v.at[tt, pl.ds(pl.multiple_of(xx * rows_f, rows_f), rows_f), :]
-
-    def room(n):
-        return lambda tt, i=0, size=hrows: u_v.at[tt, pl.ds((4 + n) * hrows + i * qrows, size), :]
-
-    xg_at, yg_at, zl_at, zr_at = (room(n) for n in range(4))
-
-    for xx in (far, x):
-        for tt in range(4):
-            ff = xx * 2 + (1 - k)
-            go(remote(g_rows(tt, ff), rc_all(xx, tt), r["rc_send"].at[xx, tt], r["rc_recv"].at[xx, tt], me.core))
-
+        g_v[tt, :, 1728:1792] = jnp.zeros((depth, UW - 1728), bf16)
+    rc_step(TAIL)
+    near_step(ORDER[0])
+    far_step(ORDER[3])
+    near_step(ORDER[1])
     lo_line.step(1)
-
-    def rc_rows(xx, tt, h, q0, n):
-        return u_v.at[tt, pl.ds(pl.multiple_of(xx * rows_f + h * hrows + q0, qrows), n), :]
-
-    def core_step(xx, tt):
-        view = rc_all(xx, tt)
-        remote(view, view, r["rc_send"].at[xx, tt], r["rc_recv"].at[xx, tt], me.core).wait_recv()
-        add_rows(view, view, g_rows(tt, xx * 2 + k))
-
-    def far_step(tt):
-        core_step(far, tt)
-        dx, dy = r["dx"], r["dy"]
-        go(remote(rc_rows(far, tt, 1 - c, 0, qrows), dx.at[tt], r["dx_send"].at[tt], r["dx_recv"].at[tt], me.xdev))
-        go(remote(rc_rows(far, tt, 1 - c, qrows, qrows), dy.at[tt], r["dy_send"].at[tt], r["dy_recv"].at[tt], me.ydev))
-        go(remote(rc_rows(far, tt, c, 0, qrows), xg_at(tt, 0, qrows), r["xg_send"].at[tt, 0], r["xg_recv"].at[tt, 0], me.xdev))
-
-    def near_step(tt):
-        core_step(x, tt)
-        go(remote(rc_rows(x, tt, 1 - c, qrows, qrows), yg_at(tt, 1, qrows), r["yg_send"].at[tt, 1], r["yg_recv"].at[tt, 1], me.ydev))
-
-    def diag_step(tt):
-        dx, dy = r["dx"], r["dy"]
-        remote(dx.at[tt], dx.at[tt], r["dx_send"].at[tt], r["dx_recv"].at[tt], me.xdev).wait_recv()
-        mine = rc_rows(x, tt, 1 - c, 0, qrows)
-        add_rows(mine, mine, dx.at[tt])
-        go(remote(mine, yg_at(tt, 0, qrows), r["yg_send"].at[tt, 0], r["yg_recv"].at[tt, 0], me.ydev))
-        remote(dy.at[tt], dy.at[tt], r["dy_send"].at[tt], r["dy_recv"].at[tt], me.ydev).wait_recv()
-        mine = rc_rows(far, tt, c, qrows, qrows)
-        add_rows(mine, mine, dy.at[tt])
-        go(remote(mine, xg_at(tt, 1, qrows), r["xg_send"].at[tt, 1], r["xg_recv"].at[tt, 1], me.xdev))
-
-    def sum_step(tt):
-        for i in (0, 1):
-            xg, yg = xg_at(tt, i, qrows), yg_at(tt, i, qrows)
-            mine = rc_rows(x, tt, c, i * qrows, qrows)
-            remote(xg, xg, r["xg_send"].at[tt, i], r["xg_recv"].at[tt, i], me.xdev).wait_recv()
-            add_rows(mine, mine, xg)
-            remote(yg, yg, r["yg_send"].at[tt, i], r["yg_recv"].at[tt, i], me.ydev).wait_recv()
-            add_rows(mine, mine, yg)
-
-    ORDER = (3, 0, 2, 1)
-    w_chain = Chain(
-        me, go, lambda tt: rc_rows(x, tt, c, 0, hrows), zl_at, zr_at,
-        r["zw_send"], r["zw_recv_l"], r["zw_recv_r"],
-    )
-
-    for tt in ORDER:
-        far_step(tt)
+    diag_step(ORDER[0])
+    far_step(TAIL)
+    near_step(ORDER[2])
+    near_step(ORDER[3])
+    near_step(TAIL)
+    for unit in (*ORDER, TAIL):
+        sends.extend((copy, None) for copy in rc_copies(unit) + far_copies(unit))
     lo_line.step(2)
 
-    for name in ("pt", "q", "k", "v", "kt", "w", "t"):
-        loads[name].wait()
-    do, proj, dqt, dk, dv = r["do"], r["proj"], r["dqt"], r["dk"], r["dv"]
+    for copy in later:
+        copy.wait()
+    do, proj, dqt, dk, dv = r.do, r.proj, r.dqt, r.dk, r.dv
     for d in (1, 2, 3):
         src = (t + 4 - d) % 4
-        remote(do_in.at[src], do_in.at[src], r["a_send"].at[d], r["a_recv"].at[d], me.z(src)).wait_recv()
+        remote(do_in.at[src], do_in.at[src], r.a_send.at[d], r.a_recv.at[d], me.z(src)).wait_recv()
     for s in range(2):
         for tt in range(4):
             at = s * half + tt * 128
             for h in range(heads):
                 do[h, at : at + 128, :] = do_in[tt, s, :, h * HD : (h + 1) * HD]
-    q_v, k_v, v_v, kt_v, pt_v, t_v, w_v = (r[n + "_v"] for n in ("q", "k", "v", "kt", "pt", "t", "w"))
+    q_v, k_v, v_v, kt_v, pt_v, t_v, w_v = (r.q_v, r.k_v, r.v_v, r.kt_v, r.pt_v, r.t_v, r.w_v)
     scale = HD ** (-0.5)
     wide = 256
 
@@ -1013,17 +1156,13 @@
         lax.fori_loop(0, seq // wide, step, 0)
         proj[1, :, h * HD : (h + 1) * HD] = (dk[...] * scale).astype(bf16)
         proj[2, :, h * HD : (h + 1) * HD] = dv[...].astype(bf16)
-
     attend_back(0)
-    for tt in ORDER:
-        near_step(tt)
+    diag_step(ORDER[1])
     attend_back(1)
-    for tt in ORDER:
-        diag_step(tt)
-    lo_line.step(3)
+    diag_step(ORDER[2])
     attend_back(2)
     proj[0] = (dqt[...].T * scale).astype(bf16)
-    ip = r["ip"]
+    ip = r.ip
 
     def rows_step(i, carry):
         at = pl.ds(pl.multiple_of(i * 128, 128), 128)
@@ -1034,84 +1173,123 @@
         return carry
 
     lax.fori_loop(0, seq // 128, rows_step, 0)
-
     def ip_chain(j, s):
         return Chain(
             me, go, lambda tt: ip.at[s, tt], lambda tt: act.at[tt, pl.ds(j * 128, 128), :], lambda tt: slope.at[tt, pl.ds(j * 128, 128), :],
-            r["i_send"].at[j], r["i_recv_l"].at[j], r["i_recv_r"].at[j],
+            r.i_send.at[j], r.i_recv_l.at[j], r.i_recv_r.at[j],
         )
 
     chains = [ip_chain(0, 1 - c), ip_chain(1, c)]
-    for tt, way in CHAIN_ORDER[:2]:
-        chains[0].pass_on(tt, way)
-    qg = r["qg"]
-    for j in range(3):
-        qg[j] = dot_tn(t_v[...], proj[j]).astype(bf16)
+    ig, igp, qg, qc, qs, fin = r.ig, r.igp, r.qg, r.qc, r.q_sem, r.fin
 
     def q_rows(ff):
         return qg.at[:, pl.ds(pl.multiple_of(ff * rows_f, rows_f), rows_f), :]
 
-    qc, qs = r["qc"], r["q_sem"]
-    go(remote(q_rows(far * 2 + 1 - k), qc.at[0], qs.at[0], qs.at[1], me.core))
-    go(remote(q_rows(x * 2 + 1 - k), qc.at[1], qs.at[2], qs.at[3], me.core))
-    for tt, way in CHAIN_ORDER[2:]:
-        chains[0].pass_on(tt, way)
-    remote(qc.at[0], qc.at[0], qs.at[0], qs.at[1], me.core).wait_recv()
-    qc[0] = qc[0] + qg[:, pl.ds(pl.multiple_of((far * 2 + k) * rows_f, rows_f), rows_f), :]
-    go(remote(qc.at[0], qc.at[2], qs.at[4], qs.at[5], me.xdev))
-    for tt, way in CHAIN_ORDER:
-        chains[1].pass_on(tt, way)
-    remote(qc.at[1], qc.at[1], qs.at[2], qs.at[3], me.core).wait_recv()
-    qc[1] = qc[1] + qg[:, pl.ds(pl.multiple_of((x * 2 + k) * rows_f, rows_f), rows_f), :]
-    for tt in ORDER:
-        sum_step(tt)
-    remote(qc.at[2], qc.at[2], qs.at[4], qs.at[5], me.xdev).wait_recv()
-    qc[1] = qc[1] + qc[2]
-    go(remote(qc.at[1], qc.at[3], qs.at[6], qs.at[7], me.ydev))
-
-    ig = r["ig"]
-    igp = r["igp"]
-
     def finish(j, s):
         chains[j].end()
-        igp[j] = (ip[s, t].astype(f32) + r["gone"][s]).astype(bf16)
-
-    finish(0, 1 - c)
-    go(remote(igp.at[0], ig.at[c, part], r["s_sem"].at[2], r["s_sem"].at[3], me.ydev))
-    finish(1, c)
-    own_ig = pltpu.make_async_copy(igp.at[1], ig.at[c, part], r["load_sem"].at[13])
-    own_ig.start()
+        igp[j] = (ip[s, t].astype(f32) + r.gone[s]).astype(bf16)
 
     def ig_line(j, s):
         def block(tt):
             return ig.at[s, pl.ds(pl.multiple_of(tt * 128, 128), 128), :]
 
-        return Line(me, go, block, r["ig_send"].at[j], r["ig_recv"].at[j])
+        return Line(me, go, block, r.ig_send.at[j], r.ig_recv.at[j])
 
     lines = [ig_line(0, c), ig_line(1, 1 - c)]
+
+    def sum_pass(tt, passes):
+        sum_step(tt)
+        for at, way in passes:
+            w_chain.pass_on(at, way)
+
+    def q_take(i, j, dev):
+        remote(qc.at[i], qc.at[i], qs.at[j], qs.at[j + 1], dev).wait_recv()
+
+    def q_add(i, ff):
+        qc[i] = qc[i] + qg[:, pl.ds(pl.multiple_of(ff * rows_f, rows_f), rows_f), :]
+
+    for tt, way in CHAIN_ORDER[:2]:
+        chains[0].pass_on(tt, way)
+    diag_step(ORDER[3])
+    diag_step(TAIL)
+    sums_on()
+    for tt, way in CHAIN_ORDER[2:]:
+        chains[0].pass_on(tt, way)
+    for j in range(3):
+        qg[j] = dot_tn(t_v[...], proj[j]).astype(bf16)
+    go(remote(q_rows(far * 2 + 1 - k), qc.at[0], qs.at[0], qs.at[1], me.core))
+    go(remote(q_rows(x * 2 + 1 - k), qc.at[1], qs.at[2], qs.at[3], me.core))
+    for tt, way in CHAIN_ORDER:
+        chains[1].pass_on(tt, way)
+    q_take(0, 0, me.core)
+    q_add(0, far * 2 + k)
+    go(remote(qc.at[0], qc.at[2], qs.at[4], qs.at[5], me.xdev))
+    q_take(1, 2, me.core)
+    q_add(1, x * 2 + k)
+    finish(0, 1 - c)
+    go(remote(igp.at[0], ig.at[c, part], r.s_sem.at[2], r.s_sem.at[3], me.ydev))
+    lo_line.step(3)
+    sum_step(TAIL)
+    sum_pass(3, CHAIN_ORDER[:1])
+    sum_pass(0, CHAIN_ORDER[1:2])
+    finish(1, c)
+    own_ig = pltpu.make_async_copy(igp.at[1], ig.at[c, part], r.load_sem.at[13])
+    own_ig.start()
     own_ig.wait()
     lines[0].start()
     there = ig.at[1 - c, part]
-    remote(there, there, r["s_sem"].at[2], r["s_sem"].at[3], me.ydev).wait_recv()
+    remote(there, there, r.s_sem.at[2], r.s_sem.at[3], me.ydev).wait_recv()
     lines[1].start()
-    for tt, way in CHAIN_ORDER[:2]:
-        w_chain.pass_on(tt, way)
+    q_take(2, 4, me.xdev)
+    qc[1] = qc[1] + qc[2]
+    go(remote(qc.at[1], qc.at[3], qs.at[6], qs.at[7], me.ydev))
+    sum_pass(2, ((2, 0),))
+    sum_pass(1, ((1, 1), (1, 0), (2, 1)))
     lines[0].step(1)
     lines[1].step(1)
-    for tt, way in CHAIN_ORDER[2:]:
-        w_chain.pass_on(tt, way)
+    w_chain.end()
+    fin[c] = own_rows(t)[...]
+    go(remote(fin.at[c], fin.at[c], r.s_sem.at[4], r.s_sem.at[5], me.ydev))
+    q_take(3, 6, me.ydev)
+    qsum = r.qsum
+    total = jnp.zeros((1, width), f32)
+    for j in range(3):
+        qsum[j] = qc[1, j].astype(f32) + qc[3, j].astype(f32)
+        total += jnp.sum(qsum[j] * qsum[j], 0, keepdims=True)
+    total = 0.5 * jnp.sum(total, 1, keepdims=True)
+
+    def square_step(i, carry):
+        row = fin[c, pl.ds(pl.multiple_of(i * 16, 16), 16), :].astype(f32)
+        return carry + jnp.sum(row * row, 0, keepdims=True)
+
+    wide_total = lax.fori_loop(0, hrows // 16, square_step, jnp.zeros((1, UW), f32))
+    total += jnp.sum(wide_total, 1, keepdims=True)
+    sz, sf = r.sz, r.sf
+    sz[t] = jnp.broadcast_to(total, (8, 128))
+    for d in (1, 2, 3):
+        go(remote(sz.at[t], sz.at[t], r.f_sem.at[0, d], r.f_sem.at[1, d], me.z((t + d) % 4)))
     lines[0].step(2)
     lines[1].step(2)
-    w_chain.end()
-    fin = r["fin"]
-    fin[c] = rc_rows(x, t, c, 0, hrows)[...]
-    go(remote(fin.at[c], fin.at[c], r["s_sem"].at[4], r["s_sem"].at[5], me.ydev))
+    for d in (1, 2, 3):
+        src = sz.at[(t + 4 - d) % 4]
+        remote(src, src, r.f_sem.at[0, d], r.f_sem.at[1, d], me.z(t)).wait_recv()
+    mine = f * 2 + c
+    sf[mine] = (sz[0] + sz[1]) + (sz[2] + sz[3])
+    for d, dev in me.owners():
+        go(remote(sf.at[mine], sf.at[mine], r.f_sem.at[0, 3 + d], r.f_sem.at[1, 3 + d], dev))
     lines[0].step(3)
     lines[1].step(3)
-    remote(qc.at[3], qc.at[3], qs.at[6], qs.at[7], me.ydev).wait_recv()
-    r["qsum"][...] = qc[1].astype(f32) + qc[3].astype(f32)
-    remote(fin.at[1 - c], fin.at[1 - c], r["s_sem"].at[4], r["s_sem"].at[5], me.ydev).wait_recv()
-    r["gsum"][...] = fin[...].reshape(rows_f, UW).astype(f32)
+    remote(fin.at[1 - c], fin.at[1 - c], r.s_sem.at[4], r.s_sem.at[5], me.ydev).wait_recv()
+    r.gsum[...] = fin[...].reshape(rows_f, UW)
+    sums_end()
+    for d, dev in me.owners():
+        ff, cc = me.flipped(d)
+        src = sf.at[ff * 2 + cc]
+        remote(src, src, r.f_sem.at[0, 3 + d], r.f_sem.at[1, 3 + d], dev).wait_recv()
+    all_sq = sf[0]
+    for i in range(1, 8):
+        all_sq += sf[i]
+    r.squares[...] = all_sq
     for copy, pred in sends:
         when(pred, copy.wait_send)
 
@@ -1133,15 +1311,16 @@
         return pltpu.VMEM(shape, f32)
 
     ins = dict(
-        lengths=(lengths, smem), count=(count, smem), att=(att, hbm), u=(u, hbm), tok=(tok, vm), teach=(teach, vm),
+        lengths=(lengths, smem), count=(count, vm), att=(att, hbm), u=(u, hbm), tok=(tok, vm), teach=(teach, vm),
         live=(live, vm), q=(q, hbm), k=(k, hbm), v=(v, hbm), kt=(kt, hbm), pt=(pt, hbm), t=(tokens, hbm), w=(w, hbm),
     )
     outs = dict(
         lo=((2, seq // 2, depth), bf16, hbm),
         ig=((2, seq // 2, depth), bf16, hbm),
-        gsum=((rows_f, UW), f32, vm),
+        gsum=((rows_f, UW), bf16, vm),
         qsum=((3, rows_f, width), f32, vm),
-        err=((1, 1), f32, smem),
+        sums=((8, depth), f32, vm),
+        squares=((8, 128), f32, vm),
     )
     h, qr = rows_f // 2, rows_f // 4
     scratch = dict(
@@ -1153,10 +1332,12 @@
         dk=vf(seq, HD), dv=vf(seq, HD), ip=vb(2, 4, 128, depth),
         igp=vb(2, 128, depth), qg=vb(3, depth, width), qc=vb(4, 3, rows_f, width), fin=vb(2, h, UW),
         load_sem=dma((14,)), s_sem=dma((6,)), lo_send=dma((2, 4)), lo_recv=dma((4,)), a_send=dma((4,)), a_recv=dma((4,)),
-        rc_send=dma((2, 4)), rc_recv=dma((2, 4)), dx_send=dma((4,)), dx_recv=dma((4,)), dy_send=dma((4,)),
-        dy_recv=dma((4,)), xg_send=dma((4, 2)), xg_recv=dma((4, 2)), yg_send=dma((4, 2)), yg_recv=dma((4, 2)),
+        rc_send=dma((2, 5)), rc_recv=dma((2, 5)), dx_send=dma((5,)), dx_recv=dma((5,)), dy_send=dma((5,)),
+        dy_recv=dma((5,)), xg_send=dma((5, 2)), xg_recv=dma((5, 2)), yg_send=dma((5, 2)), yg_recv=dma((5, 2)),
         zw_send=dma((4,)), zw_recv_l=dma((4,)), zw_recv_r=dma((4,)), i_send=dma((2, 4)), i_recv_l=dma((2, 4)),
-        i_recv_r=dma((2, 4)), ig_send=dma((2, 2, 4)), ig_recv=dma((2, 4)), q_sem=dma((8,)), free=pltpu.SemaphoreType.REGULAR((3,)),
+        i_recv_r=dma((2, 4)), ig_send=dma((2, 2, 4)), ig_recv=dma((2, 4)), q_sem=dma((8,)), ez=vf(4, 8, depth), ef=vf(8, 8, depth),
+        sz=vf(4, 8, 128), sf=vf(8, 8, 128), e_sem=dma((2, 11)), f_sem=dma((2, 11)),
+        free=pltpu.SemaphoreType.REGULAR((3, 5)),
     )
     return pl.pallas_call(
         functools.partial(backward_kernel, (*ins, *outs, *scratch)),
@@ -1168,6 +1349,92 @@
         compiler_params=pltpu.CompilerParams(
             collective_id=1, has_side_effects=True, vmem_limit_bytes=60 * 2**20
         ),
+    )(*(a for a, _ in ins.values()))
+
+
+def update_kernel(names, *refs):
+    r = types.SimpleNamespace(**dict(zip(names, refs, strict=True)))
+    f = lax.axis_index("fsdp")
+    copy = pltpu.make_async_copy(r.lo, r.held, r.sem.at[0])
+    copy.start()
+    depth = r.sums.shape[1]
+    rows_f = depth // 4
+    sums = r.sums[0:4, :]
+    total = r.squares[0:1, 0:1] + jnp.sum(jnp.sum(sums * sums, 1, keepdims=True), 0, keepdims=True)
+    norm = jnp.sqrt(total)
+    factor = jnp.minimum(1.0, clip_level / (norm + 1e-06))
+    r.norm[...] = norm
+    r.loss[...] = r.sums[4:5, 0:1] / (r.count[0:1, 0:1] * depth)
+    steps = jnp.full((1, 1), r.steps[0]).astype(f32)
+    one = 1.0 / (1.0 - jnp.exp(steps * -0.10536051565782628))
+    two = 1.0 / (1.0 - jnp.exp(steps * -0.0010005003335835335))
+
+    def move(name, grad, at, rate):
+        clipped = grad * factor
+        new_moment = beta_one * getattr(r, name + "_m")[at] + (1.0 - beta_one) * clipped
+        new_square = beta_two * getattr(r, name + "_s")[at] + (1.0 - beta_two) * clipped * clipped
+        weight = getattr(r, name + "_w")[at]
+        step = new_moment * one / (jnp.sqrt(new_square * two) + adam_eps) + decay_rate * weight
+        getattr(r, name + "_w_new")[at] = weight - rate * step
+        getattr(r, name + "_m_new")[at] = new_moment
+        getattr(r, name + "_s_new")[at] = new_square
+
+    gsum = r.gsum
+
+    def rows_step(i, carry):
+        rows = pl.ds(pl.multiple_of(i * 16, 16), 16)
+        move("up", gsum[rows, 0:768].astype(f32), (rows, slice(None)), rate_list[2])
+        move("down", gsum[rows, 768:1536].astype(f32), (rows, slice(None)), rate_list[3])
+        for j in range(3):
+            move("qkv", r.qsum[j, rows, :], (j, rows, slice(None)), rate_list[0])
+        return carry
+
+    lax.fori_loop(0, rows_f // 16, rows_step, 0)
+    move("out", gsum[:, 1536:1728].astype(f32).T, (slice(None), slice(None)), rate_list[1])
+    mine = sums[:, 0:rows_f]
+    for i in range(1, 4):
+        mine = jnp.where(f == i, sums[:, i * rows_f : (i + 1) * rows_f], mine)
+    move("norm", mine, (slice(None), slice(None)), rate_list[4])
+
+    def cast_step(i, carry):
+        rows = pl.ds(pl.multiple_of(i * 64, 64), 64)
+        for s in range(2):
+            r.input_grad[s, rows, :] = r.ig[s, rows, :].astype(f32)
+        return carry
+
+    copy.wait()
+    copy = pltpu.make_async_copy(r.held, r.layer_out, r.sem.at[1])
+    copy.start()
+    lax.fori_loop(0, r.ig.shape[1] // 64, cast_step, 0)
+    copy.wait()
+
+
+def update(steps, lo, ig, gsum, qsum, sums, squares, count, state):
+    vm = pl.BlockSpec(memory_space=pltpu.VMEM)
+    smem = pl.BlockSpec(memory_space=pltpu.SMEM)
+    hbm = pl.BlockSpec(memory_space=pl.ANY)
+    ins = dict(
+        steps=(steps, smem), lo=(lo, hbm), ig=(ig, vm), gsum=(gsum, vm), qsum=(qsum, vm), sums=(sums, vm),
+        squares=(squares, vm), count=(count, vm),
+    )
+    outs = dict(
+        layer_out=(jax.ShapeDtypeStruct(lo.shape, bf16), hbm),
+        loss=(jax.ShapeDtypeStruct((1, 1), f32), vm),
+        input_grad=(jax.ShapeDtypeStruct(ig.shape, f32), vm),
+        norm=(jax.ShapeDtypeStruct((1, 1), f32), vm),
+    )
+    for name, group in state.items():
+        for kind, array in zip("wms", group):
+            ins[f"{name}_{kind}"] = (array, vm)
+            outs[f"{name}_{kind}_new"] = (jax.ShapeDtypeStruct(array.shape, f32), vm)
+    return pl.pallas_call(
+        functools.partial(update_kernel, (*ins, *outs, "held", "sem")),
+        name="update",
+        out_shape=[shape for shape, _ in outs.values()],
+        in_specs=[m for _, m in ins.values()],
+        out_specs=[m for _, m in outs.values()],
+        scratch_shapes=[pltpu.VMEM(lo.shape, bf16), pltpu.SemaphoreType.DMA((2,))],
+        compiler_params=pltpu.CompilerParams(vmem_limit_bytes=50 * 2**20),
     )(*(a for a, _ in ins.values()))
 
 
@@ -1194,54 +1461,23 @@
     norm_moment,
     norm_square,
 ):
-    c, t = lax.axis_index("ctx"), lax.axis_index("tp")
-    seqs, tok_count, width = tokens.shape
-    seq = tok_count * 2
-    upack = jnp.concatenate(
-        [
-            up_weight,
-            down_weight.T,
-            out_weight.T,
-            norm_params.T,
-            jnp.zeros((192, 60), f32),
-        ],
-        1,
-    ).astype(bf16)
-    qkvb = qkv_weight.astype(bf16)
-    rbt = jnp.pad(
-        jnp.swapaxes(random_blocks, 1, 2).astype(f32), ((0, 0), (0, 5), (0, 120))
-    )
-    mask = jnp.broadcast_to(valid_mask.reshape(seqs, 4, 1, 128).astype(f32), (seqs, 4, 8, 128))
-    positions = c * tok_count + jnp.arange(tok_count, dtype=jnp.int32)
-    live_rows = ((valid_mask == 1) & (positions[None, :] < lengths[:, None])).astype(f32)
-    live_count = lax.psum(jnp.sum(live_rows), ("fsdp", "ctx"))
-    att, u, tk, w, q, k, v, kt, pt, tok, teach, live = forward_attention(
-        lengths, tokens, teacher, qkvb, upack, rbt, mask, seq
-    )
-    layer_out, ig, g, qkv_grad, err = backward(
-        lengths, live_count.reshape(1, 1), att, u, tok, teach, live, q, k, v, kt, pt, tk, w
-    )
-    error_total = lax.psum(err[0, 0], ("fsdp", "ctx", "tp"))
-    loss_value = error_total / (live_count * width)
-    input_grad = ig.astype(f32)
-    up_grad, down_grad, out_grad, norm_grad = g[:, :768], g[:, 768:1536].T, g[:, 1536:1728].T, g[:, 1728:1732].T
-    shards = (qkv_grad, out_grad, up_grad, down_grad, norm_grad)
-    squares = sum(jnp.sum(m * m) for m in shards[:4]) + jnp.where(t == 0, jnp.sum(norm_grad * norm_grad), 0.0)
-    grad_norm = jnp.sqrt(lax.psum(squares, ("fsdp", "tp")))
-    factor = jnp.minimum(1.0, clip_level / (grad_norm + 1e-06))
-    steps_done = step_count[0].astype(f32)
-    state = (
-        (qkv_weight, qkv_moment, qkv_square),
-        (out_weight, out_moment, out_square),
-        (up_weight, up_moment, up_square),
-        (down_weight, down_moment, down_square),
-        (norm_params, norm_moment, norm_square),
-    )
-    new = [
-        adam_update(weight, grad, moment, square, factor, steps_done, rate)
-        for (weight, moment, square), grad, rate in zip(state, shards, rate_list)
-    ]
-    return (layer_out, loss_value, input_grad, grad_norm, *(v for group in new for v in group))
+    blocks = jnp.transpose(random_blocks, (2, 0, 1))
+    att, u, tk, w, q, k, v, kt, pt, tok, teach, live, count = forward_attention(
+        lengths, tokens, teacher, qkv_weight, up_weight, down_weight.T, out_weight, norm_params, blocks, valid_mask
+    )
+    lo, ig, gsum, qsum, sums, squares = backward(lengths, count, att, u, tok, teach, live, q, k, v, kt, pt, tk, w)
+    state = dict(
+        qkv=(qkv_weight, qkv_moment, qkv_square),
+        out=(out_weight, out_moment, out_square),
+        up=(up_weight, up_moment, up_square),
+        down=(down_weight.T, down_moment.T, down_square.T),
+        norm=(norm_params, norm_moment, norm_square),
+    )
+    layer_out, loss, input_grad, grad_norm, *new = update(
+        step_count, lo, ig, gsum, qsum, sums, squares, count, state
+    )
+    new[9:12] = [v.T for v in new[9:12]]
+    return (layer_out, loss.reshape(()), input_grad, grad_norm.reshape(()), *new)
 
 
 def solution(mesh):

time: 383 us -> 239 us (0.62)
  blocking collectives: 85.4 us -> 0 us
  other arithmetic: 20.6 us -> 0 us
  Pallas kernels: 253 us -> 235 us
  local copies, waits for them, and re-layouts: 13.9 us -> 2.54 us
  between operations: 9.32 us -> 1.66 us
    psum x3 -> x0, blocking collectives: 85.4 us -> none  [the longest x1 40.1 us: body_swapped(): error_total = lax.psum(err[0, 0], ('fsdp', 'ctx', 'tp'))]
    pallas_call x1, Pallas kernels: 165 us -> 150 us  [backward(): pl.pallas_call(functools.partial(backward_kernel, (*ins, *outs, *scratch)...]
    pallas_call x1, Pallas kernels: 88 us -> 75.3 us  [forward_attention(): pl.pallas_call(forward_attention_kernel, name='forward_attention', out_sh...]
    pallas_call x0 -> x1, Pallas kernels: none -> 9.54 us  [update(): pl.pallas_call(functools.partial(update_kernel, (*ins, *outs, 'held', 'se...]
    sub x5 -> x0, other arithmetic: 9.02 us -> none  [adam_update(): weight - rate * (corrected / (jnp.sqrt(scaled) + adam_eps) + decay_rate *...]
    unnamed x47 -> x28, local copies, waits for them, and re-layouts: 10.2 us -> 2.54 us
    reduce_sum x5 -> x0, other arithmetic: 6.87 us -> none  [the longest x3 5.51 us: body_swapped(): jnp.sum(m * m)]
where the time goes in v3:
time: 239 us
  Pallas kernels  235 us (98%)
  local copies, waits for them, and re-layouts  2.54 us (1%)
    pallas_call x1, Pallas kernels, backward(): pl.pallas_call(functools.partial(backward_kernel, (*ins, *outs, *scratch)...  150 us
    pallas_call x1, Pallas kernels, forward_attention(): pl.pallas_call(forward_attention_kernel, name='forward_attention', out_sh...  75.3 us
    pallas_call x1, Pallas kernels, update(): pl.pallas_call(functools.partial(update_kernel, (*ins, *outs, 'held', 'se...  9.54 us

profile of v3, /device:TPU:0, one launch (start us, length us, event | category | flops | bytes accessed | tf_op | source)
XLA Modules:
  0.0 239.0 jit_solution(13259258031583529371)
XLA Ops:
  0.7 75.3 %forward_attention.1 = (bf16[4,2,128,192]{3,2,1,0:T(8,128)(2,1)}, bf16[4,768,1792]{2,1,0:T(8,128)(2,1)}, bf16[1024,768]{1,0:T(8,128)(2,1)}, bf16[3,768,192]{2,1,...) custom-call(s32[2]{0:T(128)} %refs_0_.2, ...), custom_call_target="tpu_custom_call" | custom-call | tf_op jit(solution)/shard_map/forward_attention/pallas_call | solution.py:707
  75.9 0.0 copy-start
  75.9 0.0 copy-start.1
  75.9 0.0 copy-start.2
  76.0 0.0 copy-start.3
  76.0 0.0 copy-start.4
  76.0 0.0 copy-start.6
  76.0 0.0 copy-start.7
  76.0 0.0 copy-start.9
  76.0 0.0 copy-start.10
  76.0 0.0 copy-start.11
  76.0 0.0 copy-start.12
  76.1 150.0 %backward.1 = (bf16[2,512,768]{2,1,0:T(8,128)(2,1)}, bf16[2,512,768]{2,1,0:T(8,128)(2,1)}, bf16[192,1792]{1,0:T(8,128)(2,1)}, f32[3,192,192]{2,1,0:T(8,128)}, f32[8,768]{1,0:T(8,128)}, /*index=5*/f32[8,128]{1,0:T(8,128)}) custom-call(s32[2]{0:T(128)} %refs_0_.2, f32[8,128]{1,0:T(8,128)} %get-tuple-element.57.refs_1_.refs_7_, ...), custom_call_target="tpu_custom_call" | custom-call | tf_op jit(solution)/shard_map/backward/pallas_call | solution.py:1342
  226.7 0.0 copy-done
  226.7 0.0 copy-done.1
  226.7 0.0 copy-done.2
  226.7 0.0 copy-done.3
  226.7 0.0 copy-done.4
  226.7 0.0 copy-done.6
  226.7 0.0 copy-done.7
  226.8 0.0 copy-done.9
  226.8 0.0 copy-done.10
  226.8 0.0 copy-done.11
  226.8 0.0 copy-done.12
  226.8 0.0 copy-start.5
  226.8 1.1 copy-done.5
  227.9 0.0 copy-start.8
  227.9 0.7 copy-done.8
  228.6 0.0 copy-start.13
  228.6 0.7 copy-done.13
  229.3 9.5 %update.1 = (bf16[2,512,768]{2,1,0:T(8,128)(2,1)}, f32[1,1]{1,0:T(1,128)}, f32[2,512,768]{2,1,0:T(8,128)}, f32[1,1]{1,0:T(1,128)}, f32[3,192,192]{2,1,0:T(8,128)...) custom-call(s32[1]{0:T(128)S(6)} %copy.40.refs_0_, ...), custom_call_target="tpu_custom_call" | custom-call | tf_op jit(solution)/shard_map/update/pallas_call | solution.py:1430
Async XLA Ops:
  75.9 150.8 %copy-start = (f32[3,192,192]{2,1,0:T(8,128)S(1)}, f32[3,192,192]{2,1,0:T(8,128)}, u32[]{:S(2)}) copy-start(f32[3,192,192]{2,1,0:T(8,128)} %refs_8_.1) | copy-start | bytes 1327108
  75.9 150.8 %copy-start.1 = (f32[192,768]{1,0:T(8,128)S(1)}, f32[192,768]{1,0:T(8,128)}, u32[]{:S(2)}) copy-start(f32[192,768]{1,0:T(8,128)} %refs_14_.1) | copy-start | bytes 1769476
  75.9 150.8 %copy-start.2 = (f32[192,192]{1,0:T(8,128)S(1)}, f32[192,192]{1,0:T(8,128)}, u32[]{:S(2)}) copy-start(f32[192,192]{1,0:T(8,128)} %refs_11_.1) | copy-start | bytes 442372
  76.0 150.8 %copy-start.3 = (f32[3,192,192]{2,1,0:T(8,128)S(1)}, f32[3,192,192]{2,1,0:T(8,128)}, u32[]{:S(2)}) copy-start(f32[3,192,192]{2,1,0:T(8,128)} %refs_9_.1) | copy-start | bytes 1327108
  76.0 150.8 %copy-start.4 = (f32[3,192,192]{2,1,0:T(8,128)S(1)}, f32[3,192,192]{2,1,0:T(8,128)}, u32[]{:S(2)}) copy-start(f32[3,192,192]{2,1,0:T(8,128)} %refs_10_.1) | copy-start | bytes 1327108
  76.0 150.8 %copy-start.6 = (f32[192,192]{1,0:T(8,128)S(1)}, f32[192,192]{1,0:T(8,128)}, u32[]{:S(2)}) copy-start(f32[192,192]{1,0:T(8,128)} %refs_12_.1) | copy-start | bytes 442372
  76.0 150.8 %copy-start.7 = (f32[192,192]{1,0:T(8,128)S(1)}, f32[192,192]{1,0:T(8,128)}, u32[]{:S(2)}) copy-start(f32[192,192]{1,0:T(8,128)} %refs_13_.1) | copy-start | bytes 442372
  76.0 150.8 %copy-start.9 = (f32[8,128]{1,0:T(8,128)S(1)}, f32[8,128]{1,0:T(8,128)}, u32[]{:S(2)}) copy-start(f32[8,128]{1,0:T(8,128)} %get-tuple-element.57.refs_1_.refs_7_) | copy-start | bytes 12292
  76.0 150.8 %copy-start.10 = (f32[4,192]{1,0:T(4,128)S(1)}, f32[4,192]{1,0:T(4,128)}, u32[]{:S(2)}) copy-start(f32[4,192]{1,0:T(4,128)} %refs_20_.1) | copy-start | bytes 9220
  76.0 150.7 %copy-start.11 = (f32[4,192]{1,0:T(4,128)S(1)}, f32[4,192]{1,0:T(4,128)}, u32[]{:S(2)}) copy-start(f32[4,192]{1,0:T(4,128)} %refs_21_.1) | copy-start | bytes 9220
  76.0 150.7 %copy-start.12 = (f32[4,192]{1,0:T(4,128)S(1)}, f32[4,192]{1,0:T(4,128)}, u32[]{:S(2)}) copy-start(f32[4,192]{1,0:T(4,128)} %refs_22_.1) | copy-start | bytes 9220
  226.8 1.1 copy-start.5
  227.9 0.7 copy-start.8
  228.6 0.7 copy-start.13

commit v4 on v3

--- a/solution.py
+++ b/solution.py
@@ -392,80 +392,125 @@
         pl.semaphore_wait(sem, len(devs))
 
 
-def forward_attention_kernel(
-    lengths_ref,
-    tokens_ref,
-    teacher_ref,
-    qkv_ref,
-    up_ref,
-    down_ref,
-    out_ref,
-    norm_ref,
-    blocks_ref,
-    valid_ref,
-    att_ref,
-    u_ref,
-    t_ref,
-    w_ref,
-    q_ref,
-    k_ref,
-    v_ref,
-    kt_ref,
-    pt_ref,
-    tok_ref,
-    teach_ref,
-    live_ref,
-    count_ref,
-    upack_ref,
-    qkvb_ref,
-    rbt_ref,
-    mask_ref,
-    tally,
-    vt,
-    bias,
-    rb,
-    att_out,
-    att_tok,
-    loc_sem,
-    w_sem,
-    y_sem,
-    z_send,
-    z_recv,
-    x_send,
-    x_recv,
-    yw_send,
-    yw_recv,
-    c_send,
-    c_recv,
-    h_send,
-    h_recv,
-    a_send,
-    a_recv,
-    n_sem,
-):
+def column(row):
+    return row.T[:, 0:1]
+
+
+def add_rows(dst, a, b, step=16):
+    if len(dst.shape) == 3:
+        for i in range(dst.shape[0]):
+            add_rows(dst.at[i], a.at[i], b.at[i], step)
+        return
+
+    def one(i, carry):
+        rows = pl.ds(pl.multiple_of(i * step, step), step)
+        dst[rows, :] = a[rows, :] + b[rows, :]
+        return carry
+
+    lax.fori_loop(0, dst.shape[0] // step, one, 0)
+
+
+class Line:
+    def __init__(self, me, go, block, send, recv):
+        self.me, self.go, self.block, self.send, self.recv = me, go, block, send, recv
+
+    def first(self, src=None):
+        t = self.me.t
+        mine = self.block(t)
+        src = mine if src is None else src
+        return [
+            (remote(src, mine, self.send.at[0, t], self.recv.at[t], self.me.z(t + 1)), t < 3),
+            (remote(src, mine, self.send.at[1, t], self.recv.at[t], self.me.z(t - 1)), t > 0),
+        ]
+
+    def start(self, src=None):
+        for copy, pred in self.first(src):
+            self.go(copy, pred)
+
+    def step(self, d):
+        t = self.me.t
+        for tt, ok, on, nxt, way in ((t - d, t - d >= 0, t < 3, t + 1, 0), (t + d, t + d <= 3, t > 0, t - 1, 1)):
+            piece = self.block(tt)
+            pl.when(ok)(remote(piece, piece, self.send.at[way, tt], self.recv.at[tt], self.me.z(t)).wait_recv)
+            if d < 3:
+                self.go(remote(piece, piece, self.send.at[way, tt], self.recv.at[tt], self.me.z(nxt)), ok & on)
+
+
+class Chain:
+    def __init__(self, me, go, own, left, right, send, recv_l, recv_r):
+        self.me, self.go, self.own, self.left, self.right = me, go, own, left, right
+        self.send, self.recv_l, self.recv_r = send, recv_l, recv_r
+
+    def arrived(self, tt, way):
+        buf, recv = (self.left, self.recv_l) if way == 0 else (self.right, self.recv_r)
+        remote(buf(tt), buf(tt), self.send.at[tt], recv.at[tt], self.me.z(self.me.t)).wait_recv()
+
+    def pass_on(self, tt, way):
+        t = self.me.t
+        inner = (t > 0) if way == 0 else (t < 3)
+        ahead = (tt > t) if way == 0 else (tt < t)
+        buf, recv = (self.left, self.recv_l) if way == 0 else (self.right, self.recv_r)
+
+        @pl.when(ahead & inner)
+        def _():
+            self.arrived(tt, way)
+            add_rows(self.own(tt), self.own(tt), buf(tt))
+
+        to = self.me.z(t + 1 if way == 0 else t - 1)
+        self.go(remote(self.own(tt), buf(tt), self.send.at[tt], recv.at[tt], to), ahead)
+
+    def end(self):
+        t = self.me.t
+        mine = self.own(t)
+
+        @pl.when(t > 0)
+        def _():
+            self.arrived(t, 0)
+            add_rows(mine, mine, self.left(t))
+
+        @pl.when(t < 3)
+        def _():
+            self.arrived(t, 1)
+            add_rows(mine, mine, self.right(t))
+
+
+CHAIN_ORDER = ((3, 0), (0, 1), (2, 0), (1, 1), (1, 0), (2, 1))
+
+
+TAIL = None
+FF_COLS = 1536
+
+
+def train_kernel(names, *refs):
+    r = types.SimpleNamespace(**dict(zip(names, refs, strict=True)))
     me = Peers()
     f, c, t = me.f, me.c, me.t
-    seq = t_ref.shape[0]
+    seq = r.t_v.shape[0]
     half = seq // 2
-    rows_f = qkvb_ref.shape[1]
+    rows_f = r.qkvb.shape[1]
     sends = []
-    qkvb_ref[...] = qkv_ref[...].astype(bf16)
-    upack_ref[:, 0:768] = up_ref[...].astype(bf16)
-    upack_ref[:, 768:1536] = down_ref[...].astype(bf16)
+    heads = r.q_v.shape[0]
+    width = heads * HD
+    depth = rows_f * 4
+    hrows = rows_f // 2
+    qrows = rows_f // 4
+    r.qkvb[...] = r.qkv[...].astype(bf16)
+    r.upack[:, 0:768] = r.up[...].astype(bf16)
+    r.upack[:, 768:1536] = r.down[...].astype(bf16)
     tail = jnp.concatenate(
-        [out_ref[...].T, jnp.concatenate([norm_ref[...], jnp.zeros((60, rows_f), f32)], 0).T], 1
-    )
-    upack_ref[:, 1536:1792] = tail.astype(bf16)
+        [r.out[...].T, jnp.concatenate([r.norm[...], jnp.zeros((60, rows_f), f32)], 0).T], 1
+    )
+    r.upack[:, 1536:1792] = tail.astype(bf16)
     for s in range(2):
-        rbt_ref[s] = jnp.zeros((8, 128), f32)
-        rbt_ref[s, 0:3, 0 : blocks_ref.shape[2]] = blocks_ref[:, s, :].astype(f32)
-        mask_ref[s] = jnp.broadcast_to(valid_ref[s : s + 1, :].astype(f32), (8, half))
+        r.rbt[s] = jnp.zeros((8, 128), f32)
+        r.rbt[s, 0:3, 0 : r.blocks.shape[2]] = r.blocks[:, s, :].astype(f32)
+        r.mask[s] = jnp.broadcast_to(r.valid[s : s + 1, :].astype(f32), (8, half))
     spot = c * half + lax.broadcasted_iota(jnp.int32, (1, half), 1)
     found = jnp.zeros((1, half), f32)
     for s in range(2):
-        found += jnp.where((valid_ref[s : s + 1, :] == 1) & (spot < lengths_ref[s]), 1.0, 0.0)
-    count_ref[...] = jnp.broadcast_to(jnp.sum(found, 1, keepdims=True), (8, 128))
-    me.barrier()
+        found += jnp.where((r.valid[s : s + 1, :] == 1) & (spot < r.lengths[s]), 1.0, 0.0)
+    r.count[...] = jnp.broadcast_to(jnp.sum(found, 1, keepdims=True), (8, 128))
+    me.barrier(True)
 
     def go(copy, pred=None):
         if pred is None:
@@ -474,69 +519,73 @@
             pl.when(pred)(copy.start)
         sends.append((copy, pred))
     own_rows = pl.ds(pl.multiple_of(c * half, half), half)
-    go(remote(tokens_ref.at[1 - c], t_ref.at[own_rows], y_sem.at[0], y_sem.at[1], me.ydev))
-    go(remote(rbt_ref.at[1 - c], rb.at[c], y_sem.at[2], y_sem.at[3], me.ydev))
-    go(remote(mask_ref.at[1 - c], live_ref.at[c], y_sem.at[4], y_sem.at[5], me.ydev))
+    go(remote(r.tokens.at[1 - c], r.t_v.at[own_rows], r.y_sem.at[0], r.y_sem.at[1], me.ydev))
+    go(remote(r.rbt.at[1 - c], r.rb.at[c], r.y_sem.at[2], r.y_sem.at[3], me.ydev))
+    go(remote(r.mask.at[1 - c], r.live.at[c], r.y_sem.at[4], r.y_sem.at[5], me.ydev))
     part = pl.ds(pl.multiple_of(t * 128, 128), 128)
-    go(remote(teacher_ref.at[1 - c, part], teach_ref.at[c], y_sem.at[6], y_sem.at[7], me.ydev))
+    go(remote(r.teacher.at[1 - c, part], r.teach.at[c], r.y_sem.at[6], r.y_sem.at[7], me.ydev))
 
     def wblock(ff):
-        return w_ref.at[:, pl.ds(pl.multiple_of(ff * rows_f, rows_f), rows_f), :]
-
-    go(remote(qkvb_ref, wblock(f), w_sem.at[0], w_sem.at[1], me.xdev))
-    go(remote(qkvb_ref, wblock(f), w_sem.at[2], w_sem.at[3], me.core))
-
-    def shard(tt, ff):
-        return u_ref.at[tt, pl.ds(pl.multiple_of(ff * rows_f, rows_f), rows_f), :]
-
-    hrows = rows_f // 2
-
-    def slab(tt, ff, h):
-        return u_ref.at[tt, pl.ds(pl.multiple_of(ff * rows_f + h * hrows, hrows), hrows), :]
-
-    def own_half(h):
-        return upack_ref.at[pl.ds(pl.multiple_of(h * hrows, hrows), hrows), :]
+        return r.w_v.at[:, pl.ds(pl.multiple_of(ff * rows_f, rows_f), rows_f), :]
+
+    go(remote(r.qkvb, wblock(f), r.w_sem.at[0], r.w_sem.at[1], me.xdev))
+    go(remote(r.qkvb, wblock(f), r.w_sem.at[2], r.w_sem.at[3], me.core))
+
+    def cols(u):
+        return slice(FF_COLS, UW) if u == 0 else slice(0, FF_COLS)
+
+    def shard(tt, ff, u):
+        return r.u_v.at[tt, pl.ds(pl.multiple_of(ff * rows_f, rows_f), rows_f), cols(u)]
+
+    def slab(tt, ff, h, u):
+        return r.u_v.at[tt, pl.ds(pl.multiple_of(ff * rows_f + h * hrows, hrows), hrows), cols(u)]
+
+    def own_half(h, u):
+        return r.upack.at[pl.ds(pl.multiple_of(h * hrows, hrows), hrows), cols(u)]
 
     hs = (c, 1 - c)
-    go(remote(own_half(c), slab(t, f, c), x_send.at[t], x_recv.at[t], me.xdev))
-    for i in (0, 1):
-        go(remote(own_half(hs[i]), slab(t, f, hs[i]), z_send.at[0, t, i], z_recv.at[t, i], me.z(t + 1)), t < 3)
-        go(remote(own_half(hs[i]), slab(t, f, hs[i]), z_send.at[1, t, i], z_recv.at[t, i], me.z(t - 1)), t > 0)
-    go(remote(upack_ref, shard(t, f), c_send.at[t], c_recv.at[t], me.core))
+    for u in (0, 1):
+        go(remote(own_half(c, u), slab(t, f, c, u), r.x_send.at[u, t], r.x_recv.at[u, t], me.xdev))
+        for i in (0, 1):
+            mine, there = own_half(hs[i], u), slab(t, f, hs[i], u)
+            go(remote(mine, there, r.z_send.at[u, 0, t, i], r.z_recv.at[u, t, i], me.z(t + 1)), t < 3)
+            go(remote(mine, there, r.z_send.at[u, 1, t, i], r.z_recv.at[u, t, i], me.z(t - 1)), t > 0)
+        go(remote(r.upack.at[:, cols(u)], shard(t, f, u), r.c_send.at[u, t], r.c_recv.at[u, t], me.core))
 
     local = [
-        pltpu.make_async_copy(tokens_ref.at[c], t_ref.at[own_rows], loc_sem.at[0]),
-        pltpu.make_async_copy(qkvb_ref, wblock(f), loc_sem.at[1]),
-        pltpu.make_async_copy(upack_ref, shard(t, f), loc_sem.at[2]),
-        pltpu.make_async_copy(teacher_ref.at[c, part], teach_ref.at[c], loc_sem.at[3]),
+        pltpu.make_async_copy(r.tokens.at[c], r.t_v.at[own_rows], r.loc_sem.at[0]),
+        pltpu.make_async_copy(r.qkvb, wblock(f), r.loc_sem.at[1]),
+        pltpu.make_async_copy(r.upack, r.u_v.at[t, pl.ds(pl.multiple_of(f * rows_f, rows_f), rows_f), :], r.loc_sem.at[2]),
+        pltpu.make_async_copy(r.teacher.at[c, part], r.teach.at[c], r.loc_sem.at[3]),
     ]
     for copy in local:
         copy.start()
-    rb[c] = rbt_ref[c]
-    live_ref[c] = mask_ref[c]
+    r.rb[c] = r.rbt[c]
+    r.live[c] = r.mask[c]
 
     peers = (me.core, me.xdev, me.ydev)
 
     def tally_send(i):
-        go(remote(count_ref if i == 0 else tally.at[i + 2], tally.at[i], n_sem.at[0, i], n_sem.at[1, i], peers[i]))
+        go(remote(r.count if i == 0 else r.tally.at[i + 2], r.tally.at[i], r.n_sem.at[0, i], r.n_sem.at[1, i], peers[i]))
 
     def tally_take(i):
-        remote(tally.at[i], tally.at[i], n_sem.at[0, i], n_sem.at[1, i], peers[i]).wait_recv()
-        tally[3 + i] = (count_ref[...] if i == 0 else tally[i + 2]) + tally[i]
+        remote(r.tally.at[i], r.tally.at[i], r.n_sem.at[0, i], r.n_sem.at[1, i], peers[i]).wait_recv()
+        r.tally[3 + i] = (r.count[...] if i == 0 else r.tally[i + 2]) + r.tally[i]
 
     tally_send(0)
 
-    def z_step(d):
+    def z_step(d, u):
         for tt, ok, on, nxt, way in ((t - d, t - d >= 0, t < 3, t + 1, 0), (t + d, t + d <= 3, t > 0, t - 1, 1)):
             go_on = ok & on
             for i in (0, 1):
-                piece = slab(tt, f, hs[i])
-                arrived = remote(piece, piece, z_send.at[way, tt, i], z_recv.at[tt, i], me.z(t))
-                pl.when(ok)(arrived.wait_recv)
-                go(remote(piece, piece, z_send.at[way, tt, i], z_recv.at[tt, i], me.z(nxt)), go_on)
+                piece = slab(tt, f, hs[i], u)
+                send, recv = r.z_send.at[u, way, tt, i], r.z_recv.at[u, tt, i]
+                pl.when(ok)(remote(piece, piece, send, recv, me.z(t)).wait_recv)
+                go(remote(piece, piece, send, recv, me.z(nxt)), go_on)
                 if i == 0:
-                    go(remote(piece, piece, x_send.at[tt], x_recv.at[tt], me.xdev), ok)
-            go(remote(shard(tt, f), shard(tt, f), c_send.at[tt], c_recv.at[tt], me.core), ok)
+                    go(remote(piece, piece, r.x_send.at[u, tt], r.x_recv.at[u, tt], me.xdev), ok)
+            whole = shard(tt, f, u)
+            go(remote(whole, whole, r.c_send.at[u, tt], r.c_recv.at[u, tt], me.core), ok)
 
     def around(d):
         return ((t, None),) if d == 0 else ((t - d, t - d >= 0), (t + d, t + d <= 3))
@@ -547,58 +596,69 @@
         else:
             pl.when(ok)(fn)
 
-    def x_step(d):
+    def x_step(d, u):
         for tt, ok in around(d):
-            piece = slab(tt, me.f_x, c)
-            when(ok, remote(piece, piece, x_send.at[tt], x_recv.at[tt], me.xdev).wait_recv)
-            go(remote(piece, piece, yw_send.at[tt], yw_recv.at[tt], me.ydev), ok)
-            go(remote(piece, piece, h_send.at[tt, 0], h_recv.at[tt, 0], me.core), ok)
-
-    def y_step(d):
+            piece = slab(tt, me.f_x, c, u)
+            when(ok, remote(piece, piece, r.x_send.at[u, tt], r.x_recv.at[u, tt], me.xdev).wait_recv)
+            go(remote(piece, piece, r.yw_send.at[u, tt], r.yw_recv.at[u, tt], me.ydev), ok)
+            go(remote(piece, piece, r.h_send.at[u, tt, 0], r.h_recv.at[u, tt, 0], me.core), ok)
+
+    def y_step(d, u):
         for tt, ok in around(d):
-            piece = slab(tt, me.f_x, 1 - c)
-            when(ok, remote(piece, piece, yw_send.at[tt], yw_recv.at[tt], me.ydev).wait_recv)
-            go(remote(piece, piece, h_send.at[tt, 1], h_recv.at[tt, 1], me.core), ok)
-    remote(wblock(me.f_x), wblock(me.f_x), w_sem.at[0], w_sem.at[1], me.xdev).wait_recv()
-    go(remote(wblock(me.f_x), wblock(me.f_x), w_sem.at[4], w_sem.at[5], me.core))
-    remote(wblock(me.f_core), wblock(me.f_core), w_sem.at[2], w_sem.at[3], me.core).wait_recv()
+            piece = slab(tt, me.f_x, 1 - c, u)
+            when(ok, remote(piece, piece, r.yw_send.at[u, tt], r.yw_recv.at[u, tt], me.ydev).wait_recv)
+            go(remote(piece, piece, r.h_send.at[u, tt, 1], r.h_recv.at[u, tt, 1], me.core), ok)
+
+    def core_wait(tt, u):
+        whole = shard(tt, me.f_core, u)
+        remote(whole, whole, r.c_send.at[u, tt], r.c_recv.at[u, tt], me.core).wait_recv()
+        for i in (0, 1):
+            piece = slab(tt, me.f_xc, hs[i], u)
+            remote(piece, piece, r.h_send.at[u, tt, i], r.h_recv.at[u, tt, i], me.core).wait_recv()
+
+    remote(wblock(me.f_x), wblock(me.f_x), r.w_sem.at[0], r.w_sem.at[1], me.xdev).wait_recv()
+    go(remote(wblock(me.f_x), wblock(me.f_x), r.w_sem.at[4], r.w_sem.at[5], me.core))
+    remote(wblock(me.f_core), wblock(me.f_core), r.w_sem.at[2], r.w_sem.at[3], me.core).wait_recv()
     for copy in local[:2]:
         copy.wait()
-    remote(wblock(me.f_xc), wblock(me.f_xc), w_sem.at[4], w_sem.at[5], me.core).wait_recv()
-
-    width = q_ref.shape[0] * HD
-    heads = q_ref.shape[0]
+    remote(wblock(me.f_xc), wblock(me.f_xc), r.w_sem.at[4], r.w_sem.at[5], me.core).wait_recv()
+
 
     def project(base, count):
         def step(i, carry):
             rows = pl.ds(pl.multiple_of(base + i * 256, 256), 256)
-            piece = t_ref[rows, :]
-            for j, ref in enumerate((q_ref, k_ref, v_ref)):
-                made = dot_nn(piece, w_ref[j])
+            piece = r.t_v[rows, :]
+            for j, ref in enumerate((r.q_v, r.k_v, r.v_v)):
+                made = dot_nn(piece, r.w_v[j])
                 for h in range(heads):
                     ref[h, rows, :] = made[:, h * HD : (h + 1) * HD].astype(bf16)
                 if j:
-                    (kt_ref if j == 1 else vt)[:, rows] = made.T.astype(bf16)
+                    (r.kt_v if j == 1 else r.vt)[:, rows] = made.T.astype(bf16)
             return carry
 
         lax.fori_loop(0, count, step, 0)
     tally_take(0)
     tally_send(1)
     project(c * half, half // 256)
+    x_step(0, 0)
+    z_step(1, 0)
+    x_step(0, 1)
+    z_step(1, 1)
+    x_step(1, 0)
+    z_step(2, 0)
+    y_step(0, 0)
     tally_take(1)
     tally_send(2)
-    x_step(0)
-    z_step(1)
     other_rows = pl.ds(pl.multiple_of((1 - c) * half, half), half)
-    remote(t_ref.at[other_rows], t_ref.at[other_rows], y_sem.at[0], y_sem.at[1], me.ydev).wait_recv()
+    remote(r.t_v.at[other_rows], r.t_v.at[other_rows], r.y_sem.at[0], r.y_sem.at[1], me.ydev).wait_recv()
     project((1 - c) * half, half // 256)
-    remote(rb.at[1 - c], rb.at[1 - c], y_sem.at[2], y_sem.at[3], me.ydev).wait_recv()
-    length = lengths_ref[c]
+    remote(r.rb.at[1 - c], r.rb.at[1 - c], r.y_sem.at[2], r.y_sem.at[3], me.ydev).wait_recv()
+    length = r.lengths[c]
     nblk = seq // BLK
     pos_block = lax.broadcasted_iota(jnp.int32, (128, seq), 1) // BLK
     row = lax.broadcasted_iota(jnp.int32, (128, seq), 0)
-    picks = dot_nn(rb[0].astype(bf16), (pos_block == row).astype(bf16)) + dot_nn(
-        rb[1].astype(bf16), (pos_block == row + nblk // 2).astype(bf16)
+    picks = dot_nn(r.rb[0].astype(bf16), (pos_block == row).astype(bf16)) + dot_nn(
+        r.rb[1].astype(bf16), (pos_block == row + nblk // 2).astype(bf16)
     )
     key_block = lax.broadcasted_iota(jnp.int32, (nblk, seq), 0)
     query = lax.broadcasted_iota(jnp.int32, (nblk, seq), 1)
@@ -613,256 +673,72 @@
         times += same(key_block.astype(f32), picks[j : j + 1, :])
     times = jnp.where(query < 2 * BLK, 1.0, times)
     level = jnp.where(times > 0, jnp.log2(jnp.maximum(times, 1.0)), negative)
-    for b in range(nblk):
-        place = b * BLK + lax.broadcasted_iota(jnp.int32, (BLK, seq), 0)
-        bias[b * BLK : (b + 1) * BLK, :] = jnp.where(
-            place < length, jnp.broadcast_to(level[b : b + 1, :], (BLK, seq)), negative
-        )
-
+    r.level[...] = level
     factor = HD ** (-0.5) * 1.4426950408889634
     wide = 256
 
-    def attend(h):
-        def step(i, carry):
-            cols = pl.ds(pl.multiple_of(i * wide, wide), wide)
-            scores = dot_nt(k_ref[h], q_ref[h, cols, :]) * factor + bias[:, cols]
+    def attend(i):
+        cols = slice(i * wide, (i + 1) * wide)
+        for b in range(nblk):
+            place = b * BLK + lax.broadcasted_iota(jnp.int32, (BLK, wide), 0)
+            row = jnp.broadcast_to(r.level[b : b + 1, cols], (BLK, wide))
+            r.bias[b * BLK : (b + 1) * BLK, :] = jnp.where(place < length, row, negative)
+
+        def step(h, carry):
+            scores = dot_nt(r.k_v[h], r.q_v[h, cols, :]) * factor + r.bias[...]
             top = jnp.max(scores, 0, keepdims=True)
             expo = jnp.exp2(scores - top)
             probs = (expo * (1.0 / jnp.sum(expo, 0, keepdims=True))).astype(bf16)
-            pt_ref[h, :, cols] = probs
-            att_out[h * HD : (h + 1) * HD, cols] = dot_nn(vt[h * HD : (h + 1) * HD, :], probs)
+            r.pt_v[h, :, cols] = probs
+            rows = pl.ds(pl.multiple_of(h * HD, HD), HD)
+            r.dqt[rows, cols] = dot_nn(r.vt[rows, :], probs)
             return carry
 
-        lax.fori_loop(0, seq // wide, step, 0)
+        lax.fori_loop(0, heads, step, 0)
+        s = i * wide // half
+        for tt in range(i * wide % half // 128, i * wide % half // 128 + 2):
+            at = s * half + tt * 128
+            made = r.dqt[:, at : at + 128].T.astype(bf16)
+            r.gatt[tt, s] = made
+
+            @pl.when(t == tt)
+            def _():
+                r.att_v[tt, s] = made
+
+            go(remote(r.gatt.at[tt, s], r.att_v.at[t, s], r.o_send.at[s, tt], r.o_recv.at[s, t], me.z(tt)), t != tt)
+
     attend(0)
-    x_step(1)
-    z_step(2)
+    x_step(1, 1)
+    z_step(2, 1)
+    z_step(3, 0)
+    x_step(2, 0)
+    y_step(1, 0)
     attend(1)
-    y_step(0)
+    y_step(0, 1)
+    x_step(3, 0)
+    y_step(2, 0)
     attend(2)
+    y_step(3, 0)
+    attend(3)
+    y_step(1, 1)
+    x_step(2, 1)
+    z_step(3, 1)
     for s in range(2):
-        for tt in range(4):
-            at = s * half + tt * 128
-            tok_at = att_out[:, at : at + 128].T.astype(bf16)
-            att_tok[s, tt] = tok_at
-    for d in (1, 2, 3):
-        to = (t + d) % 4
-        go(remote(att_tok.at[:, to], att_ref.at[t], a_send.at[d], a_recv.at[d], me.z(to)))
-    own_copy = pltpu.make_async_copy(att_tok.at[:, t], att_ref.at[t], loc_sem.at[4])
-    own_copy.start()
-    y_step(1)
-    x_step(2)
-    z_step(3)
-    y_step(2)
-    x_step(3)
-    y_step(3)
+        r.tok[s] = r.t_v[pl.ds(pl.multiple_of(s * half + t * 128, 128), 128), :]
     for s in range(2):
-        tok_ref[s] = t_ref[pl.ds(pl.multiple_of(s * half + t * 128, 128), 128), :]
-    for d in (1, 2, 3):
-        src = (t + 4 - d) % 4
-        remote(att_ref.at[src], att_ref.at[src], a_send.at[d], a_recv.at[d], me.z(src)).wait_recv()
-    for tt in range(4):
-        whole = shard(tt, me.f_core)
-        remote(whole, whole, c_send.at[tt], c_recv.at[tt], me.core).wait_recv()
-        for i in (0, 1):
-            piece = slab(tt, me.f_xc, hs[i])
-            remote(piece, piece, h_send.at[tt, i], h_recv.at[tt, i], me.core).wait_recv()
-    there = live_ref.at[1 - c]
-    remote(there, there, y_sem.at[4], y_sem.at[5], me.ydev).wait_recv()
-    there = teach_ref.at[1 - c]
-    remote(there, there, y_sem.at[6], y_sem.at[7], me.ydev).wait_recv()
+        for d in (1, 2, 3):
+            src = (t + d) % 4
+            piece = r.att_v.at[src, s]
+            remote(piece, piece, r.o_send.at[s, t], r.o_recv.at[s, src], me.z(t)).wait_recv()
     for copy in local[2:]:
         copy.wait()
-    own_copy.wait()
-    tally_take(2)
-    for copy, pred in sends:
-        when(pred, copy.wait_send)
-    count_ref[...] = tally[5]
-
-
-def forward_attention(lengths, tokens, teacher, qkv, up, down, out, norm, blocks, valid):
-    seq = tokens.shape[1] * 2
-    heads = qkv.shape[2] // HD
-    width = heads * HD
-    rows_f = qkv.shape[1]
-    depth = rows_f * 4
-    vm = pl.BlockSpec(memory_space=pltpu.VMEM)
-    hbm = pl.BlockSpec(memory_space=pl.ANY)
-    dma = pltpu.SemaphoreType.DMA
-    outs = [
-        ((4, 2, 128, width), bf16, vm),
-        ((4, depth, UW), bf16, hbm),
-        ((seq, depth), bf16, vm),
-        ((3, depth, width), bf16, vm),
-        ((heads, seq, HD), bf16, vm),
-        ((heads, seq, HD), bf16, vm),
-        ((heads, seq, HD), bf16, vm),
-        ((width, seq), bf16, vm),
-        ((heads, seq, seq), bf16, vm),
-        ((2, 128, depth), bf16, vm),
-        ((2, 128, depth), bf16, vm),
-        ((2, 8, seq // 2), f32, vm),
-        ((8, 128), f32, vm),
-    ]
-    return pl.pallas_call(
-        forward_attention_kernel,
-        name="forward_attention",
-        out_shape=[jax.ShapeDtypeStruct(s, d) for s, d, _ in outs],
-        in_specs=[pl.BlockSpec(memory_space=pltpu.SMEM), hbm, hbm, *[vm] * 7],
-        out_specs=[m for _, _, m in outs],
-        scratch_shapes=[
-            pltpu.VMEM((rows_f, UW), bf16),
-            pltpu.VMEM(qkv.shape, bf16),
-            pltpu.VMEM((2, 8, 128), f32),
-            pltpu.VMEM((2, 8, seq // 2), f32),
-            pltpu.VMEM((6, 8, 128), f32),
-            pltpu.VMEM((width, seq), bf16),
-            pltpu.VMEM((seq, seq), f32),
-            pltpu.VMEM((2, 8, 128), f32),
-            pltpu.VMEM((width, seq), f32),
-            pltpu.VMEM((2, 4, 128, width), bf16),
-            dma((5,)),
-            dma((6,)),
-            dma((8,)),
-            dma((2, 4, 2)),
-            dma((4, 2)),
-            dma((4,)),
-            dma((4,)),
-            dma((4,)),
-            dma((4,)),
-            dma((4,)),
-            dma((4,)),
-            dma((4, 2)),
-            dma((4, 2)),
-            dma((4,)),
-            dma((4,)),
-            dma((2, 3)),
-        ],
-        compiler_params=pltpu.CompilerParams(
-            collective_id=0, has_side_effects=True, vmem_limit_bytes=VMEM_LIMIT
-        ),
-    )(lengths, tokens, teacher, qkv, up, down, out, norm, blocks, valid)
-
-
-def column(row):
-    return row.T[:, 0:1]
-
-
-def add_rows(dst, a, b, step=16):
-    if len(dst.shape) == 3:
-        for i in range(dst.shape[0]):
-            add_rows(dst.at[i], a.at[i], b.at[i], step)
-        return
-
-    def one(i, carry):
-        rows = pl.ds(pl.multiple_of(i * step, step), step)
-        dst[rows, :] = a[rows, :] + b[rows, :]
-        return carry
-
-    lax.fori_loop(0, dst.shape[0] // step, one, 0)
-
-
-class Line:
-    def __init__(self, me, go, block, send, recv):
-        self.me, self.go, self.block, self.send, self.recv = me, go, block, send, recv
-
-    def start(self):
-        t = self.me.t
-        mine = self.block(t)
-        self.go(remote(mine, mine, self.send.at[0, t], self.recv.at[t], self.me.z(t + 1)), t < 3)
-        self.go(remote(mine, mine, self.send.at[1, t], self.recv.at[t], self.me.z(t - 1)), t > 0)
-
-    def step(self, d):
-        t = self.me.t
-        for tt, ok, on, nxt, way in ((t - d, t - d >= 0, t < 3, t + 1, 0), (t + d, t + d <= 3, t > 0, t - 1, 1)):
-            piece = self.block(tt)
-            pl.when(ok)(remote(piece, piece, self.send.at[way, tt], self.recv.at[tt], self.me.z(t)).wait_recv)
-            if d < 3:
-                self.go(remote(piece, piece, self.send.at[way, tt], self.recv.at[tt], self.me.z(nxt)), ok & on)
-
-
-class Chain:
-    def __init__(self, me, go, own, left, right, send, recv_l, recv_r):
-        self.me, self.go, self.own, self.left, self.right = me, go, own, left, right
-        self.send, self.recv_l, self.recv_r = send, recv_l, recv_r
-
-    def arrived(self, tt, way):
-        buf, recv = (self.left, self.recv_l) if way == 0 else (self.right, self.recv_r)
-        remote(buf(tt), buf(tt), self.send.at[tt], recv.at[tt], self.me.z(self.me.t)).wait_recv()
-
-    def pass_on(self, tt, way):
-        t = self.me.t
-        inner = (t > 0) if way == 0 else (t < 3)
-        ahead = (tt > t) if way == 0 else (tt < t)
-        buf, recv = (self.left, self.recv_l) if way == 0 else (self.right, self.recv_r)
-
-        @pl.when(ahead & inner)
-        def _():
-            self.arrived(tt, way)
-            add_rows(self.own(tt), self.own(tt), buf(tt))
-
-        to = self.me.z(t + 1 if way == 0 else t - 1)
-        self.go(remote(self.own(tt), buf(tt), self.send.at[tt], recv.at[tt], to), ahead)
-
-    def end(self):
-        t = self.me.t
-        mine = self.own(t)
-
-        @pl.when(t > 0)
-        def _():
-            self.arrived(t, 0)
-            add_rows(mine, mine, self.left(t))
-
-        @pl.when(t < 3)
-        def _():
-            self.arrived(t, 1)
-            add_rows(mine, mine, self.right(t))
-
-
-CHAIN_ORDER = ((3, 0), (0, 1), (2, 0), (1, 1), (1, 0), (2, 1))
-
-
-TAIL = None
-FF_COLS = 1536
-
-
-def backward_kernel(names, *refs):
-    r = types.SimpleNamespace(**dict(zip(names, refs, strict=True)))
-    me = Peers()
-    f, c, t = me.f, me.c, me.t
+    for tt in range(4):
+        core_wait(tt, 0)
+
     x = f // 2
     k = f % 2
-    depth = r.u.shape[1]
-    rows_f = depth // 4
-    hrows = rows_f // 2
-    qrows = rows_f // 4
-    seq = r.t.shape[0]
-    half = seq // 2
-    heads = r.q.shape[0]
-    width = heads * HD
-    sends = []
-
-    def when(ok, fn):
-        if ok is None:
-            fn()
-        else:
-            pl.when(ok)(fn)
-
-    def go(copy, pred=None):
-        when(pred, copy.start)
-        sends.append((copy, pred))
-
-    def load(i, src, dst):
-        copy = pltpu.make_async_copy(src, dst, r.load_sem.at[i])
-        copy.start()
-        return copy
-
-    first = [load(0, r.att, r.att_v), *(load(1 + j, r.u.at[j], r.u_v.at[j]) for j in range(4))]
-    me.barrier(True)
-
     att_v, u_v, g_v, act, slope = r.att_v, r.u_v, r.g_v, r.act, r.slope
     rows = 2 * 128
-    length = r.lengths[c]
     inv_width = 1.0 / depth
 
     def both(ref):
@@ -879,10 +755,6 @@
     def back(up, normed, inverse, gain):
         scaled = up * gain
         return inverse * (scaled - mean(scaled) - normed * mean(scaled * normed))
-    for copy in first:
-        copy.wait()
-    pairs = ((r.pt, r.pt_v), (r.q, r.q_v), (r.k, r.k_v), (r.v, r.v_v), (r.kt, r.kt_v), (r.w, r.w_v), (r.t, r.t_v))
-    later = [load(5 + i, src, dst) for i, (src, dst) in enumerate(pairs)]
     norms = u_v[0, :, 1728:1736].astype(f32).T
     gains = [norms[i : i + 1, :] for i in range(4)]
     att = [att_v[tt].reshape(rows, width) for tt in range(4)]
@@ -904,15 +776,36 @@
         bend = 0.5 * (1.0 + th) + 0.5 * upper * (1.0 - th * th) * root * (1.0 + 3.0 * cube * square)
         slope[tt] = bend.astype(bf16)
         return mixed + dot_nt(act_t, u_v[tt, :, 768:1536])
-    mixed = lax.fori_loop(0, 4, up_step, jnp.zeros((rows, depth), f32))
+    second = t - 1 + 2 * ((3 - t) // 3)
+    fourth = 3 * (1 - t // 2)
+    x_step(3, 1)
+    core_wait(t, 1)
+    mixed = up_step(t, jnp.zeros((rows, depth), f32))
+    y_step(2, 1)
+    core_wait(second, 1)
+    mixed = up_step(second, mixed)
+    core_wait(6 - t - second - fourth, 1)
+    mixed = up_step(6 - t - second - fourth, mixed)
+    y_step(3, 1)
+    core_wait(fourth, 1)
+    mixed = up_step(fourth, mixed)
+    there = r.live.at[1 - c]
+    remote(there, there, r.y_sem.at[4], r.y_sem.at[5], me.ydev).wait_recv()
+    there = r.teach.at[1 - c]
+    remote(there, there, r.y_sem.at[6], r.y_sem.at[7], me.ydev).wait_recv()
+    tally_take(2)
+    for copy, pred in sends:
+        when(pred, copy.wait_send)
+    r.count[...] = r.tally[5]
+    sends.clear()
     normed_two, inverse_two = normalize(hidden + mixed)
     result = normed_two * gains[2] + gains[3]
 
     r.piece[...] = result.astype(bf16).reshape(2, 128, depth)
-    part = pl.ds(pl.multiple_of(t * 128, 128), 128)
     lo = r.lo
-    go(remote(r.piece.at[1 - c], lo.at[c, part], r.s_sem.at[0], r.s_sem.at[1], me.ydev))
-    own_lo = pltpu.make_async_copy(r.piece.at[c], lo.at[c, part], r.load_sem.at[12])
+    lo_send = remote(r.piece.at[1 - c], lo.at[c, part], r.s_sem.at[0], r.s_sem.at[1], me.ydev)
+    lo_send.start()
+    own_lo = pltpu.make_async_copy(r.piece.at[c], lo.at[c, part], r.load_sem.at[1])
     own_lo.start()
 
     def lo_block(tt):
@@ -936,15 +829,17 @@
     gm_t = grad_two.T.astype(bf16)
     hidden_t = hidden.T.astype(bf16)
     there = lo.at[1 - c, part]
-    remote(there, there, r.s_sem.at[0], r.s_sem.at[1], me.ydev).wait_recv()
-    own_lo.wait()
-    lo_line.start()
+    lo_there = remote(there, there, r.s_sem.at[0], r.s_sem.at[1], me.ydev)
+    lo_first = lo_line.first()
+    sends.extend(lo_first)
 
     far = 1 - x
     trio = (me.core, me.xdev, me.ydev)
 
-    def region(ref, unit, at, n):
+    def region(ref, unit, at, n, whole=None):
         rows_at = pl.ds(pl.multiple_of(at, qrows), n)
+        if whole is not None:
+            return ref.at[unit, rows_at, :]
         return ref.at[:, rows_at, FF_COLS:UW] if unit is TAIL else ref.at[unit, rows_at, 0:FF_COLS]
 
     def g_rows(unit, ff):
@@ -1030,11 +925,11 @@
             remote(yg, yg, r.yg_send.at[at, i], r.yg_recv.at[at, i], me.ydev).wait_recv()
             add_rows(mine, mine, yg)
 
-    def own_rows(tt):
+    def sum_rows(tt):
         return u_v.at[tt, pl.ds(pl.multiple_of(x * rows_f + c * hrows, hrows), hrows), :]
 
     w_chain = Chain(
-        me, go, own_rows, lambda tt: u_v.at[tt, pl.ds(6 * hrows, hrows), :],
+        me, go, sum_rows, lambda tt: u_v.at[tt, pl.ds(6 * hrows, hrows), :],
         lambda tt: u_v.at[tt, pl.ds(7 * hrows, hrows), :], r.zw_send, r.zw_recv_l, r.zw_recv_r,
     )
 
@@ -1051,6 +946,13 @@
         g_v[tt, :, 0:768] = dot_nn(hidden_t, gu).astype(bf16)
         total = total + dot_nt(gu, u_v[tt, :, 0:768])
         credit(tt)
+
+        @pl.when(i == 1)
+        def _():
+            lo_there.wait_recv()
+            own_lo.wait()
+            for copy, pred in lo_first:
+                when(pred, copy.start)
 
         @pl.when(i >= 1)
         def _():
@@ -1112,18 +1014,15 @@
     far_step(ORDER[3])
     near_step(ORDER[1])
     lo_line.step(1)
-    diag_step(ORDER[0])
     far_step(TAIL)
     near_step(ORDER[2])
     near_step(ORDER[3])
     near_step(TAIL)
     for unit in (*ORDER, TAIL):
         sends.extend((copy, None) for copy in rc_copies(unit) + far_copies(unit))
-    lo_line.step(2)
-
-    for copy in later:
-        copy.wait()
-    do, proj, dqt, dk, dv = r.do, r.proj, r.dqt, r.dk, r.dv
+
+    do, proj, dqt = r.do, r.proj, r.dqt
+    dk, dv = r.bias.at[:, 0:HD], r.bias.at[:, 128 : 128 + HD]
     for d in (1, 2, 3):
         src = (t + 4 - d) % 4
         remote(do_in.at[src], do_in.at[src], r.a_send.at[d], r.a_recv.at[d], me.z(src)).wait_recv()
@@ -1134,11 +1033,10 @@
                 do[h, at : at + 128, :] = do_in[tt, s, :, h * HD : (h + 1) * HD]
     q_v, k_v, v_v, kt_v, pt_v, t_v, w_v = (r.q_v, r.k_v, r.v_v, r.kt_v, r.pt_v, r.t_v, r.w_v)
     scale = HD ** (-0.5)
-    wide = 256
 
     def attend_back(h):
-        dk[...] = jnp.zeros_like(dk)
-        dv[...] = jnp.zeros_like(dv)
+        dk[...] = jnp.zeros((seq, HD), f32)
+        dv[...] = jnp.zeros((seq, HD), f32)
 
         def step(i, carry):
             cols = pl.ds(pl.multiple_of(i * wide, wide), wide)
@@ -1157,22 +1055,28 @@
         proj[1, :, h * HD : (h + 1) * HD] = (dk[...] * scale).astype(bf16)
         proj[2, :, h * HD : (h + 1) * HD] = dv[...].astype(bf16)
     attend_back(0)
+    diag_step(ORDER[0])
+    lo_line.step(2)
     diag_step(ORDER[1])
     attend_back(1)
+    diag_step(TAIL)
     diag_step(ORDER[2])
     attend_back(2)
+    lo_send.wait_send()
     proj[0] = (dqt[...].T * scale).astype(bf16)
     ip = r.ip
 
-    def rows_step(i, carry):
-        at = pl.ds(pl.multiple_of(i * 128, 128), 128)
-        total = dot_nt(proj[0, at, :], w_v[0])
-        for j in (1, 2):
-            total += dot_nt(proj[j, at, :], w_v[j])
-        ip[i // 4, i % 4] = total.astype(bf16)
-        return carry
-
-    lax.fori_loop(0, seq // 128, rows_step, 0)
+    def input_part(s):
+        def rows_step(i, carry):
+            at = pl.ds(pl.multiple_of(s * half + i * 128, 128), 128)
+            total = dot_nt(proj[0, at, :], w_v[0])
+            for j in (1, 2):
+                total += dot_nt(proj[j, at, :], w_v[j])
+            ip[s, i] = total.astype(bf16)
+            return carry
+
+        lax.fori_loop(0, half // 128, rows_step, 0)
+
     def ip_chain(j, s):
         return Chain(
             me, go, lambda tt: ip.at[s, tt], lambda tt: act.at[tt, pl.ds(j * 128, 128), :], lambda tt: slope.at[tt, pl.ds(j * 128, 128), :],
@@ -1180,7 +1084,7 @@
         )
 
     chains = [ip_chain(0, 1 - c), ip_chain(1, c)]
-    ig, igp, qg, qc, qs, fin = r.ig, r.igp, r.qg, r.qc, r.q_sem, r.fin
+    ig, igp, qg, qc, qs = r.ig, r.piece, r.qg, r.qc, r.q_sem
 
     def q_rows(ff):
         return qg.at[:, pl.ds(pl.multiple_of(ff * rows_f, rows_f), rows_f), :]
@@ -1208,48 +1112,58 @@
     def q_add(i, ff):
         qc[i] = qc[i] + qg[:, pl.ds(pl.multiple_of(ff * rows_f, rows_f), rows_f), :]
 
-    for tt, way in CHAIN_ORDER[:2]:
-        chains[0].pass_on(tt, way)
+    def chain_pass(j, lo_at, hi_at):
+        for tt, way in CHAIN_ORDER[lo_at:hi_at]:
+            chains[j].pass_on(tt, way)
+
+    input_part(1 - c)
+    chain_pass(0, 0, 2)
+    input_part(c)
+    chain_pass(0, 2, 4)
+    chain_pass(1, 0, 2)
+    sum_step(TAIL)
+    sum_pass(3, CHAIN_ORDER[:1])
+    sum_pass(0, CHAIN_ORDER[1:2])
+    chain_pass(0, 4, 6)
+    finish(0, 1 - c)
+    go(remote(igp.at[0], ig.at[c, part], r.s_sem.at[2], r.s_sem.at[3], me.ydev))
     diag_step(ORDER[3])
-    diag_step(TAIL)
     sums_on()
-    for tt, way in CHAIN_ORDER[2:]:
-        chains[0].pass_on(tt, way)
+    chain_pass(1, 2, 4)
     for j in range(3):
         qg[j] = dot_tn(t_v[...], proj[j]).astype(bf16)
     go(remote(q_rows(far * 2 + 1 - k), qc.at[0], qs.at[0], qs.at[1], me.core))
     go(remote(q_rows(x * 2 + 1 - k), qc.at[1], qs.at[2], qs.at[3], me.core))
-    for tt, way in CHAIN_ORDER:
-        chains[1].pass_on(tt, way)
+    chain_pass(1, 4, 6)
+    there = ig.at[1 - c, part]
+    remote(there, there, r.s_sem.at[2], r.s_sem.at[3], me.ydev).wait_recv()
+    lines[1].start()
+    finish(1, c)
+    own_ig = pltpu.make_async_copy(igp.at[1], ig.at[c, part], r.load_sem.at[2])
+    own_ig.start()
+    lines[0].start(igp.at[1])
     q_take(0, 0, me.core)
     q_add(0, far * 2 + k)
     go(remote(qc.at[0], qc.at[2], qs.at[4], qs.at[5], me.xdev))
     q_take(1, 2, me.core)
     q_add(1, x * 2 + k)
-    finish(0, 1 - c)
-    go(remote(igp.at[0], ig.at[c, part], r.s_sem.at[2], r.s_sem.at[3], me.ydev))
     lo_line.step(3)
-    sum_step(TAIL)
-    sum_pass(3, CHAIN_ORDER[:1])
-    sum_pass(0, CHAIN_ORDER[1:2])
-    finish(1, c)
-    own_ig = pltpu.make_async_copy(igp.at[1], ig.at[c, part], r.load_sem.at[13])
-    own_ig.start()
-    own_ig.wait()
-    lines[0].start()
-    there = ig.at[1 - c, part]
-    remote(there, there, r.s_sem.at[2], r.s_sem.at[3], me.ydev).wait_recv()
-    lines[1].start()
+    sum_pass(2, ((2, 0),))
+    sum_pass(1, ((1, 1), (1, 0), (2, 1)))
+    lines[1].step(1)
     q_take(2, 4, me.xdev)
     qc[1] = qc[1] + qc[2]
     go(remote(qc.at[1], qc.at[3], qs.at[6], qs.at[7], me.ydev))
-    sum_pass(2, ((2, 0),))
-    sum_pass(1, ((1, 1), (1, 0), (2, 1)))
     lines[0].step(1)
-    lines[1].step(1)
     w_chain.end()
-    fin[c] = own_rows(t)[...]
-    go(remote(fin.at[c], fin.at[c], r.s_sem.at[4], r.s_sem.at[5], me.ydev))
+    fin = r.dx
+
+    def fin_half(h):
+        return fin.at[pl.ds(h * 2, 2)]
+
+    for i in (0, 1):
+        fin[c * 2 + i] = region(u_v, t, x * rows_f + c * hrows + i * qrows, qrows, 0)[...]
+    go(remote(fin_half(c), fin_half(c), r.s_sem.at[4], r.s_sem.at[5], me.ydev))
     q_take(3, 6, me.ydev)
     qsum = r.qsum
     total = jnp.zeros((1, width), f32)
@@ -1259,10 +1173,12 @@
     total = 0.5 * jnp.sum(total, 1, keepdims=True)
 
     def square_step(i, carry):
-        row = fin[c, pl.ds(pl.multiple_of(i * 16, 16), 16), :].astype(f32)
-        return carry + jnp.sum(row * row, 0, keepdims=True)
-
-    wide_total = lax.fori_loop(0, hrows // 16, square_step, jnp.zeros((1, UW), f32))
+        for j in (0, 1):
+            row = fin[c * 2 + j, pl.ds(pl.multiple_of(i * 16, 16), 16), :].astype(f32)
+            carry += jnp.sum(row * row, 0, keepdims=True)
+        return carry
+
+    wide_total = lax.fori_loop(0, qrows // 16, square_step, jnp.zeros((1, UW), f32))
     total += jnp.sum(wide_total, 1, keepdims=True)
     sz, sf = r.sz, r.sf
     sz[t] = jnp.broadcast_to(total, (8, 128))
@@ -1279,8 +1195,9 @@
         go(remote(sf.at[mine], sf.at[mine], r.f_sem.at[0, 3 + d], r.f_sem.at[1, 3 + d], dev))
     lines[0].step(3)
     lines[1].step(3)
-    remote(fin.at[1 - c], fin.at[1 - c], r.s_sem.at[4], r.s_sem.at[5], me.ydev).wait_recv()
-    r.gsum[...] = fin[...].reshape(rows_f, UW)
+    remote(fin_half(1 - c), fin_half(1 - c), r.s_sem.at[4], r.s_sem.at[5], me.ydev).wait_recv()
+    out_copy = pltpu.make_async_copy(fin, r.gsum, r.load_sem.at[0])
+    out_copy.start()
     sums_end()
     for d, dev in me.owners():
         ff, cc = me.flipped(d)
@@ -1292,13 +1209,16 @@
     r.squares[...] = all_sq
     for copy, pred in sends:
         when(pred, copy.wait_send)
-
-
-def backward(lengths, count, att, u, tok, teach, live, q, k, v, kt, pt, tokens, w):
-    depth = tok.shape[2]
-    heads, seq = q.shape[:2]
-    width = heads * HD
-    rows_f = depth // 4
+    out_copy.wait()
+    own_ig.wait()
+
+
+def train(lengths, tokens, teacher, qkv, up, down, out, norm, blocks, valid):
+    seq = tokens.shape[1] * 2
+    width = qkv.shape[2]
+    heads = width // HD
+    rows_f = qkv.shape[1]
+    depth = rows_f * 4
     vm = pl.BlockSpec(memory_space=pltpu.VMEM)
     smem = pl.BlockSpec(memory_space=pltpu.SMEM)
     hbm = pl.BlockSpec(memory_space=pl.ANY)
@@ -1311,27 +1231,35 @@
         return pltpu.VMEM(shape, f32)
 
     ins = dict(
-        lengths=(lengths, smem), count=(count, vm), att=(att, hbm), u=(u, hbm), tok=(tok, vm), teach=(teach, vm),
-        live=(live, vm), q=(q, hbm), k=(k, hbm), v=(v, hbm), kt=(kt, hbm), pt=(pt, hbm), t=(tokens, hbm), w=(w, hbm),
-    )
+        lengths=(lengths, smem), tokens=(tokens, hbm), teacher=(teacher, hbm), qkv=(qkv, vm), up=(up, vm), down=(down, vm),
+        out=(out, vm), norm=(norm, vm), blocks=(blocks, vm), valid=(valid, vm),
+    )
+    qr = rows_f // 4
     outs = dict(
         lo=((2, seq // 2, depth), bf16, hbm),
         ig=((2, seq // 2, depth), bf16, hbm),
-        gsum=((rows_f, UW), bf16, vm),
+        gsum=((4, qr, UW), bf16, hbm),
         qsum=((3, rows_f, width), f32, vm),
         sums=((8, depth), f32, vm),
         squares=((8, 128), f32, vm),
-    )
-    h, qr = rows_f // 2, rows_f // 4
+        count=((8, 128), f32, vm),
+    )
     scratch = dict(
-        att_v=vb(*att.shape), u_v=vb(*u.shape), pt_v=vb(*pt.shape), q_v=vb(*q.shape), k_v=vb(*k.shape), v_v=vb(*v.shape),
-        kt_v=vb(*kt.shape), w_v=vb(*w.shape), t_v=vb(*tokens.shape), g_v=vb(*u.shape), act=vb(4, 256, 768),
-        slope=vb(4, 256, 768), piece=vb(2, 128, depth), gone=vf(2, 128, depth), gatt=vb(*att.shape), do_in=vb(*att.shape),
-        dx=vb(4, qr, UW), dy=vb(4, qr, UW),
-        do=vb(heads, seq, HD), proj=vb(3, seq, width), dqt=vf(width, seq),
-        dk=vf(seq, HD), dv=vf(seq, HD), ip=vb(2, 4, 128, depth),
-        igp=vb(2, 128, depth), qg=vb(3, depth, width), qc=vb(4, 3, rows_f, width), fin=vb(2, h, UW),
-        load_sem=dma((14,)), s_sem=dma((6,)), lo_send=dma((2, 4)), lo_recv=dma((4,)), a_send=dma((4,)), a_recv=dma((4,)),
+        att_v=vb(4, 2, 128, width), u_v=vb(4, depth, UW), pt_v=vb(heads, seq, seq), q_v=vb(heads, seq, HD),
+        k_v=vb(heads, seq, HD), v_v=vb(heads, seq, HD), kt_v=vb(width, seq), w_v=vb(3, depth, width), t_v=vb(seq, depth),
+        tok=vb(2, 128, depth), teach=vb(2, 128, depth), live=vf(2, 8, seq // 2), upack=vb(rows_f, UW),
+        qkvb=vb(3, rows_f, width), rbt=vf(2, 8, 128), mask=vf(2, 8, seq // 2), tally=vf(6, 8, 128), vt=vb(width, seq),
+        rb=vf(2, 8, 128), level=vf(seq // BLK, seq), bias=vf(seq, 256), loc_sem=dma((5,)), w_sem=dma((6,)), y_sem=dma((8,)),
+        z_send=dma((2, 2, 4, 2)), z_recv=dma((2, 4, 2)), x_send=dma((2, 4)), x_recv=dma((2, 4)), yw_send=dma((2, 4)),
+        yw_recv=dma((2, 4)),
+        c_send=dma((2, 4)), c_recv=dma((2, 4)), h_send=dma((2, 4, 2)), h_recv=dma((2, 4, 2)), o_send=dma((2, 4)), o_recv=dma((2, 4)),
+        n_sem=dma((2, 3)),
+        g_v=vb(4, depth, UW), act=vb(4, 256, 768),
+        slope=vb(4, 256, 768), piece=vb(2, 128, depth), gone=vf(2, 128, depth), gatt=vb(4, 2, 128, width),
+        do_in=vb(4, 2, 128, width), dx=vb(4, qr, UW), dy=vb(4, qr, UW), do=vb(heads, seq, HD), proj=vb(3, seq, width),
+        dqt=vf(width, seq), ip=vb(2, 4, 128, depth),
+        qg=vb(3, depth, width), qc=vb(4, 3, rows_f, width),
+        load_sem=dma((15,)), s_sem=dma((6,)), lo_send=dma((2, 4)), lo_recv=dma((4,)), a_send=dma((4,)), a_recv=dma((4,)),
         rc_send=dma((2, 5)), rc_recv=dma((2, 5)), dx_send=dma((5,)), dx_recv=dma((5,)), dy_send=dma((5,)),
         dy_recv=dma((5,)), xg_send=dma((5, 2)), xg_recv=dma((5, 2)), yg_send=dma((5, 2)), yg_recv=dma((5, 2)),
         zw_send=dma((4,)), zw_recv_l=dma((4,)), zw_recv_r=dma((4,)), i_send=dma((2, 4)), i_recv_l=dma((2, 4)),
@@ -1340,14 +1268,14 @@
         free=pltpu.SemaphoreType.REGULAR((3, 5)),
     )
     return pl.pallas_call(
-        functools.partial(backward_kernel, (*ins, *outs, *scratch)),
-        name="backward",
+        functools.partial(train_kernel, (*ins, *outs, *scratch)),
+        name="train",
         out_shape=[jax.ShapeDtypeStruct(s, d) for s, d, _ in outs.values()],
         in_specs=[m for _, m in ins.values()],
         out_specs=[m for _, _, m in outs.values()],
         scratch_shapes=list(scratch.values()),
         compiler_params=pltpu.CompilerParams(
-            collective_id=1, has_side_effects=True, vmem_limit_bytes=60 * 2**20
+            collective_id=0, has_side_effects=True, vmem_limit_bytes=62 * 2**20
         ),
     )(*(a for a, _ in ins.values()))
 
@@ -1462,10 +1390,10 @@
     norm_square,
 ):
     blocks = jnp.transpose(random_blocks, (2, 0, 1))
-    att, u, tk, w, q, k, v, kt, pt, tok, teach, live, count = forward_attention(
+    lo, ig, gsum, qsum, sums, squares, count = train(
         lengths, tokens, teacher, qkv_weight, up_weight, down_weight.T, out_weight, norm_params, blocks, valid_mask
     )
-    lo, ig, gsum, qsum, sums, squares = backward(lengths, count, att, u, tok, teach, live, q, k, v, kt, pt, tk, w)
+    gsum = gsum.reshape(-1, UW)
     state = dict(
         qkv=(qkv_weight, qkv_moment, qkv_square),
         out=(out_weight, out_moment, out_square),

time: 239 us -> 217 us (0.908)
  Pallas kernels: 235 us -> 209 us
  local copies, waits for them, and re-layouts: 2.54 us -> 6.09 us
    pallas_call x2 -> x1, Pallas kernels: 225 us -> 199 us  [train(): pl.pallas_call(functools.partial(train_kernel, (*ins, *outs, *scratch)),...]
    unnamed x28, local copies, waits for them, and re-layouts: 2.54 us -> 6.09 us
where the time goes in v4:
time: 217 us
  Pallas kernels  209 us (96%)
  local copies, waits for them, and re-layouts  6.09 us (3%)
    pallas_call x1, Pallas kernels, train(): pl.pallas_call(functools.partial(train_kernel, (*ins, *outs, *scratch)),...  199 us
    pallas_call x1, Pallas kernels, update(): pl.pallas_call(functools.partial(update_kernel, (*ins, *outs, 'held', 'se...  9.55 us
    unnamed x28, local copies, waits for them, and re-layouts  6.09 us

profile of v4, /device:TPU:0, one launch (start us, length us, event | category | flops | bytes accessed | tf_op | source)
XLA Modules:
  0.0 216.7 jit_solution(8056353127541112461)
XLA Ops:
  1.3 0.0 copy-start
  1.3 0.0 copy-start.1
  1.3 0.0 copy-start.2
  1.3 0.0 copy-start.3
  1.3 0.0 copy-start.9
  1.4 0.0 copy-start.10
  1.4 0.0 copy-start.11
  1.4 199.4 %train.1 = (bf16[2,512,768]{2,1,0:T(8,128)(2,1)}, bf16[2,512,768]{2,1,0:T(8,128)(2,1)}, bf16[4,48,1792]{2,1,0:T(8,128)(2,1)}, f32[3,192,192]{2,1,0:T(8,128)}, f3...) custom-call(s32[2]{0:T(128)} %refs_0_.2, bf16[2,512,768]{2,1,0:T(8,128)(2,1)} %refs_1_.1, ...), custom_call_target="tpu_custom_call" | custom-call | tf_op jit(solution)/shard_map/train/pallas_call | solution.py:1270
  200.8 0.0 copy-done
  200.8 0.0 copy-done.1
  200.8 0.0 copy-done.2
  200.8 0.0 copy-done.3
  200.8 0.0 copy-done.9
  200.8 0.0 copy-done.10
  200.8 0.0 copy-done.11
  200.9 0.0 copy-start.4
  200.9 1.1 copy-done.4
  201.9 0.0 copy-start.5
  201.9 1.1 copy-done.5
  203.0 0.0 copy-start.6
  203.0 0.9 copy-done.6
  203.9 0.0 copy-start.7
  203.9 0.9 copy-done.7
  204.8 0.0 copy-start.8
  204.8 0.7 copy-done.8
  205.6 0.0 copy-start.12
  205.6 0.7 copy-done.12
  206.3 0.0 copy-start.13
  206.3 0.7 copy-done.13
  206.9 9.5 %update.1 = (bf16[2,512,768]{2,1,0:T(8,128)(2,1)}, f32[1,1]{1,0:T(1,128)}, f32[2,512,768]{2,1,0:T(8,128)}, f32[1,1]{1,0:T(1,128)}, f32[3,192,192]{2,1,0:T(8,128)...) custom-call(s32[1]{0:T(128)S(6)} %copy.40.refs_0_, ...), custom_call_target="tpu_custom_call" | custom-call | tf_op jit(solution)/shard_map/update/pallas_call | solution.py:1358
Async XLA Ops:
  1.3 199.5 %copy-start = (f32[3,192,192]{2,1,0:T(8,128)S(1)}, f32[3,192,192]{2,1,0:T(8,128)}, u32[]{:S(2)}) copy-start(f32[3,192,192]{2,1,0:T(8,128)} %refs_8_.1) | copy-start | bytes 1327108
  1.3 199.5 %copy-start.1 = (f32[192,768]{1,0:T(8,128)S(1)}, f32[192,768]{1,0:T(8,128)}, u32[]{:S(2)}) copy-start(f32[192,768]{1,0:T(8,128)} %refs_14_.1) | copy-start | bytes 1769476
  1.3 199.5 %copy-start.2 = (f32[192,192]{1,0:T(8,128)S(1)}, f32[192,192]{1,0:T(8,128)}, u32[]{:S(2)}) copy-start(f32[192,192]{1,0:T(8,128)} %refs_11_.1) | copy-start | bytes 442372
  1.3 199.5 %copy-start.3 = (f32[3,192,192]{2,1,0:T(8,128)S(1)}, f32[3,192,192]{2,1,0:T(8,128)}, u32[]{:S(2)}) copy-start(f32[3,192,192]{2,1,0:T(8,128)} %refs_9_.3) | copy-start | bytes 1327108
  1.3 199.5 %copy-start.9 = (f32[4,192]{1,0:T(4,128)S(1)}, f32[4,192]{1,0:T(4,128)}, u32[]{:S(2)}) copy-start(f32[4,192]{1,0:T(4,128)} %refs_20_.1) | copy-start | bytes 9220
  1.4 199.5 %copy-start.10 = (f32[4,192]{1,0:T(4,128)S(1)}, f32[4,192]{1,0:T(4,128)}, u32[]{:S(2)}) copy-start(f32[4,192]{1,0:T(4,128)} %refs_21_.1) | copy-start | bytes 9220
  1.4 199.5 %copy-start.11 = (f32[4,192]{1,0:T(4,128)S(1)}, f32[4,192]{1,0:T(4,128)}, u32[]{:S(2)}) copy-start(f32[4,192]{1,0:T(4,128)} %refs_22_.1) | copy-start | bytes 9220
  200.9 1.1 copy-start.4
  201.9 1.1 copy-start.5
  203.0 0.9 copy-start.6
  203.9 0.9 copy-start.7
  204.8 0.7 copy-start.8
  205.6 0.7 copy-start.12
  206.3 0.7 copy-start.13

commit v5 on v4

--- a/solution.py
+++ b/solution.py
@@ -523,7 +523,6 @@
     go(remote(r.rbt.at[1 - c], r.rb.at[c], r.y_sem.at[2], r.y_sem.at[3], me.ydev))
     go(remote(r.mask.at[1 - c], r.live.at[c], r.y_sem.at[4], r.y_sem.at[5], me.ydev))
     part = pl.ds(pl.multiple_of(t * 128, 128), 128)
-    go(remote(r.teacher.at[1 - c, part], r.teach.at[c], r.y_sem.at[6], r.y_sem.at[7], me.ydev))
 
     def wblock(ff):
         return r.w_v.at[:, pl.ds(pl.multiple_of(ff * rows_f, rows_f), rows_f), :]
@@ -720,6 +719,7 @@
     attend(2)
     y_step(3, 0)
     attend(3)
+    go(remote(r.teacher.at[1 - c, part], r.teach.at[c], r.y_sem.at[6], r.y_sem.at[7], me.ydev))
     y_step(1, 1)
     x_step(2, 1)
     z_step(3, 1)
@@ -1280,11 +1280,16 @@
     )(*(a for a, _ in ins.values()))
 
 
-def update_kernel(names, *refs):
+def update_kernel(kinds, names, *refs):
     r = types.SimpleNamespace(**dict(zip(names, refs, strict=True)))
     f = lax.axis_index("fsdp")
-    copy = pltpu.make_async_copy(r.lo, r.held, r.sem.at[0])
-    copy.start()
+    copies = [pltpu.make_async_copy(getattr(r, n), getattr(r, n + "_v"), r.in_sem.at[i]) for i, n in enumerate(kinds[0])]
+    ready = dict(zip(kinds[0], copies, strict=True))
+    for copy in copies:
+        copy.start()
+    outs = {
+        n: pltpu.make_async_copy(getattr(r, n + "_v"), getattr(r, n), r.out_sem.at[i]) for i, n in enumerate(kinds[1])
+    }
     depth = r.sums.shape[1]
     rows_f = depth // 4
     sums = r.sums[0:4, :]
@@ -1298,72 +1303,102 @@
     two = 1.0 / (1.0 - jnp.exp(steps * -0.0010005003335835335))
 
     def move(name, grad, at, rate):
+        read = [getattr(r, f"{name}_{k}_v")[at] for k in "wms"]
+        write = [getattr(r, f"{name}_{k}_new_v") for k in "wms"]
         clipped = grad * factor
-        new_moment = beta_one * getattr(r, name + "_m")[at] + (1.0 - beta_one) * clipped
-        new_square = beta_two * getattr(r, name + "_s")[at] + (1.0 - beta_two) * clipped * clipped
-        weight = getattr(r, name + "_w")[at]
-        step = new_moment * one / (jnp.sqrt(new_square * two) + adam_eps) + decay_rate * weight
-        getattr(r, name + "_w_new")[at] = weight - rate * step
-        getattr(r, name + "_m_new")[at] = new_moment
-        getattr(r, name + "_s_new")[at] = new_square
-
-    gsum = r.gsum
-
-    def rows_step(i, carry):
-        rows = pl.ds(pl.multiple_of(i * 16, 16), 16)
-        move("up", gsum[rows, 0:768].astype(f32), (rows, slice(None)), rate_list[2])
-        move("down", gsum[rows, 768:1536].astype(f32), (rows, slice(None)), rate_list[3])
+        new_moment = beta_one * read[1] + (1.0 - beta_one) * clipped
+        new_square = beta_two * read[2] + (1.0 - beta_two) * clipped * clipped
+        step = new_moment * one / (jnp.sqrt(new_square * two) + adam_eps) + decay_rate * read[0]
+        write[0][at] = read[0] - rate * step
+        write[1][at] = new_moment
+        write[2][at] = new_square
+
+    def begin(name):
+        for k in "wms":
+            ready[f"{name}_{k}"].wait()
+
+    def end(name):
+        for k in "wms":
+            outs[f"{name}_{k}_new"].start()
+
+    def by_rows(name, work):
+        begin(name)
+
+        def one_step(i, carry):
+            work(pl.ds(pl.multiple_of(i * 16, 16), 16))
+            return carry
+
+        lax.fori_loop(0, rows_f // 16, one_step, 0)
+        end(name)
+
+    every = slice(None)
+    ready["gsum"].wait()
+    by_rows("up", lambda rows: move("up", r.gsum_v[rows, 0:768].astype(f32), (rows, every), rate_list[2]))
+    by_rows("down", lambda rows: move("down", r.gsum_v[rows, 768:1536].astype(f32), (rows, every), rate_list[3]))
+    ready["ig"].wait()
+
+    def cast_step(i, carry):
+        rows = pl.ds(pl.multiple_of(i * 64, 64), 64)
+        for s in range(2):
+            r.input_grad_v[s, rows, :] = r.ig_v[s, rows, :].astype(f32)
+        return carry
+
+    lax.fori_loop(0, r.ig_v.shape[1] // 64, cast_step, 0)
+    outs["input_grad"].start()
+    ready["qsum"].wait()
+
+    def qkv_rows(rows):
         for j in range(3):
-            move("qkv", r.qsum[j, rows, :], (j, rows, slice(None)), rate_list[0])
-        return carry
-
-    lax.fori_loop(0, rows_f // 16, rows_step, 0)
-    move("out", gsum[:, 1536:1728].astype(f32).T, (slice(None), slice(None)), rate_list[1])
+            move("qkv", r.qsum_v[j, rows, :], (j, rows, every), rate_list[0])
+
+    by_rows("qkv", qkv_rows)
+    begin("out")
+    move("out", r.gsum_v[:, 1536:1728].astype(f32).T, (every, every), rate_list[1])
+    end("out")
+    ready["lo"].wait()
+    layer_out = pltpu.make_async_copy(r.lo_v, r.layer_out, r.out_sem.at[len(kinds[1])])
+    layer_out.start()
     mine = sums[:, 0:rows_f]
     for i in range(1, 4):
         mine = jnp.where(f == i, sums[:, i * rows_f : (i + 1) * rows_f], mine)
-    move("norm", mine, (slice(None), slice(None)), rate_list[4])
-
-    def cast_step(i, carry):
-        rows = pl.ds(pl.multiple_of(i * 64, 64), 64)
-        for s in range(2):
-            r.input_grad[s, rows, :] = r.ig[s, rows, :].astype(f32)
-        return carry
-
-    copy.wait()
-    copy = pltpu.make_async_copy(r.held, r.layer_out, r.sem.at[1])
-    copy.start()
-    lax.fori_loop(0, r.ig.shape[1] // 64, cast_step, 0)
-    copy.wait()
+    begin("norm")
+    move("norm", mine, (every, every), rate_list[4])
+    end("norm")
+    for copy in (*outs.values(), layer_out):
+        copy.wait()
 
 
 def update(steps, lo, ig, gsum, qsum, sums, squares, count, state):
     vm = pl.BlockSpec(memory_space=pltpu.VMEM)
     smem = pl.BlockSpec(memory_space=pltpu.SMEM)
     hbm = pl.BlockSpec(memory_space=pl.ANY)
-    ins = dict(
-        steps=(steps, smem), lo=(lo, hbm), ig=(ig, vm), gsum=(gsum, vm), qsum=(qsum, vm), sums=(sums, vm),
-        squares=(squares, vm), count=(count, vm),
-    )
-    outs = dict(
-        layer_out=(jax.ShapeDtypeStruct(lo.shape, bf16), hbm),
-        loss=(jax.ShapeDtypeStruct((1, 1), f32), vm),
-        input_grad=(jax.ShapeDtypeStruct(ig.shape, f32), vm),
-        norm=(jax.ShapeDtypeStruct((1, 1), f32), vm),
-    )
-    for name, group in state.items():
-        for kind, array in zip("wms", group):
-            ins[f"{name}_{kind}"] = (array, vm)
-            outs[f"{name}_{kind}_new"] = (jax.ShapeDtypeStruct(array.shape, f32), vm)
-    return pl.pallas_call(
-        functools.partial(update_kernel, (*ins, *outs, "held", "sem")),
+    shape = jax.ShapeDtypeStruct
+    ins = dict(steps=(steps, smem), sums=(sums, vm), squares=(squares, vm), count=(count, vm))
+    moved = dict(gsum=gsum)
+    order = ("up", "down", "qkv", "out", "norm")
+    for name in order:
+        if name == "qkv":
+            moved.update(ig=ig, qsum=qsum)
+        moved.update({f"{name}_{k}": a for k, a in zip("wms", state[name])})
+    moved.update(lo=lo)
+    ins.update({n: (a, hbm) for n, a in moved.items()})
+    made = dict(input_grad=shape(ig.shape, f32))
+    made.update({f"{n}_{k}_new": shape(a.shape, f32) for n, group in state.items() for k, a in zip("wms", group)})
+    outs = dict(layer_out=(shape(lo.shape, bf16), hbm), loss=(shape((1, 1), f32), vm), norm=(shape((1, 1), f32), vm))
+    outs.update({n: (a, hbm) for n, a in made.items()})
+    scratch = {n + "_v": pltpu.VMEM(a.shape, a.dtype) for n, a in (*moved.items(), *made.items())}
+    scratch.update(in_sem=pltpu.SemaphoreType.DMA((len(moved),)), out_sem=pltpu.SemaphoreType.DMA((len(made) + 1,)))
+    results = pl.pallas_call(
+        functools.partial(update_kernel, (tuple(moved), tuple(made)), (*ins, *outs, *scratch)),
         name="update",
-        out_shape=[shape for shape, _ in outs.values()],
+        out_shape=[a for a, _ in outs.values()],
         in_specs=[m for _, m in ins.values()],
         out_specs=[m for _, m in outs.values()],
-        scratch_shapes=[pltpu.VMEM(lo.shape, bf16), pltpu.SemaphoreType.DMA((2,))],
-        compiler_params=pltpu.CompilerParams(vmem_limit_bytes=50 * 2**20),
+        scratch_shapes=list(scratch.values()),
+        compiler_params=pltpu.CompilerParams(vmem_limit_bytes=62 * 2**20),
     )(*(a for a, _ in ins.values()))
+    got = dict(zip(outs, results, strict=True))
+    return got.pop("layer_out"), got.pop("loss"), got.pop("input_grad"), got.pop("norm"), *got.values()
 
 
 def body_swapped(

time: 217 us -> 208 us (0.959)
  local copies, waits for them, and re-layouts: 6.09 us -> 0 us
    unnamed x28 -> x0, local copies, waits for them, and re-layouts: 6.09 us -> none
where the time goes in v5:
time: 208 us
  Pallas kernels  207 us (100%)
    pallas_call x1, Pallas kernels, train(): pl.pallas_call(functools.partial(train_kernel, (*ins, *outs, *scratch)),...  198 us
    pallas_call x1, Pallas kernels, update(): pl.pallas_call(functools.partial(update_kernel, (tuple(moved), tuple(made...  8.34 us

profile of v5, /device:TPU:0, one launch (start us, length us, event | category | flops | bytes accessed | tf_op | source)
XLA Modules:
  0.0 208.3 jit_solution(6392870069777188517)
XLA Ops:
  1.3 198.4 %train.1 = (bf16[2,512,768]{2,1,0:T(8,128)(2,1)}, bf16[2,512,768]{2,1,0:T(8,128)(2,1)}, bf16[4,48,1792]{2,1,0:T(8,128)(2,1)}, f32[3,192,192]{2,1,0:T(8,128)}, f3...) custom-call(s32[2]{0:T(128)} %refs_0_.2, bf16[2,512,768]{2,1,0:T(8,128)(2,1)} %refs_1_.1, ...), custom_call_target="tpu_custom_call" | custom-call | tf_op jit(solution)/shard_map/train/pallas_call | solution.py:1270
  199.7 8.3 %update.1 = (bf16[2,512,768]{2,1,0:T(8,128)(2,1)}, f32[1,1]{1,0:T(1,128)}, f32[1,1]{1,0:T(1,128)}, f32[2,512,768]{2,1,0:T(8,128)}, f32[3,192,192]{2,1,0:T(8,128)...) custom-call(s32[1]{0:T(128)S(6)} %copy.40.refs_0_, ...), custom_call_target="tpu_custom_call" | custom-call | tf_op jit(solution)/shard_map/update/pallas_call | solution.py:1391

commit v6 on v5

--- a/solution.py
+++ b/solution.py
@@ -531,7 +531,7 @@
     go(remote(r.qkvb, wblock(f), r.w_sem.at[2], r.w_sem.at[3], me.core))
 
     def cols(u):
-        return slice(FF_COLS, UW) if u == 0 else slice(0, FF_COLS)
+        return (slice(FF_COLS, UW), slice(0, FF_COLS // 2), slice(FF_COLS // 2, FF_COLS))[u]
 
     def shard(tt, ff, u):
         return r.u_v.at[tt, pl.ds(pl.multiple_of(ff * rows_f, rows_f), rows_f), cols(u)]
@@ -543,7 +543,7 @@
         return r.upack.at[pl.ds(pl.multiple_of(h * hrows, hrows), hrows), cols(u)]
 
     hs = (c, 1 - c)
-    for u in (0, 1):
+    for u in (0, 1, 2):
         go(remote(own_half(c, u), slab(t, f, c, u), r.x_send.at[u, t], r.x_recv.at[u, t], me.xdev))
         for i in (0, 1):
             mine, there = own_half(hs[i], u), slab(t, f, hs[i], u)
@@ -642,7 +642,9 @@
     x_step(0, 0)
     z_step(1, 0)
     x_step(0, 1)
+    x_step(0, 2)
     z_step(1, 1)
+    z_step(1, 2)
     x_step(1, 0)
     z_step(2, 0)
     y_step(0, 0)
@@ -708,12 +710,15 @@
 
     attend(0)
     x_step(1, 1)
+    x_step(1, 2)
     z_step(2, 1)
+    z_step(2, 2)
     z_step(3, 0)
     x_step(2, 0)
     y_step(1, 0)
     attend(1)
     y_step(0, 1)
+    y_step(0, 2)
     x_step(3, 0)
     y_step(2, 0)
     attend(2)
@@ -721,8 +726,13 @@
     attend(3)
     go(remote(r.teacher.at[1 - c, part], r.teach.at[c], r.y_sem.at[6], r.y_sem.at[7], me.ydev))
     y_step(1, 1)
+    y_step(1, 2)
     x_step(2, 1)
+    x_step(2, 2)
     z_step(3, 1)
+    x_step(3, 1)
+    z_step(3, 2)
+    x_step(3, 2)
     for s in range(2):
         r.tok[s] = r.t_v[pl.ds(pl.multiple_of(s * half + t * 128, 128), 128), :]
     for s in range(2):
@@ -778,16 +788,21 @@
         return mixed + dot_nt(act_t, u_v[tt, :, 768:1536])
     second = t - 1 + 2 * ((3 - t) // 3)
     fourth = 3 * (1 - t // 2)
-    x_step(3, 1)
     core_wait(t, 1)
+    core_wait(t, 2)
     mixed = up_step(t, jnp.zeros((rows, depth), f32))
     y_step(2, 1)
+    y_step(2, 2)
     core_wait(second, 1)
+    core_wait(second, 2)
     mixed = up_step(second, mixed)
     core_wait(6 - t - second - fourth, 1)
+    core_wait(6 - t - second - fourth, 2)
     mixed = up_step(6 - t - second - fourth, mixed)
     y_step(3, 1)
+    y_step(3, 2)
     core_wait(fourth, 1)
+    core_wait(fourth, 2)
     mixed = up_step(fourth, mixed)
     there = r.live.at[1 - c]
     remote(there, there, r.y_sem.at[4], r.y_sem.at[5], me.ydev).wait_recv()
@@ -1250,9 +1265,9 @@
         tok=vb(2, 128, depth), teach=vb(2, 128, depth), live=vf(2, 8, seq // 2), upack=vb(rows_f, UW),
         qkvb=vb(3, rows_f, width), rbt=vf(2, 8, 128), mask=vf(2, 8, seq // 2), tally=vf(6, 8, 128), vt=vb(width, seq),
         rb=vf(2, 8, 128), level=vf(seq // BLK, seq), bias=vf(seq, 256), loc_sem=dma((5,)), w_sem=dma((6,)), y_sem=dma((8,)),
-        z_send=dma((2, 2, 4, 2)), z_recv=dma((2, 4, 2)), x_send=dma((2, 4)), x_recv=dma((2, 4)), yw_send=dma((2, 4)),
-        yw_recv=dma((2, 4)),
-        c_send=dma((2, 4)), c_recv=dma((2, 4)), h_send=dma((2, 4, 2)), h_recv=dma((2, 4, 2)), o_send=dma((2, 4)), o_recv=dma((2, 4)),
+        z_send=dma((3, 2, 4, 2)), z_recv=dma((3, 4, 2)), x_send=dma((3, 4)), x_recv=dma((3, 4)), yw_send=dma((3, 4)),
+        yw_recv=dma((3, 4)),
+        c_send=dma((3, 4)), c_recv=dma((3, 4)), h_send=dma((3, 4, 2)), h_recv=dma((3, 4, 2)), o_send=dma((2, 4)), o_recv=dma((2, 4)),
         n_sem=dma((2, 3)),
         g_v=vb(4, depth, UW), act=vb(4, 256, 768),
         slope=vb(4, 256, 768), piece=vb(2, 128, depth), gone=vf(2, 128, depth), gatt=vb(4, 2, 128, width),

time: 208 us -> 210 us (level)
  no operation moved by 1% of the time
where the time goes in v6:
time: 210 us
  Pallas kernels  208 us (99%)
    pallas_call x1, Pallas kernels, train(): pl.pallas_call(functools.partial(train_kernel, (*ins, *outs, *scratch)),...  200 us
    pallas_call x1, Pallas kernels, update(): pl.pallas_call(functools.partial(update_kernel, (tuple(moved), tuple(made...  8.34 us

profile of v6, /device:TPU:0, one launch (start us, length us, event | category | flops | bytes accessed | tf_op | source)
XLA Modules:
  0.0 209.6 jit_solution(33793281999792152)
XLA Ops:
  1.3 199.7 %train.1 = (bf16[2,512,768]{2,1,0:T(8,128)(2,1)}, bf16[2,512,768]{2,1,0:T(8,128)(2,1)}, bf16[4,48,1792]{2,1,0:T(8,128)(2,1)}, f32[3,192,192]{2,1,0:T(8,128)}, f3...) custom-call(s32[2]{0:T(128)} %refs_0_.2, bf16[2,512,768]{2,1,0:T(8,128)(2,1)} %refs_1_.1, ...), custom_call_target="tpu_custom_call" | custom-call | tf_op jit(solution)/shard_map/train/pallas_call | solution.py:1285
  201.1 8.3 %update.1 = (bf16[2,512,768]{2,1,0:T(8,128)(2,1)}, f32[1,1]{1,0:T(1,128)}, f32[1,1]{1,0:T(1,128)}, f32[2,512,768]{2,1,0:T(8,128)}, f32[3,192,192]{2,1,0:T(8,128)...) custom-call(s32[1]{0:T(128)S(6)} %copy.40.refs_0_, ...), custom_call_target="tpu_custom_call" | custom-call | tf_op jit(solution)/shard_map/update/pallas_call | solution.py:1406
